TPU v7x, 32 devices: a whole 2x2x4 slice. The times are simulated.
32 devices in a mesh: dp: 16 (over z, x, core), tensor: 2 (over y).
Axes of the slice: x: 2, y: 2, z: 4, core: 2. Of those that a mesh axis runs over, the one named last changes fastest.
Arguments:
- layer_in: float32 [32768, 768], P(('dp', 'tensor')), may hold values from -6 to 6
- qkv_weight: bfloat16 [768, 2304], P(None, 'tensor'), may hold values from -0.21875 to 0.21875
- qkv_bias: float32 [2304], P('tensor'), may hold values from -2 to 2
- key_scorer: float32 [768], P('tensor'), may hold values from -2 to 2
- out_weight: bfloat16 [768, 768], P('tensor'), may hold values from -0.875 to 0.875
- out_bias: float32 [768], replicated, may hold values from -2 to 2
- fc_weight: bfloat16 [768, 3072], P(None, 'tensor'), may hold values from -0.21875 to 0.21875
- fc_bias: float32 [3072], P('tensor'), may hold values from -2 to 2
- proj_weight: bfloat16 [3072, 768], P('tensor'), may hold values from -0.109375 to 0.109375
- proj_bias: float32 [768], replicated, may hold values from -2 to 2
- norm1_gain: float32 [768], replicated, may hold values from 0.5 to 1.5
- norm1_shift: float32 [768], replicated, may hold values from -2 to 2
- norm2_gain: float32 [768], replicated, may hold values from 0.5 to 1.5
- norm2_shift: float32 [768], replicated, may hold values from -2 to 2
- key_index: int32 [32768, 64], P('dp'), may hold values from -1 to 2046, as said below
- key_count: int32 [32768], P('dp'), may hold values from 0 to 64, as said below
- out_grad: float32 [32768, 768], P(('dp', 'tensor')), may hold values from -18 to 18
Outputs:
- layer_out: float32 [32768, 768], P(('dp', 'tensor'))
- input_grad: float32 [32768, 768], P(('dp', 'tensor'))
- grad_qkv_weight: float32 [768, 2304], P(None, 'tensor')
- grad_qkv_bias: float32 [2304], P('tensor')
- grad_key_scorer: float32 [768], P('tensor')
- grad_out_weight: float32 [768, 768], P('tensor')
- grad_out_bias: float32 [768], replicated
- grad_fc_weight: float32 [768, 3072], P(None, 'tensor')
- grad_fc_bias: float32 [3072], P('tensor')
- grad_proj_weight: float32 [3072, 768], P('tensor')
- grad_proj_bias: float32 [768], replicated
- grad_norm1_gain: float32 [768], replicated
- grad_norm1_shift: float32 [768], replicated
- grad_norm2_gain: float32 [768], replicated
- grad_norm2_shift: float32 [768], replicated
Inputs may be any that keep to these rules, and one draw needn't show every extreme that they name: `key_index`: for a token at position p of its sequence, slots 0 to min(64, p) - 1 hold distinct positions below p of the same sequence, slot 0 holding p - 1; the other slots hold -1. At position p, key_count lies between (min(64, p) + 1) // 2 and min(64, p), and equals min(64, p) at the last position of every sequence.
All inputs are finite; a program needn't handle non-finite values.
Results may differ from a plain program's by a relative error of at most 0.014.
Values may be sent and summed in bfloat16 or wider, within the bound.
No kernel may reach another device: no remote copies, remote signals or barrier semaphores. Data moves between devices by JAX's collectives and lax.ppermute only.
A program may use at most 256 MiB of HBM per device.

v0:
```python
import jax
import jax.numpy as jnp
from jax import lax
from jax.sharding import PartitionSpec as P

HD = 64
TOPK = 64
WIN = 64
QBLK = 512


HIGHEST = lax.Precision.HIGHEST


def layer_norm(inputs, norm_gain, norm_shift):
    center = inputs - jnp.mean(inputs, axis=-1, keepdims=True)
    variance = jnp.mean(center * center, axis=-1, keepdims=True)
    return center * lax.rsqrt(variance + 1e-05) * norm_gain + norm_shift


def smooth_gelu(inputs):
    return jax.nn.gelu(inputs, approximate=True)


def block_mask(index_rows, count_rows, first_pos, seq_len):
    row_total = index_rows.shape[0]
    query_pos = first_pos + jnp.arange(row_total, dtype=jnp.int32)
    key_pos = jnp.arange(seq_len, dtype=jnp.int32)
    window_hit = (key_pos[None, :] <= query_pos[:, None]) & (
        key_pos[None, :] > query_pos[:, None] - WIN
    )
    slot_ids = jnp.arange(index_rows.shape[1], dtype=jnp.int32)
    picked = jnp.where(
        (slot_ids[None, :] < count_rows[:, None]) & (index_rows >= 0), index_rows, seq_len
    )
    chosen = jnp.any(picked[:, :, None] == key_pos[None, None, :], axis=1)
    return window_hit | chosen


def masked_scores(query_blk, keys_all, key_gate, index_blk, count_blk, first_pos):
    scores = (
        jnp.einsum("qhe,khe->hqk", query_blk, keys_all, preferred_element_type=jnp.float32) * 0.125
        + key_gate[:, None, :]
    )
    allowed = block_mask(index_blk, count_blk, first_pos, keys_all.shape[0])
    return jnp.where(allowed[None], scores, -1e30)


def shards(
    layer_in,
    qkv_weight,
    qkv_bias,
    key_scorer,
    out_weight,
    out_bias,
    fc_weight,
    fc_bias,
    proj_weight,
    proj_bias,
    norm1_gain,
    norm1_shift,
    norm2_gain,
    norm2_shift,
    key_index,
    key_count,
    out_grad,
):
    seq_len = key_index.shape[0]
    heads_here = key_scorer.shape[0] // HD
    block_total = seq_len // QBLK
    firsts = jnp.arange(block_total, dtype=jnp.int32) * QBLK
    index_blocks = key_index.reshape(block_total, QBLK, TOPK)
    count_blocks = key_count.reshape(block_total, QBLK)
    normed_one, norm1_back = jax.vjp(layer_norm, layer_in, norm1_gain, norm1_shift)
    normed_one_all = lax.all_gather(normed_one.astype(jnp.bfloat16), "tensor", axis=0, tiled=True)
    joined_proj = jnp.dot(normed_one_all, qkv_weight, preferred_element_type=jnp.float32) + qkv_bias
    joined_low = joined_proj.astype(jnp.bfloat16).reshape(seq_len, heads_here, 3, HD)
    queries = joined_low[:, :, 0]
    keys_all = joined_low[:, :, 1]
    values_all = joined_low[:, :, 2]
    keys_wide = keys_all.astype(jnp.float32)
    scorer_heads = key_scorer.reshape(heads_here, HD)
    gate_raw = jnp.einsum("she,he->hs", keys_wide, scorer_heads, precision=HIGHEST)
    key_gate, gate_back = jax.vjp(jax.nn.log_sigmoid, gate_raw)
    query_blocks = queries.reshape(block_total, QBLK, heads_here, HD)

    def forward_block(block_args):
        query_blk, index_blk, count_blk, first_pos = block_args
        scores = masked_scores(query_blk, keys_all, key_gate, index_blk, count_blk, first_pos)
        row_peak = jnp.max(scores, axis=-1, keepdims=True)
        weights = jnp.exp(scores - row_peak)
        totals = jnp.sum(weights, axis=-1, keepdims=True)
        probs_low = (weights / totals).astype(jnp.bfloat16)
        attended = jnp.einsum(
            "hqk,khe->qhe", probs_low, values_all, preferred_element_type=jnp.float32
        )
        return (attended, (row_peak + jnp.log(totals))[..., 0])

    attended, log_totals = lax.map(
        forward_block, (query_blocks, index_blocks, count_blocks, firsts)
    )
    attended_low = attended.astype(jnp.bfloat16).reshape(seq_len, heads_here * HD)
    picked_rows = attended_low
    mixed = (
        layer_in
        + lax.psum_scatter(
            jnp.dot(picked_rows, out_weight, preferred_element_type=jnp.float32),
            "tensor",
            scatter_dimension=0,
            tiled=True,
        )
        + out_bias
    )
    normed_two, norm2_back = jax.vjp(layer_norm, mixed, norm2_gain, norm2_shift)
    normed_two_all = lax.all_gather(normed_two.astype(jnp.bfloat16), "tensor", axis=0, tiled=True)
    hidden = jnp.dot(normed_two_all, fc_weight, preferred_element_type=jnp.float32) + fc_bias
    active, gelu_back = jax.vjp(smooth_gelu, hidden)
    active_low = active.astype(jnp.bfloat16)
    picked_rows = active_low
    layer_out = (
        mixed
        + lax.psum_scatter(
            jnp.dot(picked_rows, proj_weight, preferred_element_type=jnp.float32).astype(
                jnp.bfloat16
            ),
            "tensor",
            scatter_dimension=0,
            tiled=True,
        ).astype(jnp.float32)
        + proj_bias
    )
    grad_proj_bias = jnp.sum(out_grad, axis=0)
    grad_all = lax.all_gather(out_grad.astype(jnp.bfloat16), "tensor", axis=0, tiled=True)
    grad_proj_weight = jnp.einsum(
        "sf,sd->fd", active_low, grad_all, preferred_element_type=jnp.float32
    )
    grad_active = jnp.einsum("sd,fd->sf", grad_all, proj_weight, preferred_element_type=jnp.float32)
    (grad_hidden,) = gelu_back(grad_active)
    grad_fc_bias = jnp.sum(grad_hidden, axis=0)
    grad_hidden_low = grad_hidden.astype(jnp.bfloat16)
    grad_fc_weight = jnp.einsum(
        "sd,sf->df", normed_two_all, grad_hidden_low, preferred_element_type=jnp.float32
    )
    picked_rows = grad_hidden_low
    grad_normed_two = lax.psum_scatter(
        jnp.einsum("sf,df->sd", picked_rows, fc_weight, preferred_element_type=jnp.float32).astype(
            jnp.bfloat16
        ),
        "tensor",
        scatter_dimension=0,
        tiled=True,
    ).astype(jnp.float32)
    grad_mixed_part, grad_norm2_gain, grad_norm2_shift = norm2_back(grad_normed_two)
    grad_mixed = out_grad + grad_mixed_part
    grad_out_bias = jnp.sum(grad_mixed, axis=0)
    grad_mixed_all = lax.all_gather(grad_mixed.astype(jnp.bfloat16), "tensor", axis=0, tiled=True)
    grad_out_weight = jnp.einsum(
        "sc,sd->cd", attended_low, grad_mixed_all, preferred_element_type=jnp.float32
    )
    grad_attended = jnp.einsum(
        "sd,cd->sc", grad_mixed_all, out_weight, preferred_element_type=jnp.float32
    )
    grad_att_blocks = grad_attended.astype(jnp.bfloat16).reshape(block_total, QBLK, heads_here, HD)

    def backward_block(running, block_args):
        grad_keys, grad_values, grad_gate = running
        query_blk, index_blk, count_blk, first_pos, log_blk, grad_out_blk = block_args
        scores = masked_scores(query_blk, keys_all, key_gate, index_blk, count_blk, first_pos)
        probs = jnp.exp(scores - log_blk[..., None])
        grad_probs = jnp.einsum(
            "qhe,khe->hqk", grad_out_blk, values_all, preferred_element_type=jnp.float32
        )
        row_inner = jnp.sum(probs * grad_probs, axis=-1, keepdims=True)
        grad_scores = (probs * (grad_probs - row_inner)).astype(jnp.bfloat16)
        grad_values = grad_values + jnp.einsum(
            "hqk,qhe->khe",
            probs.astype(jnp.bfloat16),
            grad_out_blk,
            preferred_element_type=jnp.float32,
        )
        grad_keys = (
            grad_keys
            + jnp.einsum("hqk,qhe->khe", grad_scores, query_blk, preferred_element_type=jnp.float32)
            * 0.125
        )
        grad_gate = grad_gate + jnp.sum(grad_scores.astype(jnp.float32), axis=1)
        grad_query = (
            jnp.einsum("hqk,khe->qhe", grad_scores, keys_all, preferred_element_type=jnp.float32)
            * 0.125
        )
        return ((grad_keys, grad_values, grad_gate), grad_query)

    start_state = (
        jnp.zeros((seq_len, heads_here, HD), jnp.float32),
        jnp.zeros((seq_len, heads_here, HD), jnp.float32),
        jnp.zeros((heads_here, seq_len), jnp.float32),
    )
    (grad_keys, grad_values, grad_gate), grad_query_blocks = lax.scan(
        backward_block,
        start_state,
        (query_blocks, index_blocks, count_blocks, firsts, log_totals, grad_att_blocks),
    )
    (grad_gate_raw,) = gate_back(grad_gate)
    grad_key_scorer = jnp.einsum("she,hs->he", keys_wide, grad_gate_raw, precision=HIGHEST).reshape(
        -1
    )
    grad_keys = grad_keys + jnp.einsum("hs,he->she", grad_gate_raw, scorer_heads, precision=HIGHEST)
    grad_queries = grad_query_blocks.reshape(seq_len, heads_here, HD)
    grad_joined = jnp.stack([grad_queries, grad_keys, grad_values], axis=2).reshape(
        seq_len, heads_here * 3 * HD
    )
    grad_qkv_bias = jnp.sum(grad_joined, axis=0)
    grad_joined_low = grad_joined.astype(jnp.bfloat16)
    grad_qkv_weight = jnp.einsum(
        "sd,sc->dc", normed_one_all, grad_joined_low, preferred_element_type=jnp.float32
    )
    picked_rows = grad_joined_low
    grad_normed_one = lax.psum_scatter(
        jnp.einsum("sc,dc->sd", picked_rows, qkv_weight, preferred_element_type=jnp.float32).astype(
            jnp.bfloat16
        ),
        "tensor",
        scatter_dimension=0,
        tiled=True,
    ).astype(jnp.float32)
    grad_in_part, grad_norm1_gain, grad_norm1_shift = norm1_back(grad_normed_one)
    input_grad = grad_mixed + grad_in_part
    (
        grad_qkv_weight,
        grad_qkv_bias,
        grad_key_scorer,
        grad_out_weight,
        grad_fc_weight,
        grad_fc_bias,
        grad_proj_weight,
    ) = lax.psum(
        (
            grad_qkv_weight,
            grad_qkv_bias,
            grad_key_scorer,
            grad_out_weight,
            grad_fc_weight,
            grad_fc_bias,
            grad_proj_weight,
        ),
        "dp",
    )
    (
        grad_out_bias,
        grad_proj_bias,
        grad_norm1_gain,
        grad_norm1_shift,
        grad_norm2_gain,
        grad_norm2_shift,
    ) = lax.psum(
        (
            grad_out_bias,
            grad_proj_bias,
            grad_norm1_gain,
            grad_norm1_shift,
            grad_norm2_gain,
            grad_norm2_shift,
        ),
        ("dp", "tensor"),
    )
    return (
        layer_out,
        input_grad,
        grad_qkv_weight,
        grad_qkv_bias,
        grad_key_scorer,
        grad_out_weight,
        grad_out_bias,
        grad_fc_weight,
        grad_fc_bias,
        grad_proj_weight,
        grad_proj_bias,
        grad_norm1_gain,
        grad_norm1_shift,
        grad_norm2_gain,
        grad_norm2_shift,
    )


def solution(mesh):
    in_specs = (
        P(("dp", "tensor"), None),
        P(None, "tensor"),
        P("tensor"),
        P("tensor"),
        P("tensor", None),
        P(),
        P(None, "tensor"),
        P("tensor"),
        P("tensor", None),
        P(),
        P(),
        P(),
        P(),
        P(),
        P("dp", None),
        P("dp"),
        P(("dp", "tensor"), None),
    )
    out_specs = (
        P(("dp", "tensor"), None),
        P(("dp", "tensor"), None),
        P(None, "tensor"),
        P("tensor"),
        P("tensor"),
        P("tensor", None),
        P(),
        P(None, "tensor"),
        P("tensor"),
        P("tensor", None),
        P(),
        P(),
        P(),
        P(),
        P(),
    )
    return jax.shard_map(shards, mesh=mesh, in_specs=in_specs, out_specs=out_specs, check_vma=False)
```

profile of v0, /device:TPU:0, one launch (start us, length us, event | category | flops | bytes accessed | tf_op | source)
XLA Modules:
  0.0 1833.5 jit_solution(1014160574918450175)
XLA Ops:
  16.6 46.2 %all-gather.5.cloned.1.call-done = bf16[2048,768]{1,0:T(8,128)(2,1)} async-done(((bf16[1024,768]{1,0:T(8,128)(2,1)}), bf16[2048,768]{1,0:T(8,128)(2,1)}) %all-gather.5.cloned.1.call-update) | async-done | bytes 3145744 | tf_op jit(solution)/shard_map/all_gather | solution.py:75
  81.7 391.9 %while.33 = (s32[]{:T(128)}, bf16[4,512,6,64]{1,3,2,0:T(8,128)(2,1)}, f32[4,6,512]{2,1,0:T(8,128)}, s32[4]{0:T(128)S(1)}, s32[4,512]{1,0:T(4,128)S(1)}, /*index=...) while((s32[]{:T(128)}, ...), condition=%wide.region_6.7_spmd, body=%wide.region_2.6_spmd.sunk | while | flops 1842477056 | bytes 111962368 | solution.py:99
  83.0 56.3 %fusion.140 = pred[512,2048]{1,0:T(8,128)(4,1)S(1)} fusion(s32[512,64]{1,0:T(8,128)S(1)} %bitcast_select_fusion.4), kind=kLoop, calls=%fused_computation.1.clone.1 | loop fusion | flops 133169152 | bytes 1179648 | tf_op jit(solution)/shard_map/while/body/eval_jaxpr/reduce_or | solution.py:36
  181.0 56.3 %fusion.140 = pred[512,2048]{1,0:T(8,128)(4,1)S(1)} fusion(s32[512,64]{1,0:T(8,128)S(1)} %bitcast_select_fusion.4), kind=kLoop, calls=%fused_computation.1.clone.1 | loop fusion | flops 133169152 | bytes 1179648 | tf_op jit(solution)/shard_map/while/body/eval_jaxpr/reduce_or | solution.py:36
  278.9 56.3 %fusion.140 = pred[512,2048]{1,0:T(8,128)(4,1)S(1)} fusion(s32[512,64]{1,0:T(8,128)S(1)} %bitcast_select_fusion.4), kind=kLoop, calls=%fused_computation.1.clone.1 | loop fusion | flops 133169152 | bytes 1179648 | tf_op jit(solution)/shard_map/while/body/eval_jaxpr/reduce_or | solution.py:36
  376.8 56.3 %fusion.140 = pred[512,2048]{1,0:T(8,128)(4,1)S(1)} fusion(s32[512,64]{1,0:T(8,128)S(1)} %bitcast_select_fusion.4), kind=kLoop, calls=%fused_computation.1.clone.1 | loop fusion | flops 133169152 | bytes 1179648 | tf_op jit(solution)/shard_map/while/body/eval_jaxpr/reduce_or | solution.py:36
  482.5 77.2 %reduce-scatter.5.cloned.1.call-done = f32[1024,768]{1,0:T(8,128)} async-done(((f32[2048,768]{1,0:T(8,128)}), f32[1024,768]{1,0:T(8,128)}) %reduce-scatter.5.cloned.1.call-update) | async-done | bytes 3145744 | tf_op jit(solution)/shard_map/reduce_scatter | solution.py:106
  571.3 40.1 %all-gather.7.cloned.1.call-done = bf16[2048,768]{1,0:T(8,128)(2,1)} async-done(((bf16[1024,768]{1,0:T(8,128)(2,1)}), bf16[2048,768]{1,0:T(8,128)(2,1)}) %all-gather.7.cloned.1.call-update) | async-done | bytes 3145744 | tf_op jit(solution)/shard_map/all_gather | solution.py:115
  624.9 33.5 %all-gather.9.cloned.1.call-done = bf16[2048,768]{1,0:T(8,128)(2,1)} async-done(((bf16[1024,768]{1,0:T(8,128)(2,1)}), bf16[2048,768]{1,0:T(8,128)(2,1)}) %all-gather.9.cloned.1.call-update) | async-done | bytes 3145744 | tf_op jit(solution)/shard_map/all_gather | solution.py:133
  658.4 17.3 fusion.81
  696.1 32.2 %reduce-scatter.9.cloned.1.call-done = bf16[1024,768]{1,0:T(8,128)(2,1)} async-done(((bf16[2048,768]{1,0:T(8,128)(2,1)}), bf16[1024,768]{1,0:T(8,128)(2,1)}) %reduce-scatter.9.cloned.1.call-update) | async-done | bytes 1572880 | tf_op jit(solution)/shard_map/reduce_scatter | solution.py:145
  736.2 38.1 %reduce-scatter.7.cloned.1.call-done = bf16[1024,768]{1,0:T(8,128)(2,1)} async-done(((bf16[2048,768]{1,0:T(8,128)(2,1)}), bf16[1024,768]{1,0:T(8,128)(2,1)}) %reduce-scatter.7.cloned.1.call-update) | async-done | bytes 1572880 | tf_op jit(solution)/shard_map/reduce_scatter | solution.py:122
  783.8 44.4 %all-gather.11.cloned.1.call-done = bf16[2048,768]{1,0:T(8,128)(2,1)} async-done(((bf16[1024,768]{1,0:T(8,128)(2,1)}), bf16[2048,768]{1,0:T(8,128)(2,1)}) %all-gather.11.cloned.1.call-update) | async-done | bytes 3145744 | tf_op jit(solution)/shard_map/all_gather | solution.py:156
  840.1 647.2 %while.34 = (s32[]{:T(128)}, f32[2048,6,64]{0,2,1:T(8,128)}, f32[2048,6,64]{0,2,1:T(8,128)}, f32[6,2048]{1,0:T(8,128)S(1)}, f32[4,512,6,64]{1,0,3,2:T(4,128)}, /...) while((s32[]{:T(128)}, f32[2048,6,64]{0,2,1:T(8,128)}, ...), condition=%wide.region_18.19_spmd.clone, body=%wide.region_14.18_spmd.clone.sunk | while | flops 4293994496 | bytes 225036688 | solution.py:198
  842.6 56.3 %fusion.155 = pred[512,2048]{1,0:T(8,128)(4,1)S(1)} fusion(s32[512,64]{1,0:T(8,128)S(1)} %bitcast_select_fusion.5), kind=kLoop, calls=%fused_computation.29.clone.1 | loop fusion | flops 133169152 | bytes 1179648 | tf_op jit(solution)/shard_map/while/body/eval_jaxpr/reduce_or | solution.py:36
  924.9 18.9 %multiply_reduce_fusion.4 = (f32[6,512]{1,0:T(8,128)S(1)}, f32[6,512,2048]{2,1,0:T(8,128)}) fusion(f32[6,512]{1,0:T(8,128)S(1)} %dynamic-slice_bitcast_fusion.2, f32[6,2048]{1,0:T(8,128)S(1)} %get-tuple-element.814, f32[6,512,2048]{2,1,0:T(8,128)} %fusion.154, pred[512,2048]{1,0:T(8,128)(4,1)S(1)} %fusion.156, ...), kind=kOutput, calls=%fused_computation.32.clone.1 | convolution fusion | flops 843052032 | bytes 53420036 | tf_op jit(solution)/shard_map/while/body/eval_jaxpr/qhe,khe->hqk/dot_general | solution.py:170
  943.8 22.5 %convert_reduce_fusion.4 = (f32[6,2048]{1,0:T(8,128)S(1)}, bf16[6,512,2048]{2,1,0:T(8,128)(2,1)}) fusion(f32[6,512,2048]{2,1,0:T(8,128)} %get-tuple-element.735, f32[6,512]{1,0:T(8,128)S(1)} %get-tuple-element.736, f32[6,512]{1,0:T(8,128)S(1)} %dynamic-slice_bitcast_fusion.2, f32[6,2048]{1,0:T(8,128)S(1)} %get-tuple-element.814, ...), kind=kLoop, calls=%fused_computation.30.clone.1 | loop fusion | flops 56610816 | bytes 64086016 | tf_op jit(solution)/shard_map/while/body/eval_jaxpr/reduce_sum | solution.py:186
  984.7 16.1 dynamic_update_slice.28
  1003.1 56.3 %fusion.155 = pred[512,2048]{1,0:T(8,128)(4,1)S(1)} fusion(s32[512,64]{1,0:T(8,128)S(1)} %bitcast_select_fusion.5), kind=kLoop, calls=%fused_computation.29.clone.1 | loop fusion | flops 133169152 | bytes 1179648 | tf_op jit(solution)/shard_map/while/body/eval_jaxpr/reduce_or | solution.py:36
  1086.1 18.9 %multiply_reduce_fusion.4 = (f32[6,512]{1,0:T(8,128)S(1)}, f32[6,512,2048]{2,1,0:T(8,128)}) fusion(f32[6,512]{1,0:T(8,128)S(1)} %dynamic-slice_bitcast_fusion.2, f32[6,2048]{1,0:T(8,128)S(1)} %get-tuple-element.814, f32[6,512,2048]{2,1,0:T(8,128)} %fusion.154, pred[512,2048]{1,0:T(8,128)(4,1)S(1)} %fusion.156, ...), kind=kOutput, calls=%fused_computation.32.clone.1 | convolution fusion | flops 843052032 | bytes 53420036 | tf_op jit(solution)/shard_map/while/body/eval_jaxpr/qhe,khe->hqk/dot_general | solution.py:170
  1105.0 22.5 %convert_reduce_fusion.4 = (f32[6,2048]{1,0:T(8,128)S(1)}, bf16[6,512,2048]{2,1,0:T(8,128)(2,1)}) fusion(f32[6,512,2048]{2,1,0:T(8,128)} %get-tuple-element.735, f32[6,512]{1,0:T(8,128)S(1)} %get-tuple-element.736, f32[6,512]{1,0:T(8,128)S(1)} %dynamic-slice_bitcast_fusion.2, f32[6,2048]{1,0:T(8,128)S(1)} %get-tuple-element.814, ...), kind=kLoop, calls=%fused_computation.30.clone.1 | loop fusion | flops 56610816 | bytes 64086016 | tf_op jit(solution)/shard_map/while/body/eval_jaxpr/reduce_sum | solution.py:186
  1146.8 16.1 dynamic_update_slice.28
  1165.1 56.3 %fusion.155 = pred[512,2048]{1,0:T(8,128)(4,1)S(1)} fusion(s32[512,64]{1,0:T(8,128)S(1)} %bitcast_select_fusion.5), kind=kLoop, calls=%fused_computation.29.clone.1 | loop fusion | flops 133169152 | bytes 1179648 | tf_op jit(solution)/shard_map/while/body/eval_jaxpr/reduce_or | solution.py:36
  1248.2 18.9 %multiply_reduce_fusion.4 = (f32[6,512]{1,0:T(8,128)S(1)}, f32[6,512,2048]{2,1,0:T(8,128)}) fusion(f32[6,512]{1,0:T(8,128)S(1)} %dynamic-slice_bitcast_fusion.2, f32[6,2048]{1,0:T(8,128)S(1)} %get-tuple-element.814, f32[6,512,2048]{2,1,0:T(8,128)} %fusion.154, pred[512,2048]{1,0:T(8,128)(4,1)S(1)} %fusion.156, ...), kind=kOutput, calls=%fused_computation.32.clone.1 | convolution fusion | flops 843052032 | bytes 53420036 | tf_op jit(solution)/shard_map/while/body/eval_jaxpr/qhe,khe->hqk/dot_general | solution.py:170
  1267.0 22.5 %convert_reduce_fusion.4 = (f32[6,2048]{1,0:T(8,128)S(1)}, bf16[6,512,2048]{2,1,0:T(8,128)(2,1)}) fusion(f32[6,512,2048]{2,1,0:T(8,128)} %get-tuple-element.735, f32[6,512]{1,0:T(8,128)S(1)} %get-tuple-element.736, f32[6,512]{1,0:T(8,128)S(1)} %dynamic-slice_bitcast_fusion.2, f32[6,2048]{1,0:T(8,128)S(1)} %get-tuple-element.814, ...), kind=kLoop, calls=%fused_computation.30.clone.1 | loop fusion | flops 56610816 | bytes 64086016 | tf_op jit(solution)/shard_map/while/body/eval_jaxpr/reduce_sum | solution.py:186
  1308.9 16.1 dynamic_update_slice.28
  1327.2 56.3 %fusion.155 = pred[512,2048]{1,0:T(8,128)(4,1)S(1)} fusion(s32[512,64]{1,0:T(8,128)S(1)} %bitcast_select_fusion.5), kind=kLoop, calls=%fused_computation.29.clone.1 | loop fusion | flops 133169152 | bytes 1179648 | tf_op jit(solution)/shard_map/while/body/eval_jaxpr/reduce_or | solution.py:36
  1410.2 18.9 %multiply_reduce_fusion.4 = (f32[6,512]{1,0:T(8,128)S(1)}, f32[6,512,2048]{2,1,0:T(8,128)}) fusion(f32[6,512]{1,0:T(8,128)S(1)} %dynamic-slice_bitcast_fusion.2, f32[6,2048]{1,0:T(8,128)S(1)} %get-tuple-element.814, f32[6,512,2048]{2,1,0:T(8,128)} %fusion.154, pred[512,2048]{1,0:T(8,128)(4,1)S(1)} %fusion.156, ...), kind=kOutput, calls=%fused_computation.32.clone.1 | convolution fusion | flops 843052032 | bytes 53420036 | tf_op jit(solution)/shard_map/while/body/eval_jaxpr/qhe,khe->hqk/dot_general | solution.py:170
  1429.1 22.5 %convert_reduce_fusion.4 = (f32[6,2048]{1,0:T(8,128)S(1)}, bf16[6,512,2048]{2,1,0:T(8,128)(2,1)}) fusion(f32[6,512,2048]{2,1,0:T(8,128)} %get-tuple-element.735, f32[6,512]{1,0:T(8,128)S(1)} %get-tuple-element.736, f32[6,512]{1,0:T(8,128)S(1)} %dynamic-slice_bitcast_fusion.2, f32[6,2048]{1,0:T(8,128)S(1)} %get-tuple-element.814, ...), kind=kLoop, calls=%fused_computation.30.clone.1 | loop fusion | flops 56610816 | bytes 64086016 | tf_op jit(solution)/shard_map/while/body/eval_jaxpr/reduce_sum | solution.py:186
  1541.7 64.2 %all-reduce.1 = (f32[1152]{0:T(1024)}, f32[384]{0:T(512)}, f32[1536]{0:T(1024)}) all-reduce(f32[1152]{0:T(1024)S(1)} %reduce_sum.223, f32[384]{0:T(512)S(1)} %reshape.354, f32[1536]{0:T(1024)S(1)} %copy-done.42), channel_id=1, replica_groups=mesh['dp'=16,'tensor'=2] {'dp'}, use_global_device_ids=true, to_apply=%region_24.25 | all-reduce | flops 3072 | bytes 24576 | tf_op jit(solution)/shard_map/psum | solution.py:236
  1613.1 39.1 %all-reduce = (f32[768]{0:T(1024)}, f32[768]{0:T(1024)}, f32[768]{0:T(1024)}, f32[768]{0:T(1024)}, f32[768]{0:T(1024)}, /*index=5*/f32[768]{0:T(1024)}) all-reduce(f32[768]{0:T(1024)S(1)} %copy-done.36, f32[768]{0:T(1024)S(1)} %copy-done.38, f32[768]{0:T(1024)S(1)} %get-tuple-element.480, ...), channel_id=1, replica_groups=mesh['dp'=16,'tensor'=2] {'dp','tensor'}, use_global_device_ids=true, to_apply=%region_28.29 | all-reduce | flops 4608 | bytes 36864 | tf_op jit(solution)/shard_map/psum | solution.py:255
  1656.9 159.0 %all-reduce.5.cloned.1.call-done = (f32[768,1152]{1,0:T(8,128)}, f32[384,768]{1,0:T(8,128)}, f32[768,1536]{1,0:T(8,128)}, f32[1536,768]{1,0:T(8,128)}) async-done(((f32[768,1152]{1,0:T(8,128)}, f32[384,768]{1,0:T(8,128)}, f32[768,1536]{1,0:T(8,128)}, f32[1536,768]{1,0:T(8,128)}), (f32[768,1152]{1,0:T(8,128)}, f32[384,768]{1,0:T(8,128)}, f32[768,1536]{1,0:T(8,128)}, ...) | async-done | bytes 14155792 | tf_op jit(solution)/shard_map/psum | solution.py:236
  (352 shorter events, 562.6 us)
Async XLA Ops:
  7.2 604.2 %copy-start = (bf16[768,1536]{1,0:T(8,128)(2,1)S(1)}, bf16[768,1536]{1,0:T(8,128)(2,1)}, u32[]{:S(2)}) copy-start(bf16[768,1536]{1,0:T(8,128)(2,1)} %param.27) | copy-start | bytes 7077892
  7.2 55.6 %all-gather.5.cloned.1.call-start = ((), (), s32[]{:S(2)}) async-start(), calls=%async_computation.4 | async-start | bytes 4718592 | tf_op jit(solution)/shard_map/all_gather | solution.py:75
  13.3 49.5 %copy-start.52 = (f32[1152]{0:T(1024)S(1)}, f32[1152]{0:T(1024)}, u32[]{:S(2)}) copy-start(f32[1152]{0:T(1024)} %param.23) | copy-start | bytes 13828
  15.0 544.6 %reduce-scatter.5.cloned.1.call-start = ((), (), s32[]{:S(2)}) async-start(), calls=%async_computation.5 | async-start | bytes 9437184 | tf_op jit(solution)/shard_map/reduce_scatter | solution.py:106
  81.7 59.3 %copy-start.4 = (bf16[2048,6,64]{0,2,1:T(8,128)(2,1)S(1)}, bf16[2048,6,64]{0,2,1:T(8,128)(2,1)}, u32[]{:S(2)}) copy-start(bf16[2048,6,64]{0,2,1:T(8,128)(2,1)} %get-tuple-element.768) | copy-start | bytes 4718596 | tf_op jit(solution)/shard_map/while
  179.6 59.3 %copy-start.4 = (bf16[2048,6,64]{0,2,1:T(8,128)(2,1)S(1)}, bf16[2048,6,64]{0,2,1:T(8,128)(2,1)}, u32[]{:S(2)}) copy-start(bf16[2048,6,64]{0,2,1:T(8,128)(2,1)} %get-tuple-element.768) | copy-start | bytes 4718596 | tf_op jit(solution)/shard_map/while
  277.5 59.3 %copy-start.4 = (bf16[2048,6,64]{0,2,1:T(8,128)(2,1)S(1)}, bf16[2048,6,64]{0,2,1:T(8,128)(2,1)}, u32[]{:S(2)}) copy-start(bf16[2048,6,64]{0,2,1:T(8,128)(2,1)} %get-tuple-element.768) | copy-start | bytes 4718596 | tf_op jit(solution)/shard_map/while
  375.4 59.3 %copy-start.4 = (bf16[2048,6,64]{0,2,1:T(8,128)(2,1)S(1)}, bf16[2048,6,64]{0,2,1:T(8,128)(2,1)}, u32[]{:S(2)}) copy-start(bf16[2048,6,64]{0,2,1:T(8,128)(2,1)} %get-tuple-element.768) | copy-start | bytes 4718596 | tf_op jit(solution)/shard_map/while
  482.4 77.2 %copy-start.44 = (f32[768]{0:T(1024)S(1)}, f32[768]{0:T(1024)}, u32[]{:S(2)}) copy-start(f32[768]{0:T(1024)} %param.26) | copy-start | bytes 9220
  482.4 129.0 %all-gather.7.cloned.1.call-start = ((), (), s32[]{:S(2)}) async-start(), calls=%async_computation.6 | async-start | bytes 4718592 | tf_op jit(solution)/shard_map/all_gather | solution.py:115
  566.3 45.1 %copy-start.53 = (f32[1536]{0:T(1024)S(1)}, f32[1536]{0:T(1024)}, u32[]{:S(2)}) copy-start(f32[1536]{0:T(1024)} %param.28) | copy-start | bytes 18436
  566.3 92.1 %all-gather.9.cloned.1.call-start = ((), (), s32[]{:S(2)}) async-start(), calls=%async_computation.8 | async-start | bytes 4718592 | tf_op jit(solution)/shard_map/all_gather | solution.py:133
  571.3 157.0 %reduce-scatter.9.cloned.1.call-start = ((), (), s32[]{:S(2)}) async-start(), calls=%async_computation.9 | async-start | bytes 4718592 | tf_op jit(solution)/shard_map/reduce_scatter | solution.py:145
  684.8 89.6 %reduce-scatter.7.cloned.1.call-start = ((), (), s32[]{:S(2)}) async-start(), calls=%async_computation.7 | async-start | bytes 4718592 | tf_op jit(solution)/shard_map/reduce_scatter | solution.py:122
  696.0 132.2 %all-gather.11.cloned.1.call-start = ((), (), s32[]{:S(2)}) async-start(), calls=%async_computation.10 | async-start | bytes 4718592 | tf_op jit(solution)/shard_map/all_gather | solution.py:156
  732.4 42.0 %copy-start.46 = (f32[768]{0:T(1024)S(1)}, f32[768]{0:T(1024)}, u32[]{:S(2)}) copy-start(f32[768]{0:T(1024)} %param.30) | copy-start | bytes 9220
  781.7 46.5 %copy-start.20 = (bf16[384,768]{1,0:T(8,128)(2,1)S(1)}, bf16[384,768]{1,0:T(8,128)(2,1)}, u32[]{:S(2)}) copy-start(bf16[384,768]{1,0:T(8,128)(2,1)} %param.25) | copy-start | bytes 1769476
  783.1 822.7 %reduce-scatter.11.cloned.1.call-start = ((), (), s32[]{:S(2)}) async-start(), calls=%async_computation.11 | async-start | bytes 4718592 | tf_op jit(solution)/shard_map/reduce_scatter | solution.py:218
  840.3 60.2 %copy-start.5 = (bf16[2048,6,64]{0,2,1:T(8,128)(2,1)S(1)}, bf16[2048,6,64]{0,2,1:T(8,128)(2,1)}, u32[]{:S(2)}) copy-start(bf16[2048,6,64]{0,2,1:T(8,128)(2,1)} %get-tuple-element.813) | copy-start | bytes 4718596 | tf_op jit(solution)/shard_map/while
  983.9 16.9 copy-start.56
  1000.8 60.2 %copy-start.5 = (bf16[2048,6,64]{0,2,1:T(8,128)(2,1)S(1)}, bf16[2048,6,64]{0,2,1:T(8,128)(2,1)}, u32[]{:S(2)}) copy-start(bf16[2048,6,64]{0,2,1:T(8,128)(2,1)} %get-tuple-element.813) | copy-start | bytes 4718596 | tf_op jit(solution)/shard_map/while
  1146.0 16.9 copy-start.56
  1162.9 60.2 %copy-start.5 = (bf16[2048,6,64]{0,2,1:T(8,128)(2,1)S(1)}, bf16[2048,6,64]{0,2,1:T(8,128)(2,1)}, u32[]{:S(2)}) copy-start(bf16[2048,6,64]{0,2,1:T(8,128)(2,1)} %get-tuple-element.813) | copy-start | bytes 4718596 | tf_op jit(solution)/shard_map/while
  1308.1 16.9 copy-start.56
  1324.9 60.2 %copy-start.5 = (bf16[2048,6,64]{0,2,1:T(8,128)(2,1)S(1)}, bf16[2048,6,64]{0,2,1:T(8,128)(2,1)}, u32[]{:S(2)}) copy-start(bf16[2048,6,64]{0,2,1:T(8,128)(2,1)} %get-tuple-element.813) | copy-start | bytes 4718596 | tf_op jit(solution)/shard_map/while
  1470.1 16.9 copy-start.56
  1507.0 308.9 %all-reduce.5.cloned.1.call-start = ((), (), s32[]{:S(2)}) async-start(), calls=%async_computation.12 | async-start | bytes 28311552 | tf_op jit(solution)/shard_map/psum | solution.py:236
  1507.1 21.3 %slice-start.4 = ((s8[4718592]{0:T(1024)(128)(4,1)}), s8[4194304]{0:T(1024)(128)(4,1)S(1)}, s32[]{:S(2)}) async-start(s8[4718592]{0:T(1024)(128)(4,1)} %bitcast.206), calls=%async_computation.17 | async-start | bytes 8388608
  1537.3 68.6 %copy-start.24 = (f32[1024]{0:T(1024)S(1)}, f32[1024]{0:T(1024)}, u32[]{:S(2)}) copy-start(f32[1024]{0:T(1024)} %copy-done.23) | copy-start | bytes 12292
  1537.3 68.6 %copy-start.28 = (f32[768]{0:T(1024)S(1)}, f32[768]{0:T(1024)}, u32[]{:S(2)}) copy-start(f32[768]{0:T(1024)} %param.31) | copy-start | bytes 9220
  1541.6 68.1 %copy-start.33 = (f32[1024]{0:T(1024)S(1)}, f32[1024]{0:T(1024)}, u32[]{:S(2)}) copy-start(f32[1024]{0:T(1024)} %copy-done.32) | copy-start | bytes 12292
  1541.6 68.1 %copy-start.30 = (f32[1024]{0:T(1024)S(1)}, f32[1024]{0:T(1024)}, u32[]{:S(2)}) copy-start(f32[1024]{0:T(1024)} %copy-done.29) | copy-start | bytes 12292
  (65 other events, 351.0 us)
Sparse Core Ops, SparseCore 0:
  15.2 47.6 all-gather.4
  482.6 77.0 reduce-scatter.4
  566.4 44.9 all-gather.6
  613.5 44.9 all-gather.8
  684.9 43.3 reduce-scatter.8
  731.0 43.3 reduce-scatter.6
  783.2 44.9 all-gather.10
  1507.2 43.3 reduce-scatter.10
  1555.7 260.1 all-reduce.4
where the time goes:
time: 1840 us; the launch traced here: 1830 us
  other arithmetic  667 us (36%)
  waiting for transfers between devices  471 us (26%)
  matrix products  446 us (24%)
  local copies, waits for them, and re-layouts  130 us (7%)
  blocking collectives  103 us (6%)
    reduce_or x8, other arithmetic, block_mask(): chosen = jnp.any(picked[:, :, None] == key_pos[None, None, :], axis=1)  450 us
    psum x1, waiting for transfers between devices, shards(): lax.psum((grad_qkv_weight, grad_qkv_bias, grad_key_scorer, grad_out_weigh...  159 us
    dot_general x8, matrix products, masked_scores(): jnp.einsum('qhe,khe->hqk', query_blk, keys_all, preferred_element_type=jn...  92.1 us
    reduce_sum x4, other arithmetic, backward_block(): grad_gate = grad_gate + jnp.sum(grad_scores.astype(jnp.float32), axis=1)  89.9 us
    reduce_scatter x1, waiting for transfers between devices, shards(): lax.psum_scatter(jnp.dot(picked_rows, out_weight, preferred_element_type=...  77.2 us
    dot_general x4, matrix products, backward_block(): jnp.einsum('qhe,khe->hqk', grad_out_blk, values_all, preferred_element_ty...  75.5 us
    dynamic_update_slice x8, local copies, waits for them, and re-layouts, shards(): lax.map(forward_block, (query_blocks, index_blocks, count_blocks, firsts))  67.4 us
    psum x1, blocking collectives, shards(): lax.psum((grad_qkv_weight, grad_qkv_bias, grad_key_scorer, grad_out_weigh...  64.2 us
  transfers between devices with their start and end apart: 9, of which 8 were waited for; matrix products, arithmetic and copies ran while one was open for 5% of the time, Pallas kernels for 0%

commit v1 on v0

v1 whole, which is shorter than its diff:
```python
import functools
import math

import jax
import jax.numpy as jnp
from jax import lax
from jax.experimental import pallas as pl
from jax.experimental.pallas import tpu as pltpu
from jax.sharding import PartitionSpec as P

HD = 64
LANES = 128
WIN = 64
LOG2E = math.log2(math.e)
LN2 = math.log(2.0)
NEG = -1e30
QB = 512
KB = 512
ROWS = 512
VT = 80
NT = (((1,), (1,)), ((), ()))
NN = (((1,), (0,)), ((), ()))
TN = (((0,), (0,)), ((), ()))
F32 = jnp.float32
BF16 = jnp.bfloat16
MIB = 1024 * 1024


def dot(a, b, dims=NN):
    return lax.dot_general(a, b, dims, preferred_element_type=F32)


def split3(x):
    hi = x.astype(BF16).astype(F32)
    rest = x - hi
    mid = rest.astype(BF16).astype(F32)
    low = (rest - mid).astype(BF16).astype(F32)
    return hi, mid, low


def lane_ids(rows):
    return lax.broadcasted_iota(jnp.int32, (rows, LANES), 1)


def put3(base, lanes, first, parts):
    out = base
    for n, part in enumerate(parts):
        out = jnp.where(lanes == first + n, part, out)
    return out


def whole_block(array):
    return pl.BlockSpec(array.shape, lambda *_: (0,) * array.ndim)


def scorer_rows(key_scorer):
    return jnp.pad(key_scorer.reshape(-1, HD), ((0, 0), (0, LANES - HD)))


def bits_kernel(low_ref, flag_ref, bits_ref):
    width = bits_ref.shape[1]
    first = pl.program_id(0) * width
    lane = lax.broadcasted_iota(jnp.int32, (LANES, width), 0)
    pos = lax.broadcasted_iota(jnp.int32, (LANES, width), 1) + first
    back = (pos - lane) & (LANES - 1)
    at = pos - back
    bits = jnp.where((back < WIN) & (at >= 0), 1 << (jnp.maximum(at, 0) >> 7), 0)
    for slot in range(low_ref.shape[0]):
        hit = low_ref[slot : slot + 1, :] == lane
        bits = bits | jnp.where(hit, flag_ref[slot : slot + 1, :], 0)
    bits_ref[...] = bits


def allowed_bits(key_index, key_count):
    seq = key_index.shape[0]
    index = key_index.T
    slots = index.shape[0]
    slot = lax.broadcasted_iota(jnp.int32, index.shape, 0)
    used = (slot < key_count[None, :]) & (index >= 0)
    low = index & (LANES - 1)
    flag = jnp.where(used, 1 << (jnp.maximum(index, 0) >> 7), 0)
    width = 256
    spec = pl.BlockSpec((slots, width), lambda i: (0, i))
    return pl.pallas_call(
        bits_kernel,
        grid=(seq // width,),
        in_specs=[spec, spec],
        out_specs=pl.BlockSpec((LANES, width), lambda i: (0, i)),
        out_shape=jax.ShapeDtypeStruct((LANES, seq), jnp.int32),
        cost_estimate=pl.CostEstimate(
            flops=3 * slots * LANES * seq, bytes_accessed=8 * slots * seq, transcendentals=0
        ),
        name="allowed_bits",
    )(low, flag)


def fill_bias(bias_ref, bits_ref, q0, k0):
    depth, width = bias_ref.shape
    bits = bits_ref[:, pl.ds(q0, width)]
    for part in range(depth // LANES):
        shift = k0 // LANES + part
        seen = ((bits >> shift) & 1) == 1
        bias_ref[part * LANES : (part + 1) * LANES, :] = jnp.where(seen, 0.0, NEG)


def qkv_kernel(norm_ref, weight_ref, bias_ref, scorer_ref, qa_ref, ka_ref, va_ref, vt_ref, kt_ref):
    rows = norm_ref.shape[0]
    heads = qa_ref.shape[0]
    lanes = lane_ids(rows)
    real = lanes < HD
    ones = jnp.where((lanes >= HD) & (lanes < HD + 3), 1.0, 0.0)
    for pair in range(heads // 2):
        cols = slice(pair * 6 * HD, (pair + 1) * 6 * HD)
        raw = dot(norm_ref[...], weight_ref[:, cols]) + bias_ref[:, cols]
        raw = raw.astype(BF16).astype(F32)
        blocks = [raw[:, n * LANES : (n + 1) * LANES] for n in range(3)]
        turned = [pltpu.roll(block, HD, 1) for block in blocks]
        groups = (
            (blocks[0], turned[0], blocks[1]),
            (turned[1], blocks[2], turned[2]),
        )
        for side, (query, key, value) in enumerate(groups):
            head = pair * 2 + side
            raw_gate = jnp.sum(key * scorer_ref[head : head + 1, :], axis=1, keepdims=True)
            gate = jnp.minimum(raw_gate, 0.0) - jnp.log1p(jnp.exp(-jnp.abs(raw_gate)))
            key_plain = jnp.where(real, key, 0.0)
            value_ones = jnp.where(real, value, ones)
            qa_ref[head] = jnp.where(real, query * 0.125, ones).astype(BF16)
            ka_ref[head] = put3(key_plain, lanes, HD, split3(gate)).astype(BF16)
            va_ref[head] = value_ones.astype(BF16)
            vt_ref[head] = value_ones.T[:VT, :].astype(BF16)
            kt_ref[head] = key_plain.T[:HD, :].astype(BF16)


def qkv_heads(norm_all, weight, bias, scorer):
    seq, width = norm_all.shape
    heads = scorer.shape[0]
    cols = weight.shape[1]
    row_spec = pl.BlockSpec((heads, ROWS, LANES), lambda i: (0, i, 0))
    row_shape = jax.ShapeDtypeStruct((heads, seq, LANES), BF16)
    bias = bias.reshape(1, cols)
    return pl.pallas_call(
        qkv_kernel,
        grid=(seq // ROWS,),
        in_specs=[
            pl.BlockSpec((ROWS, width), lambda i: (i, 0)),
            whole_block(weight),
            whole_block(bias),
            whole_block(scorer),
        ],
        out_specs=[
            row_spec,
            row_spec,
            row_spec,
            pl.BlockSpec((heads, VT, ROWS), lambda i: (0, 0, i)),
            pl.BlockSpec((heads, HD, ROWS), lambda i: (0, 0, i)),
        ],
        out_shape=[
            row_shape,
            row_shape,
            row_shape,
            jax.ShapeDtypeStruct((heads, VT, seq), BF16),
            jax.ShapeDtypeStruct((heads, HD, seq), BF16),
        ],
        compiler_params=pltpu.CompilerParams(vmem_limit_bytes=40 * MIB),
        cost_estimate=pl.CostEstimate(
            flops=2 * seq * width * cols, bytes_accessed=20 * MIB, transcendentals=0
        ),
        name="qkv_heads",
    )(norm_all, weight, bias, scorer)


def attend_kernel(
    qa_ref, ka_ref, vt_ref, bits_ref, out_ref, log_ref, bias_ref, total_ref, peak_ref
):
    heads = qa_ref.shape[0]
    q0 = pl.multiple_of(pl.program_id(0) * QB, QB)
    total_ref[...] = jnp.zeros_like(total_ref)
    peak_ref[...] = jnp.full_like(peak_ref, NEG)

    def step(j, carry):
        k0 = pl.multiple_of(j * KB, KB)
        fill_bias(bias_ref, bits_ref, q0, k0)

        def scores_of(head):
            return dot(ka_ref[head, pl.ds(k0, KB), :], qa_ref[head], NT)

        ahead = scores_of(0)
        for head in range(heads):
            scores = ahead
            if head + 1 < heads:
                ahead = scores_of(head + 1)
            scores = scores * LOG2E + bias_ref[...]
            old = peak_ref[head]
            new = jnp.maximum(old, jnp.max(scores, axis=0, keepdims=True))
            weights = jnp.exp2(scores - new[0:1])
            shrink = jnp.exp2(old - new)
            peak_ref[head] = new
            part = dot(vt_ref[head, :, pl.ds(k0, KB)], weights.astype(BF16))
            total_ref[head] = total_ref[head] * shrink[0:1] + part
        return carry

    lax.fori_loop(0, (q0 + QB + KB - 1) // KB, step, 0)
    for pair in range(heads // 2):
        sides = []
        for head in (2 * pair, 2 * pair + 1):
            mass = total_ref[head, HD : HD + 1, :]
            sides.append(total_ref[head, 0:HD, :] / mass)
            log_ref[head] = peak_ref[head] + jnp.log(mass) * LOG2E
        both = jnp.concatenate(sides, axis=0).T
        out_ref[:, pair * LANES : (pair + 1) * LANES] = both.astype(BF16)


def attend(qa, ka, vt, bits):
    heads, seq, _ = qa.shape
    return pl.pallas_call(
        attend_kernel,
        grid=(seq // QB,),
        in_specs=[
            pl.BlockSpec((heads, QB, LANES), lambda i: (0, i, 0)),
            whole_block(ka),
            whole_block(vt),
            whole_block(bits),
        ],
        out_specs=[
            pl.BlockSpec((QB, heads * HD), lambda i: (i, 0)),
            pl.BlockSpec((heads, 8, QB), lambda i: (0, 0, i)),
        ],
        out_shape=[
            jax.ShapeDtypeStruct((seq, heads * HD), BF16),
            jax.ShapeDtypeStruct((heads, 8, seq), F32),
        ],
        scratch_shapes=[
            pltpu.VMEM((KB, QB), F32),
            pltpu.VMEM((heads, VT, QB), F32),
            pltpu.VMEM((heads, 8, QB), F32),
        ],
        compiler_params=pltpu.CompilerParams(vmem_limit_bytes=48 * MIB),
        cost_estimate=pl.CostEstimate(
            flops=heads * seq * seq * 256, bytes_accessed=12 * MIB, transcendentals=0
        ),
        name="attend",
    )(qa, ka, vt, bits)


def attend_back_kernel(
    qa_ref,
    ka_ref,
    kt_ref,
    va_ref,
    grad_ref,
    att_ref,
    log_ref,
    bits_ref,
    scorer_ref,
    keys_ref,
    joined_ref,
    bias_out_ref,
    scorer_out_ref,
    bias_ref,
    ga_ref,
    dq_ref,
    dk_ref,
    dv_ref,
):
    j = pl.program_id(0)
    heads, seq, _ = qa_ref.shape
    k0 = pl.multiple_of(j * KB, KB)

    @pl.when(j == 0)
    def _():
        dq_ref[...] = jnp.zeros_like(dq_ref)
        lanes = lane_ids(ROWS)

        def prepare(step, carry):
            rows = pl.ds(pl.multiple_of(step * ROWS, ROWS), ROWS)
            for pair in range(heads // 2):
                cols = slice(pair * LANES, (pair + 1) * LANES)
                grad = grad_ref[rows, cols].astype(F32)
                prod = grad * att_ref[rows, cols].astype(F32)
                turned = pltpu.roll(grad, HD, 1)
                for side, values in enumerate((grad, turned)):
                    mine = (lanes < HD) if side == 0 else (lanes >= HD)
                    inner = jnp.sum(jnp.where(mine, prod, 0.0), axis=1, keepdims=True)
                    plain = jnp.where(lanes < HD, values, 0.0)
                    filled = put3(plain, lanes, HD, split3(-inner))
                    ga_ref[pair * 2 + side, rows, :] = filled.astype(BF16)
            return carry

        lax.fori_loop(0, seq // ROWS, prepare, 0)

    mine = pl.ds(k0, KB)
    dk_ref[:, mine, :] = jnp.zeros((heads, KB, LANES), F32)
    dv_ref[:, mine, :] = jnp.zeros((heads, KB, LANES), F32)

    def step(i, carry):
        q0 = pl.multiple_of(i * QB, QB)
        queries = pl.ds(q0, QB)
        fill_bias(bias_ref, bits_ref, q0, k0)

        def first_of(head):
            qa = qa_ref[head, queries, :]
            ga = ga_ref[head, queries, :]
            return qa, ga, dot(ka_ref[head], qa, NT), dot(va_ref[head], ga, NT)

        ahead = first_of(0)
        for head in range(heads):
            qa, ga, scores, inner = ahead
            if head + 1 < heads:
                ahead = first_of(head + 1)
            scores = scores * LOG2E + bias_ref[...]
            probs = jnp.exp2(scores - log_ref[head, 0:1, queries])
            slopes = (probs * inner).astype(BF16)
            dv_ref[head, mine, :] += dot(probs.astype(BF16), ga)
            dk_ref[head, mine, :] += dot(slopes, qa)
            dq_ref[head, :, queries] += dot(kt_ref[head], slopes)
        return carry

    lax.fori_loop(k0 // QB, seq // QB, step, 0)

    @pl.when(j == pl.num_programs(0) - 1)
    def _():
        span = 256
        lanes = lane_ids(span)
        real = lanes < HD
        bias_out_ref[...] = jnp.zeros_like(bias_out_ref)
        scorer_out_ref[...] = jnp.zeros_like(scorer_out_ref)

        def finish(step, carry):
            r0 = pl.multiple_of(step * span, span)
            rows = pl.ds(r0, span)
            for pair in range(heads // 2):
                dq = dq_ref[2 * pair : 2 * pair + 2, :, rows].reshape(LANES, span).T * 0.125
                dks, dvs = [], []
                for head in (2 * pair, 2 * pair + 1):
                    scorer = scorer_ref[head : head + 1, :]
                    key = keys_ref[head, rows, :].astype(F32)
                    dk = dk_ref[head, rows, :]
                    raw_gate = jnp.sum(key * scorer, axis=1, keepdims=True)
                    slope = dk[:, HD : HD + 1] / (1.0 + jnp.exp(raw_gate))
                    scorer_out_ref[head : head + 1, :] += jnp.sum(slope * key, axis=0, keepdims=True)
                    dks.append(dk + slope * scorer)
                    dvs.append(dv_ref[head, rows, :])
                blocks = (
                    jnp.where(real, dq, pltpu.roll(dks[0], HD, 1)),
                    jnp.where(real, dvs[0], dq),
                    jnp.where(real, dks[1], pltpu.roll(dvs[1], HD, 1)),
                )
                for n, block in enumerate(blocks):
                    cols = slice((pair * 3 + n) * LANES, (pair * 3 + n + 1) * LANES)
                    bias_out_ref[:, cols] += jnp.sum(block, axis=0, keepdims=True)
                    joined_ref[rows, cols] = block.astype(BF16)
            return carry

        lax.fori_loop(0, seq // span, finish, 0)


def attend_back(qa, ka, kt, va, grad, att, logs, bits, scorer):
    heads, seq, _ = qa.shape
    cols = heads * 3 * HD
    key_spec = pl.BlockSpec((heads, KB, LANES), lambda j: (0, j, 0))
    joined, bias_out, scorer_out = pl.pallas_call(
        attend_back_kernel,
        grid=(seq // KB,),
        in_specs=[
            whole_block(qa),
            key_spec,
            pl.BlockSpec((heads, HD, KB), lambda j: (0, 0, j)),
            key_spec,
            whole_block(grad),
            whole_block(att),
            whole_block(logs),
            whole_block(bits),
            whole_block(scorer),
            whole_block(ka),
        ],
        out_specs=[
            pl.BlockSpec((seq, cols), lambda j: (0, 0)),
            pl.BlockSpec((1, cols), lambda j: (0, 0)),
            pl.BlockSpec((heads, LANES), lambda j: (0, 0)),
        ],
        out_shape=[
            jax.ShapeDtypeStruct((seq, cols), BF16),
            jax.ShapeDtypeStruct((1, cols), F32),
            jax.ShapeDtypeStruct((heads, LANES), F32),
        ],
        scratch_shapes=[
            pltpu.VMEM((KB, QB), F32),
            pltpu.VMEM((heads, seq, LANES), BF16),
            pltpu.VMEM((heads, HD, seq), F32),
            pltpu.VMEM((heads, seq, LANES), F32),
            pltpu.VMEM((heads, seq, LANES), F32),
        ],
        compiler_params=pltpu.CompilerParams(vmem_limit_bytes=60 * MIB),
        cost_estimate=pl.CostEstimate(
            flops=heads * seq * seq * 640, bytes_accessed=24 * MIB, transcendentals=0
        ),
        name="attend_back",
    )(qa, ka, kt, va, grad, att, logs, bits, scorer, ka)
    return joined, bias_out.reshape(cols), scorer_out[:, :HD].reshape(heads * HD)


def layer_norm(inputs, norm_gain, norm_shift):
    center = inputs - jnp.mean(inputs, axis=-1, keepdims=True)
    variance = jnp.mean(center * center, axis=-1, keepdims=True)
    return center * lax.rsqrt(variance + 1e-05) * norm_gain + norm_shift


def smooth_gelu(inputs):
    return jax.nn.gelu(inputs, approximate=True)


def scatter_rows(partial):
    return lax.psum_scatter(
        partial.astype(BF16), "tensor", scatter_dimension=0, tiled=True
    ).astype(F32)


def shards(
    layer_in,
    qkv_weight,
    qkv_bias,
    key_scorer,
    out_weight,
    out_bias,
    fc_weight,
    fc_bias,
    proj_weight,
    proj_bias,
    norm1_gain,
    norm1_shift,
    norm2_gain,
    norm2_shift,
    key_index,
    key_count,
    out_grad,
):
    bits = allowed_bits(key_index, key_count)
    scorer = scorer_rows(key_scorer)
    normed_one, norm1_back = jax.vjp(layer_norm, layer_in, norm1_gain, norm1_shift)
    normed_one_all = lax.all_gather(normed_one.astype(BF16), "tensor", axis=0, tiled=True)
    qa, ka, va, vt, kt = qkv_heads(normed_one_all, qkv_weight, qkv_bias, scorer)
    attended_low, logs = attend(qa, ka, vt, bits)
    mixed = layer_in + scatter_rows(dot(attended_low, out_weight)) + out_bias
    normed_two, norm2_back = jax.vjp(layer_norm, mixed, norm2_gain, norm2_shift)
    normed_two_all = lax.all_gather(normed_two.astype(BF16), "tensor", axis=0, tiled=True)
    hidden = dot(normed_two_all, fc_weight) + fc_bias
    active, gelu_back = jax.vjp(smooth_gelu, hidden)
    active_low = active.astype(BF16)
    layer_out = mixed + scatter_rows(dot(active_low, proj_weight)) + proj_bias
    grad_proj_bias = jnp.sum(out_grad, axis=0)
    grad_all = lax.all_gather(out_grad.astype(BF16), "tensor", axis=0, tiled=True)
    grad_proj_weight = dot(active_low, grad_all, TN)
    grad_active = dot(grad_all, proj_weight, NT)
    (grad_hidden,) = gelu_back(grad_active)
    grad_fc_bias = jnp.sum(grad_hidden, axis=0)
    grad_hidden_low = grad_hidden.astype(BF16)
    grad_fc_weight = dot(normed_two_all, grad_hidden_low, TN)
    grad_normed_two = scatter_rows(dot(grad_hidden_low, fc_weight, NT))
    grad_mixed_part, grad_norm2_gain, grad_norm2_shift = norm2_back(grad_normed_two)
    grad_mixed = out_grad + grad_mixed_part
    grad_out_bias = jnp.sum(grad_mixed, axis=0)
    grad_mixed_all = lax.all_gather(grad_mixed.astype(BF16), "tensor", axis=0, tiled=True)
    grad_out_weight = dot(attended_low, grad_mixed_all, TN)
    grad_attended = dot(grad_mixed_all, out_weight, NT).astype(BF16)
    joined_grad, grad_qkv_bias, grad_key_scorer = attend_back(
        qa, ka, kt, va, grad_attended, attended_low, logs, bits, scorer
    )
    grad_qkv_weight = dot(normed_one_all, joined_grad, TN)
    grad_normed_one = scatter_rows(dot(joined_grad, qkv_weight, NT))
    grad_in_part, grad_norm1_gain, grad_norm1_shift = norm1_back(grad_normed_one)
    input_grad = grad_mixed + grad_in_part
    (grad_out_weight, grad_fc_weight, grad_proj_weight) = lax.psum(
        tuple(g.astype(BF16) for g in (grad_out_weight, grad_fc_weight, grad_proj_weight)), "dp"
    )
    grad_qkv_weight = lax.psum(grad_qkv_weight.astype(BF16), "dp")
    (grad_qkv_bias, grad_key_scorer, grad_fc_bias) = lax.psum(
        (grad_qkv_bias, grad_key_scorer, grad_fc_bias), "dp"
    )
    (
        grad_out_bias,
        grad_proj_bias,
        grad_norm1_gain,
        grad_norm1_shift,
        grad_norm2_gain,
        grad_norm2_shift,
    ) = lax.psum(
        (
            grad_out_bias,
            grad_proj_bias,
            grad_norm1_gain,
            grad_norm1_shift,
            grad_norm2_gain,
            grad_norm2_shift,
        ),
        ("dp", "tensor"),
    )
    return (
        layer_out,
        input_grad,
        grad_qkv_weight.astype(F32),
        grad_qkv_bias,
        grad_key_scorer,
        grad_out_weight.astype(F32),
        grad_out_bias,
        grad_fc_weight.astype(F32),
        grad_fc_bias,
        grad_proj_weight.astype(F32),
        grad_proj_bias,
        grad_norm1_gain,
        grad_norm1_shift,
        grad_norm2_gain,
        grad_norm2_shift,
    )


def solution(mesh):
    rows = P(("dp", "tensor"), None)
    in_specs = (
        rows,
        P(None, "tensor"),
        P("tensor"),
        P("tensor"),
        P("tensor", None),
        P(),
        P(None, "tensor"),
        P("tensor"),
        P("tensor", None),
        P(),
        P(),
        P(),
        P(),
        P(),
        P("dp", None),
        P("dp"),
        rows,
    )
    out_specs = (
        rows,
        rows,
        P(None, "tensor"),
        P("tensor"),
        P("tensor"),
        P("tensor", None),
        P(),
        P(None, "tensor"),
        P("tensor"),
        P("tensor", None),
        P(),
        P(),
        P(),
        P(),
        P(),
    )
    return jax.shard_map(shards, mesh=mesh, in_specs=in_specs, out_specs=out_specs, check_vma=False)
```

time: 1840 us -> 769 us (0.42)
  other arithmetic: 667 us -> 52.4 us
  matrix products: 446 us -> 90.9 us
  waiting for transfers between devices: 471 us -> 352 us
  Pallas kernels: 0 us -> 116 us
  local copies, waits for them, and re-layouts: 130 us -> 17.2 us
    reduce_or x8 -> x0, other arithmetic: 450 us -> none  [block_mask(): chosen = jnp.any(picked[:, :, None] == key_pos[None, None, :], axis=1)]
    dot_general x42 -> x11, matrix products: 446 us -> 90.9 us  [dot(): return lax.dot_general(a, b, dims, preferred_element_type=F32)]
    reduce_sum x9 -> x0, other arithmetic: 145 us -> none  [the longest x4 89.9 us: backward_block(): grad_gate = grad_gate + jnp.sum(grad_scores.astype(jnp.float32), axis=1)]
    pallas_call x0 -> x4, Pallas kernels: none -> 116 us  [the longest x1 61.5 us: attend_back(): pl.pallas_call(attend_back_kernel, grid=(seq // KB,), in_specs=[whole_blo...]
    psum x1, waiting for transfers between devices: 159 us -> 78.2 us  [shards(): grad_qkv_weight = lax.psum(grad_qkv_weight.astype(BF16), 'dp')]
    dynamic_update_slice x8 -> x0, local copies, waits for them, and re-layouts: 67.4 us -> none  [shards(): lax.map(forward_block, (query_blocks, index_blocks, count_blocks, firsts))]
    all_gather x4, waiting for transfers between devices: 164 us -> 134 us  [the longest x1 40.3 us: shards(): lax.all_gather(normed_two.astype(BF16), 'tensor', axis=0, tiled=True)]
  transfers between devices with their start and end apart: 9 -> 9, of which waited for: 8 -> 9; matrix products, arithmetic and copies ran while one was open for 5% -> 10% of each run, Pallas kernels for 0% -> 1%
where the time goes in v1:
time: 769 us; the launch traced here: 760 us
  waiting for transfers between devices  352 us (46%)
  Pallas kernels  116 us (15%)
  blocking collectives  104 us (14%)
  matrix products  90.9 us (12%)
  other arithmetic  52.4 us (7%)
  local copies, waits for them, and re-layouts  17.2 us (2%)
  between operations  14.6 us (2%)
  starting transfers between devices  12.3 us (2%)
    reduce_scatter x4, waiting for transfers between devices, scatter_rows(): lax.psum_scatter(partial.astype(BF16), 'tensor', scatter_dimension=0, til...  140 us
    dot_general x11, matrix products, dot(): return lax.dot_general(a, b, dims, preferred_element_type=F32)  90.9 us
    psum x1, waiting for transfers between devices, shards(): grad_qkv_weight = lax.psum(grad_qkv_weight.astype(BF16), 'dp')  78.2 us
    psum x1, blocking collectives, shards(): lax.psum((grad_qkv_bias, grad_key_scorer, grad_fc_bias), 'dp')  64.1 us
    pallas_call x1, Pallas kernels, attend_back(): pl.pallas_call(attend_back_kernel, grid=(seq // KB,), in_specs=[whole_blo...  61.5 us
    all_gather x1, waiting for transfers between devices, shards(): lax.all_gather(normed_two.astype(BF16), 'tensor', axis=0, tiled=True)  40.3 us
    psum x1, blocking collectives, shards(): lax.psum((grad_out_bias, grad_proj_bias, grad_norm1_gain, grad_norm1_shif...  40 us
    all_gather x1, waiting for transfers between devices, shards(): lax.all_gather(normed_one.astype(BF16), 'tensor', axis=0, tiled=True)  34.7 us
  transfers between devices with their start and end apart: 9, of which 9 were waited for; matrix products, arithmetic and copies ran while one was open for 10% of the time, Pallas kernels for 1%

profile of v1, /device:TPU:0, one launch (start us, length us, event | category | flops | bytes accessed | tf_op | source)
XLA Modules:
  0.0 759.9 jit_solution(16161427081256079458)
XLA Ops:
  17.0 11.1 %allowed_bits.1.bits_ref = s32[128,2048]{1,0:T(8,128)} custom-call(s32[64,2048]{1,0:T(8,128)} %and_bitcast_fusion.low_ref, s32[64,2048]{1,0:T(8,128)} %bitcast_select_fusion.flag_ref), custom_call_target="tpu_custom_call" | custom-call | flops 50331648 | bytes 1048576 | tf_op jit(solution)/shard_map/allowed_bits/pallas_call | solution.py:84
  28.1 34.7 %all-gather.5.cloned.1.call-done.norm_ref = bf16[2048,768]{1,0:T(8,128)(2,1)} async-done(((bf16[1024,768]{1,0:T(8,128)(2,1)}), bf16[2048,768]{1,0:T(8,128)(2,1)}) %all-gather.5.cloned.1.call-update) | async-done | bytes 3145744 | tf_op jit(solution)/shard_map/all_gather | solution.py:441
  64.3 16.5 %qkv_heads.1 = (bf16[6,2048,128]{2,1,0:T(8,128)(2,1)S(1)}, bf16[6,2048,128]{2,1,0:T(8,128)(2,1)S(1)}, bf16[6,2048,128]{2,1,0:T(8,128)(2,1)}, bf16[6,80,2048]{2,1,0:T(8,128)(2,1)S(1)}, bf16[6,64,2048]{2,1,0:T(8,128)(2,1)S(1)}) custom-call(bf16[2048,768]{1,0:T(8,128)(2,1)} %all-gather.5.cloned.1.call-done.norm_ref, bf16[768,1152]{1,0:T(8,128)(2,1)S(1)} %copy-done.4, ...), custom_call_target="tpu_custom_call" | custom-call | flops 3623878656 | bytes 20971520 | tf_op jit(solution)/shard_map/qkv_heads/pallas_call | solution.py:142
  85.3 27.1 %attend.1 = (bf16[2048,384]{1,0:T(8,128)(2,1)S(1)}, f32[6,8,2048]{2,1,0:T(8,128)S(1)}) custom-call(bf16[6,2048,128]{2,1,0:T(8,128)(2,1)} %copy-done.8, bf16[6,2048,128]{2,1,0:T(8,128)(2,1)} %copy-done.9, bf16[6,80,2048]{2,1,0:T(8,128)(2,1)S(1)} %get-tuple-element.27.vt_ref, s32[128,2048]{1,0:T(8,128)S(1)} %copy-done.2), custom_call_target="tpu_custom_call" | custom-call | flops 6442450944 | bytes 12582912 | tf_op jit(solution)/shard_map/attend/pallas_call | solution.py:216
  117.9 43.5 %reduce-scatter.5.cloned.1.call-done = bf16[1024,768]{1,0:T(8,128)(2,1)} async-done(((bf16[2048,768]{1,0:T(8,128)(2,1)}), bf16[1024,768]{1,0:T(8,128)(2,1)}) %reduce-scatter.5.cloned.1.call-update) | async-done | bytes 1572880 | tf_op jit(solution)/shard_map/reduce_scatter | solution.py:414
  167.6 4.4 fusion.23
  172.3 40.3 %all-gather.7.cloned.1.call-done = bf16[2048,768]{1,0:T(8,128)(2,1)} async-done(((bf16[1024,768]{1,0:T(8,128)(2,1)}), bf16[2048,768]{1,0:T(8,128)(2,1)}) %all-gather.7.cloned.1.call-update) | async-done | bytes 3145744 | tf_op jit(solution)/shard_map/all_gather | solution.py:446
  212.7 13.3 %multiply_convert_fusion = (bf16[2048,1536]{1,0:T(8,128)(2,1)}, f32[2048,1536]{1,0:T(8,128)}) fusion(f32[1536]{0:T(1024)S(1)} %copy-done.44, bf16[2048,768]{1,0:T(8,128)(2,1)} %all-gather.7.cloned.1.call-done, bf16[768,1536]{1,0:T(8,128)(2,1)S(1)} %copy-done), kind=kOutput, calls=%fused_computation.8 | convolution fusion | flops 4863295488 | bytes 24385536 | tf_op jit(solution)/shard_map/dot_general | solution.py:30
  226.0 33.1 %all-gather.9.cloned.1.call-done = bf16[2048,768]{1,0:T(8,128)(2,1)} async-done(((bf16[1024,768]{1,0:T(8,128)(2,1)}), bf16[2048,768]{1,0:T(8,128)(2,1)}) %all-gather.9.cloned.1.call-update) | async-done | bytes 3145744 | tf_op jit(solution)/shard_map/all_gather | solution.py:452
  259.1 16.8 %fusion.24 = (f32[1536]{0:T(1024)S(1)}, bf16[2048,1536]{1,0:T(8,128)(2,1)S(1)}) fusion(f32[2048,1536]{1,0:T(8,128)} %get-tuple-element.64, f32[1536]{0:T(1024)S(1)} %copy-done.44, bf16[2048,768]{1,0:T(8,128)(2,1)} %all-gather.9.cloned.1.call-done, bf16[1536,768]{1,0:T(8,128)(2,1)} %param.25), kind=kOutput, calls=%fused_computation.63 | convolution fusion | flops 4901042688 | bytes 24391680 | tf_op jit(solution)/shard_map/dot_general | solution.py:30
  278.5 6.4 convolution_convert_fusion.5
  285.0 11.7 %reduce-scatter.7.cloned.1.call-start = ((), (), s32[]{:S(2)}) async-start(), calls=%async_computation.7 | async-start | bytes 4718592 | tf_op jit(solution)/shard_map/reduce_scatter | solution.py:414
  296.7 9.3 %convolution_convert_fusion.6 = bf16[2048,768]{1,0:T(8,128)(2,1)} fusion(bf16[2048,1536]{1,0:T(8,128)(2,1)} %get-tuple-element.63, bf16[1536,768]{1,0:T(8,128)(2,1)S(1)} %copy-done.41), kind=kOutput, calls=%fused_computation.27 | convolution fusion | flops 4833411072 | bytes 11796480 | tf_op jit(solution)/shard_map/dot_general | solution.py:30
  306.0 22.5 %reduce-scatter.9.cloned.1.call-done = bf16[1024,768]{1,0:T(8,128)(2,1)} async-done(((bf16[2048,768]{1,0:T(8,128)(2,1)}), bf16[1024,768]{1,0:T(8,128)(2,1)}) %reduce-scatter.9.cloned.1.call-update) | async-done | bytes 1572880 | tf_op jit(solution)/shard_map/reduce_scatter | solution.py:414
  328.5 3.5 convert_reduce_fusion.1
  335.3 38.7 %reduce-scatter.7.cloned.1.call-done = bf16[1024,768]{1,0:T(8,128)(2,1)} async-done(((bf16[2048,768]{1,0:T(8,128)(2,1)}), bf16[1024,768]{1,0:T(8,128)(2,1)}) %reduce-scatter.7.cloned.1.call-update) | async-done | bytes 1572880 | tf_op jit(solution)/shard_map/reduce_scatter | solution.py:414
  374.0 5.1 fusion.21
  382.2 9.4 %convolution_convert_fusion = bf16[1536,768]{1,0:T(8,128)(2,1)} fusion(bf16[2048,1536]{1,0:T(8,128)(2,1)} %get-tuple-element.63, bf16[2048,768]{1,0:T(8,128)(2,1)} %all-gather.9.cloned.1.call-done), kind=kOutput, calls=%fused_computation.21 | convolution fusion | flops 4833017856 | bytes 11796480 | tf_op jit(solution)/shard_map/dot_general | solution.py:30
  391.6 9.6 %convolution_convert_fusion.1 = bf16[768,1536]{1,0:T(8,128)(2,1)} fusion(bf16[2048,768]{1,0:T(8,128)(2,1)S(1)} %copy-done.40, bf16[2048,1536]{1,0:T(8,128)(2,1)} %copy-done.45), kind=kOutput, calls=%fused_computation.22 | convolution fusion | flops 4833017856 | bytes 11796480 | tf_op jit(solution)/shard_map/dot_general | solution.py:30
  401.2 26.0 %all-gather.11.cloned.1.call-done = bf16[2048,768]{1,0:T(8,128)(2,1)} async-done(((bf16[1024,768]{1,0:T(8,128)(2,1)}), bf16[2048,768]{1,0:T(8,128)(2,1)}) %all-gather.11.cloned.1.call-update) | async-done | bytes 3145744 | tf_op jit(solution)/shard_map/all_gather | solution.py:463
  427.2 4.9 convolution_convert_fusion.7.grad_ref
  432.1 61.5 %attend_back.1 = (bf16[2048,1152]{1,0:T(8,128)(2,1)}, f32[1,1152]{1,0:T(1,128)}, f32[6,128]{1,0:T(8,128)}) custom-call(bf16[6,2048,128]{2,1,0:T(8,128)(2,1)} %copy-done.8, bf16[6,2048,128]{2,1,0:T(8,128)(2,1)} %copy-done.9, bf16[6,64,2048]{2,1,0:T(8,128)(2,1)} %copy-done.10, bf16[6,2048,128]{2,1,0:T(8,128)(2,1)} %get-tuple-element.30.va_ref, ...), custom_call_target="tpu_custom_call" | custom-call | flops 16106127360 | bytes 25165824 | tf_op jit(solution)/shard_map/attend_back/pallas_call | solution.py:362
  493.6 4.3 convolution_convert_fusion.8
  497.9 5.5 convolution_convert_fusion.4
  504.9 8.0 %convolution_convert_fusion.2 = bf16[2048,768]{1,0:T(8,128)(2,1)} fusion(bf16[2048,1152]{1,0:T(8,128)(2,1)} %get-tuple-element.32, bf16[768,1152]{1,0:T(8,128)(2,1)S(1)} %copy-done.5), kind=kOutput, calls=%fused_computation.23 | convolution fusion | flops 3625451520 | bytes 9633792 | tf_op jit(solution)/shard_map/dot_general | solution.py:30
  513.7 64.1 %all-reduce.2 = (f32[1152]{0:T(1024)}, f32[384]{0:T(512)}, f32[1536]{0:T(1024)}) all-reduce(f32[1152]{0:T(1024)S(1)} %reduce, f32[384]{0:T(512)S(1)} %reshape.113, f32[1536]{0:T(1024)S(1)} %get-tuple-element.65), channel_id=1, replica_groups=mesh['dp'=16,'tensor'=2] {'dp'}, use_global_device_ids=true, to_apply=%region_13.14 | all-reduce | flops 3072 | bytes 24576 | tf_op jit(solution)/shard_map/psum | solution.py:477
  577.8 78.2 %all-reduce.6.cloned.1.call-done = (bf16[768,1152]{1,0:T(8,128)(2,1)}, bf16[384,768]{1,0:T(8,128)(2,1)}, bf16[768,1536]{1,0:T(8,128)(2,1)}, bf16[1536,768]{1,0:T(8,128)(2,1)}) async-done(((bf16[768,1152]{1,0:T(8,128)(2,1)}, bf16[384,768]{1,0:T(8,128)(2,1)}, bf16[768,1536]{1,0:T(8,128)(2,1)}, bf16[1536,768]{1,0:T(8,128)(2,1)}), (bf16[768,1152]{1,0:T(8,128)(2,1)}, bf16[384,768]{1,0:T(8,128)(2,1)}, ...) | async-done | bytes 7077904 | tf_op jit(solution)/shard_map/psum | solution.py:476
  658.3 3.5 convert_element_type.87
  667.2 35.2 %reduce-scatter.11.cloned.1.call-done = bf16[1024,768]{1,0:T(8,128)(2,1)} async-done(((bf16[2048,768]{1,0:T(8,128)(2,1)}), bf16[1024,768]{1,0:T(8,128)(2,1)}) %reduce-scatter.11.cloned.1.call-update) | async-done | bytes 1572880 | tf_op jit(solution)/shard_map/reduce_scatter | solution.py:414
  702.4 3.5 convert_reduce_fusion
  708.0 40.0 %all-reduce.1 = (f32[768]{0:T(1024)}, f32[768]{0:T(1024)}, f32[768]{0:T(1024)}, f32[768]{0:T(1024)}, f32[768]{0:T(1024)}, /*index=5*/f32[768]{0:T(1024)}) all-reduce(f32[768]{0:T(1024)S(1)} %get-tuple-element.56, f32[768]{0:T(1024)S(1)} %get-tuple-element.60, ...), channel_id=1, replica_groups=mesh['dp'=16,'tensor'=2] {'dp','tensor'}, use_global_device_ids=true, to_apply=%region_17.18 | all-reduce | flops 4608 | bytes 36864 | tf_op jit(solution)/shard_map/psum | solution.py:487
  748.0 5.0 add_add_fusion.2
  (139 shorter events, 48.7 us)
Async XLA Ops:
  7.2 205.5 %copy-start = (bf16[768,1536]{1,0:T(8,128)(2,1)S(1)}, bf16[768,1536]{1,0:T(8,128)(2,1)}, u32[]{:S(2)}) copy-start(bf16[768,1536]{1,0:T(8,128)(2,1)} %param.23) | copy-start | bytes 7077892
  7.2 6.1 copy-start.23
  7.2 6.1 copy-start.33
  7.2 55.6 %all-gather.5.cloned.1.call-start = ((), (), s32[]{:S(2)}) async-start(), calls=%async_computation.4 | async-start | bytes 4718592 | tf_op jit(solution)/shard_map/all_gather | solution.py:441
  9.5 3.8 copy-start.12
  15.0 146.3 %reduce-scatter.5.cloned.1.call-start = ((), (), s32[]{:S(2)}) async-start(), calls=%async_computation.5 | async-start | bytes 4718592 | tf_op jit(solution)/shard_map/reduce_scatter | solution.py:414
  15.2 65.6 %copy-start.3 = (f32[6,128]{1,0:T(8,128)}, f32[6,128]{1,0:T(8,128)S(1)}, u32[]{:S(2)}) copy-start(f32[6,128]{1,0:T(8,128)S(1)} %pad.4.scorer_ref) | copy-start | bytes 9220
  28.1 57.2 %copy-start.2 = (s32[128,2048]{1,0:T(8,128)S(1)}, s32[128,2048]{1,0:T(8,128)}, u32[]{:S(2)}) copy-start(s32[128,2048]{1,0:T(8,128)} %allowed_bits.1.bits_ref) | copy-start | bytes 3145732
  85.3 29.0 %copy-start.42 = (bf16[384,768]{1,0:T(8,128)(2,1)S(1)}, bf16[384,768]{1,0:T(8,128)(2,1)}, u32[]{:S(2)}) copy-start(bf16[384,768]{1,0:T(8,128)(2,1)} %param.21) | copy-start | bytes 1769476
  117.8 43.5 %copy-start.34 = (f32[768]{0:T(1024)S(1)}, f32[768]{0:T(1024)}, u32[]{:S(2)}) copy-start(f32[768]{0:T(1024)} %param.22) | copy-start | bytes 9220
  117.8 94.8 %all-gather.7.cloned.1.call-start = ((), (), s32[]{:S(2)}) async-start(), calls=%async_computation.6 | async-start | bytes 4718592 | tf_op jit(solution)/shard_map/all_gather | solution.py:446
  167.6 45.1 %copy-start.44 = (f32[1536]{0:T(1024)S(1)}, f32[1536]{0:T(1024)}, u32[]{:S(2)}) copy-start(f32[1536]{0:T(1024)} %param.24) | copy-start | bytes 18436
  167.6 91.5 %all-gather.9.cloned.1.call-start = ((), (), s32[]{:S(2)}) async-start(), calls=%async_computation.8 | async-start | bytes 4718592 | tf_op jit(solution)/shard_map/all_gather | solution.py:452
  172.0 156.4 %reduce-scatter.9.cloned.1.call-start = ((), (), s32[]{:S(2)}) async-start(), calls=%async_computation.9 | async-start | bytes 4718592 | tf_op jit(solution)/shard_map/reduce_scatter | solution.py:414
  284.9 11.7 %copy-start.41 = (bf16[1536,768]{1,0:T(8,128)(2,1)S(1)}, bf16[1536,768]{1,0:T(8,128)(2,1)}, u32[]{:S(2)}) copy-start(bf16[1536,768]{1,0:T(8,128)(2,1)} %param.25) | copy-start | bytes 7077892
  285.0 89.0 %reduce-scatter.7.cloned.1.call-start = ((), (), s32[]{:S(2)}) async-start(), calls=%async_computation.7 | async-start | bytes 4718592 | tf_op jit(solution)/shard_map/reduce_scatter | solution.py:414
  306.0 121.2 %all-gather.11.cloned.1.call-start = ((), (), s32[]{:S(2)}) async-start(), calls=%async_computation.10 | async-start | bytes 4718592 | tf_op jit(solution)/shard_map/all_gather | solution.py:463
  332.0 42.0 %copy-start.36 = (f32[768]{0:T(1024)S(1)}, f32[768]{0:T(1024)}, u32[]{:S(2)}) copy-start(f32[768]{0:T(1024)} %param.26) | copy-start | bytes 9220
  382.1 273.9 %all-reduce.6.cloned.1.call-start = ((), (), s32[]{:S(2)}) async-start(), calls=%async_computation.12 | async-start | bytes 14155776 | tf_op jit(solution)/shard_map/psum | solution.py:476
  382.2 9.4 %copy-start.40 = (bf16[2048,768]{1,0:T(8,128)(2,1)S(1)}, bf16[2048,768]{1,0:T(8,128)(2,1)}, u32[]{:S(2)}) copy-start(bf16[2048,768]{1,0:T(8,128)(2,1)} %all-gather.7.cloned.1.call-done) | copy-start | bytes 9437188
  391.6 35.6 %copy-start.43 = (bf16[384,768]{1,0:T(8,128)(2,1)S(1)}, bf16[384,768]{1,0:T(8,128)(2,1)}, u32[]{:S(2)}) copy-start(bf16[384,768]{1,0:T(8,128)(2,1)} %param.21) | copy-start | bytes 1769476
  432.1 61.5 %copy-start.7 = (bf16[2048,384]{1,0:T(8,128)(2,1)S(1)}, bf16[2048,384]{1,0:T(8,128)(2,1)}, u32[]{:S(2)}) copy-start(bf16[2048,384]{1,0:T(8,128)(2,1)} %copy-done.6) | copy-start | bytes 4718596
  493.6 4.3 copy-start.39
  493.6 4.3 copy-start.46
  503.4 198.9 %reduce-scatter.11.cloned.1.call-start = ((), (), s32[]{:S(2)}) async-start(), calls=%async_computation.11 | async-start | bytes 4718592 | tf_op jit(solution)/shard_map/reduce_scatter | solution.py:414
  656.0 5.8 copy-start.19
  664.6 37.7 %copy-start.22 = (f32[1024]{0:T(1024)S(1)}, f32[1024]{0:T(1024)}, u32[]{:S(2)}) copy-start(f32[1024]{0:T(1024)} %copy-done.21) | copy-start | bytes 12292
  664.6 37.7 %copy-start.24 = (f32[768]{0:T(1024)S(1)}, f32[768]{0:T(1024)}, u32[]{:S(2)}) copy-start(f32[768]{0:T(1024)} %param.27) | copy-start | bytes 9220
  667.2 38.7 %copy-start.29 = (f32[1024]{0:T(1024)S(1)}, f32[1024]{0:T(1024)}, u32[]{:S(2)}) copy-start(f32[1024]{0:T(1024)} %copy-done.28) | copy-start | bytes 12292
  667.2 38.7 %copy-start.26 = (f32[1024]{0:T(1024)S(1)}, f32[1024]{0:T(1024)}, u32[]{:S(2)}) copy-start(f32[1024]{0:T(1024)} %copy-done.25) | copy-start | bytes 12292
  702.4 3.8 copy-start.16
  708.0 45.0 %copy-start.1 = (bf16[768,1536]{1,0:T(8,128)(2,1)S(1)}, bf16[768,1536]{1,0:T(8,128)(2,1)}, u32[]{:S(2)}) copy-start(bf16[768,1536]{1,0:T(8,128)(2,1)} %param.23) | copy-start | bytes 7077892
  (24 other events, 42.8 us)
Sparse Core Ops, SparseCore 0:
  15.2 47.6 all-gather.4
  117.9 43.3 reduce-scatter.4
  167.7 44.9 all-gather.6
  214.1 44.9 all-gather.8
  285.1 43.3 reduce-scatter.8
  330.6 43.3 reduce-scatter.6
  382.3 44.9 all-gather.10
  503.6 152.3 all-reduce.5
  658.9 43.3 reduce-scatter.10

commit v2 on v1

--- a/solution.py
+++ b/solution.py
@@ -103,7 +103,9 @@
         bias_ref[part * LANES : (part + 1) * LANES, :] = jnp.where(seen, 0.0, NEG)
 
 
-def qkv_kernel(norm_ref, weight_ref, bias_ref, scorer_ref, qa_ref, ka_ref, va_ref, vt_ref, kt_ref):
+def qkv_kernel(
+    at_ref, norm_ref, weight_ref, bias_ref, scorer_ref, qa_ref, ka_ref, va_ref, vt_ref, kt_ref
+):
     rows = norm_ref.shape[0]
     heads = qa_ref.shape[0]
     lanes = lane_ids(rows)
@@ -132,49 +134,64 @@
             kt_ref[head] = key_plain.T[:HD, :].astype(BF16)
 
 
-def qkv_heads(norm_all, weight, bias, scorer):
-    seq, width = norm_all.shape
+def qkv_kernel_again(at_ref, norm_ref, weight_ref, bias_ref, scorer_ref, *rest):
+    qkv_kernel(at_ref, norm_ref, weight_ref, bias_ref, scorer_ref, *rest[5:])
+
+
+def qkv_heads(norm_rows, weight, bias, scorer, block, seq, earlier=None):
+    rows, width = norm_rows.shape
     heads = scorer.shape[0]
     cols = weight.shape[1]
-    row_spec = pl.BlockSpec((heads, ROWS, LANES), lambda i: (0, i, 0))
     row_shape = jax.ShapeDtypeStruct((heads, seq, LANES), BF16)
+    row_spec = pl.BlockSpec((heads, ROWS, LANES), lambda i, at: (0, at[0] + i, 0))
     bias = bias.reshape(1, cols)
+    tall = [
+        jax.ShapeDtypeStruct((heads, VT, seq), BF16),
+        jax.ShapeDtypeStruct((heads, HD, seq), BF16),
+    ]
+    kernel = qkv_kernel
+    inputs = [norm_rows, weight, bias, scorer]
+    in_specs = [
+        pl.BlockSpec((ROWS, width), lambda i, at: (i, 0)),
+        whole_block(weight),
+        whole_block(bias),
+        whole_block(scorer),
+    ]
+    aliases = {}
+    if earlier is not None:
+        aliases = {len(inputs) + 1 + n: n for n in range(len(earlier))}
+        inputs += list(earlier)
+        in_specs += [pl.BlockSpec(memory_space=pl.ANY)] * len(earlier)
+        kernel = qkv_kernel_again
     return pl.pallas_call(
-        qkv_kernel,
-        grid=(seq // ROWS,),
-        in_specs=[
-            pl.BlockSpec((ROWS, width), lambda i: (i, 0)),
-            whole_block(weight),
-            whole_block(bias),
-            whole_block(scorer),
-        ],
-        out_specs=[
-            row_spec,
-            row_spec,
-            row_spec,
-            pl.BlockSpec((heads, VT, ROWS), lambda i: (0, 0, i)),
-            pl.BlockSpec((heads, HD, ROWS), lambda i: (0, 0, i)),
-        ],
-        out_shape=[
-            row_shape,
-            row_shape,
-            row_shape,
-            jax.ShapeDtypeStruct((heads, VT, seq), BF16),
-            jax.ShapeDtypeStruct((heads, HD, seq), BF16),
-        ],
+        kernel,
+        grid_spec=pltpu.PrefetchScalarGridSpec(
+            num_scalar_prefetch=1,
+            grid=(rows // ROWS,),
+            in_specs=in_specs,
+            out_specs=[
+                row_spec,
+                row_spec,
+                row_spec,
+                pl.BlockSpec((heads, VT, ROWS), lambda i, at: (0, 0, at[0] + i)),
+                pl.BlockSpec((heads, HD, ROWS), lambda i, at: (0, 0, at[0] + i)),
+            ],
+        ),
+        out_shape=[row_shape, row_shape, row_shape] + tall,
+        input_output_aliases=aliases,
         compiler_params=pltpu.CompilerParams(vmem_limit_bytes=40 * MIB),
         cost_estimate=pl.CostEstimate(
-            flops=2 * seq * width * cols, bytes_accessed=20 * MIB, transcendentals=0
+            flops=4 * rows * width * cols, bytes_accessed=10 * MIB, transcendentals=0
         ),
         name="qkv_heads",
-    )(norm_all, weight, bias, scorer)
+    )(block, *inputs)
 
 
 def attend_kernel(
-    qa_ref, ka_ref, vt_ref, bits_ref, out_ref, log_ref, bias_ref, total_ref, peak_ref
+    at_ref, qa_ref, ka_ref, vt_ref, bits_ref, out_ref, log_ref, bias_ref, total_ref, peak_ref
 ):
     heads = qa_ref.shape[0]
-    q0 = pl.multiple_of(pl.program_id(0) * QB, QB)
+    q0 = pl.multiple_of((at_ref[0] + pl.program_id(0)) * QB, QB)
     total_ref[...] = jnp.zeros_like(total_ref)
     peak_ref[...] = jnp.full_like(peak_ref, NEG)
 
@@ -211,36 +228,39 @@
         out_ref[:, pair * LANES : (pair + 1) * LANES] = both.astype(BF16)
 
 
-def attend(qa, ka, vt, bits):
+def attend(qa, ka, vt, bits, block, count):
     heads, seq, _ = qa.shape
     return pl.pallas_call(
         attend_kernel,
-        grid=(seq // QB,),
-        in_specs=[
-            pl.BlockSpec((heads, QB, LANES), lambda i: (0, i, 0)),
-            whole_block(ka),
-            whole_block(vt),
-            whole_block(bits),
-        ],
-        out_specs=[
-            pl.BlockSpec((QB, heads * HD), lambda i: (i, 0)),
-            pl.BlockSpec((heads, 8, QB), lambda i: (0, 0, i)),
-        ],
+        grid_spec=pltpu.PrefetchScalarGridSpec(
+            num_scalar_prefetch=1,
+            grid=(count // QB,),
+            in_specs=[
+                pl.BlockSpec((heads, QB, LANES), lambda i, at: (0, at[0] + i, 0)),
+                whole_block(ka),
+                whole_block(vt),
+                whole_block(bits),
+            ],
+            out_specs=[
+                pl.BlockSpec((QB, heads * HD), lambda i, at: (i, 0)),
+                pl.BlockSpec((heads, 8, QB), lambda i, at: (0, 0, i)),
+            ],
+            scratch_shapes=[
+                pltpu.VMEM((KB, QB), F32),
+                pltpu.VMEM((heads, VT, QB), F32),
+                pltpu.VMEM((heads, 8, QB), F32),
+            ],
+        ),
         out_shape=[
-            jax.ShapeDtypeStruct((seq, heads * HD), BF16),
-            jax.ShapeDtypeStruct((heads, 8, seq), F32),
-        ],
-        scratch_shapes=[
-            pltpu.VMEM((KB, QB), F32),
-            pltpu.VMEM((heads, VT, QB), F32),
-            pltpu.VMEM((heads, 8, QB), F32),
+            jax.ShapeDtypeStruct((count, heads * HD), BF16),
+            jax.ShapeDtypeStruct((heads, 8, count), F32),
         ],
         compiler_params=pltpu.CompilerParams(vmem_limit_bytes=48 * MIB),
         cost_estimate=pl.CostEstimate(
-            flops=heads * seq * seq * 256, bytes_accessed=12 * MIB, transcendentals=0
+            flops=heads * seq * count * 384, bytes_accessed=12 * MIB, transcendentals=0
         ),
         name="attend",
-    )(qa, ka, vt, bits)
+    )(block, qa, ka, vt, bits)
 
 
 def attend_back_kernel(
@@ -410,10 +430,85 @@
     return jax.nn.gelu(inputs, approximate=True)
 
 
-def scatter_rows(partial):
-    return lax.psum_scatter(
-        partial.astype(BF16), "tensor", scatter_dimension=0, tiled=True
-    ).astype(F32)
+def flip_bit(values, bit):
+    total = lax.axis_size("dp")
+    return lax.ppermute(values, "dp", [(n, n ^ (1 << bit)) for n in range(total)])
+
+
+def flip_core(values):
+    return flip_bit(values, 0)
+
+
+def flip_tensor(values):
+    return lax.ppermute(values, "tensor", [(0, 1), (1, 0)])
+
+
+def rows_at(values, start, count):
+    return lax.dynamic_slice_in_dim(values, start, count, 0)
+
+
+def my_bit(bit):
+    return (lax.axis_index("dp") >> bit) & 1
+
+
+def add_low(one, two):
+    return (one.astype(F32) + two.astype(F32)).astype(BF16)
+
+
+def halve(values, bit):
+    half = values.shape[0] // 2
+    mine = my_bit(bit)
+    return add_low(
+        rows_at(values, mine * half, half),
+        flip_bit(rows_at(values, (1 - mine) * half, half), bit),
+    )
+
+
+def both_sides(own, other, mine):
+    return jnp.where(
+        mine == 0,
+        jnp.concatenate([own, other], axis=0),
+        jnp.concatenate([other, own], axis=0),
+    )
+
+
+def double(values, bit):
+    return both_sides(values, flip_bit(values, bit), my_bit(bit))
+
+
+def sum_over_dp(values):
+    count = lax.axis_size("dp").bit_length() - 1
+    rest = list(range(1, count))
+    orders = (rest, rest[1:] + rest[:1])
+    rows, cols = values.shape
+    pieces = 2 << count
+    mine = halve(values.reshape(pieces, rows // pieces, cols), 0)
+    half = pieces // 4
+    parts = [mine[:half], mine[half:]]
+    for n in range(len(rest)):
+        parts = [halve(part, order[n]) for part, order in zip(parts, orders)]
+    for n in reversed(range(len(rest))):
+        parts = [double(part, order[n]) for part, order in zip(parts, orders)]
+    return double(jnp.concatenate(parts, axis=0), 0).reshape(rows, cols)
+
+
+def sum_over_all(values):
+    values = values + flip_tensor(values)
+    for bit in range(lax.axis_size("dp").bit_length() - 1):
+        values = values + flip_bit(values, bit)
+    return values
+
+
+def side_rows(own, other, side):
+    half = own.shape[0]
+    out = jnp.zeros((2 * half,) + own.shape[1:], own.dtype)
+    out = lax.dynamic_update_slice_in_dim(out, own, side * half, 0)
+    return lax.dynamic_update_slice_in_dim(out, other, (1 - side) * half, 0)
+
+
+def in_half(vector, side):
+    out = jnp.zeros((2 * vector.shape[0],), vector.dtype)
+    return lax.dynamic_update_slice_in_dim(out, vector, side * vector.shape[0], 0)
 
 
 def shards(
@@ -435,82 +530,134 @@
     key_count,
     out_grad,
 ):
+    side = lax.axis_index("tensor")
+    own_rows = layer_in.shape[0]
+    seq = key_index.shape[0]
+    blocks_here = own_rows // QB
+    own_at = (side * blocks_here).reshape(1).astype(jnp.int32)
+    peer_at = ((1 - side) * blocks_here).reshape(1).astype(jnp.int32)
+
+    normed_one, norm1_back = jax.vjp(layer_norm, layer_in, norm1_gain, norm1_shift)
+    normed_one_low = normed_one.astype(BF16)
+    normed_one_peer = flip_tensor(normed_one_low)
     bits = allowed_bits(key_index, key_count)
     scorer = scorer_rows(key_scorer)
-    normed_one, norm1_back = jax.vjp(layer_norm, layer_in, norm1_gain, norm1_shift)
-    normed_one_all = lax.all_gather(normed_one.astype(BF16), "tensor", axis=0, tiled=True)
-    qa, ka, va, vt, kt = qkv_heads(normed_one_all, qkv_weight, qkv_bias, scorer)
-    attended_low, logs = attend(qa, ka, vt, bits)
-    mixed = layer_in + scatter_rows(dot(attended_low, out_weight)) + out_bias
+    _, grad_low, out_weight_later = lax.optimization_barrier(
+        (normed_one_peer, out_grad.astype(BF16), out_weight)
+    )
+    out_peer = flip_tensor(out_weight_later)
+    grad_low_peer = flip_tensor(grad_low)
+
+    parts = qkv_heads(normed_one_low, qkv_weight, qkv_bias, scorer, own_at, seq)
+    parts = qkv_heads(normed_one_peer, qkv_weight, qkv_bias, scorer, peer_at, seq, parts)
+    qa, ka, va, vt, kt = parts
+    normed_one_all = side_rows(normed_one_low, normed_one_peer, side)
+
+    att_send, logs_send = attend(qa, ka, vt, bits, peer_at, own_rows)
+    att_peer = flip_tensor(att_send)
+    att_own, logs_own = attend(qa, ka, vt, bits, own_at, own_rows)
+    attended = side_rows(att_own, att_send, side)
+    logs = jnp.where(
+        side == 0,
+        jnp.concatenate([logs_own, logs_send], axis=2),
+        jnp.concatenate([logs_send, logs_own], axis=2),
+    )
+    mixed = layer_in + (dot(att_own, out_weight) + dot(att_peer, out_peer)) + out_bias
+
     normed_two, norm2_back = jax.vjp(layer_norm, mixed, norm2_gain, norm2_shift)
-    normed_two_all = lax.all_gather(normed_two.astype(BF16), "tensor", axis=0, tiled=True)
-    hidden = dot(normed_two_all, fc_weight) + fc_bias
-    active, gelu_back = jax.vjp(smooth_gelu, hidden)
-    active_low = active.astype(BF16)
-    layer_out = mixed + scatter_rows(dot(active_low, proj_weight)) + proj_bias
-    grad_proj_bias = jnp.sum(out_grad, axis=0)
-    grad_all = lax.all_gather(out_grad.astype(BF16), "tensor", axis=0, tiled=True)
-    grad_proj_weight = dot(active_low, grad_all, TN)
-    grad_active = dot(grad_all, proj_weight, NT)
-    (grad_hidden,) = gelu_back(grad_active)
-    grad_fc_bias = jnp.sum(grad_hidden, axis=0)
-    grad_hidden_low = grad_hidden.astype(BF16)
-    grad_fc_weight = dot(normed_two_all, grad_hidden_low, TN)
-    grad_normed_two = scatter_rows(dot(grad_hidden_low, fc_weight, NT))
+    normed_two_low = normed_two.astype(BF16)
+    normed_two_peer = flip_tensor(normed_two_low)
+
+    def feed_forward(norm_rows, grad_rows):
+        hidden = dot(norm_rows, fc_weight) + fc_bias
+        active, gelu_back = jax.vjp(smooth_gelu, hidden)
+        (grad_hidden,) = gelu_back(dot(grad_rows, proj_weight, NT))
+        grad_hidden_low = grad_hidden.astype(BF16)
+        return (
+            active.astype(BF16),
+            grad_hidden_low,
+            dot(grad_hidden_low, fc_weight, NT),
+            jnp.sum(grad_hidden, axis=0),
+        )
+
+    active_own, slope_own, back_own, fc_sum_own = feed_forward(normed_two_low, grad_low)
+    active_peer, slope_peer, back_peer, fc_sum_peer = feed_forward(normed_two_peer, grad_low_peer)
+    back_other = flip_tensor(back_peer.astype(BF16))
+    grad_fc_bias = fc_sum_own + fc_sum_peer
+    grad_fc_weight = dot(normed_two_low, slope_own, TN) + dot(normed_two_peer, slope_peer, TN)
+    grad_proj_weight = dot(active_own, grad_low, TN) + dot(active_peer, grad_low_peer, TN)
+    grad_fc_weight, grad_proj_weight = lax.psum(
+        (grad_fc_weight.astype(BF16), grad_proj_weight.astype(BF16)), "dp"
+    )
+    grad_normed_two = back_own + back_other.astype(F32)
     grad_mixed_part, grad_norm2_gain, grad_norm2_shift = norm2_back(grad_normed_two)
     grad_mixed = out_grad + grad_mixed_part
-    grad_out_bias = jnp.sum(grad_mixed, axis=0)
-    grad_mixed_all = lax.all_gather(grad_mixed.astype(BF16), "tensor", axis=0, tiled=True)
-    grad_out_weight = dot(attended_low, grad_mixed_all, TN)
-    grad_attended = dot(grad_mixed_all, out_weight, NT).astype(BF16)
+    grad_mixed_low = grad_mixed.astype(BF16)
+    grad_att_peer = flip_tensor(dot(grad_mixed_low, out_peer, NT).astype(BF16))
+    grad_att_own = dot(grad_mixed_low, out_weight, NT).astype(BF16)
+    grad_attended = side_rows(grad_att_own, grad_att_peer, side)
+
+    proj_own = dot(active_own, proj_weight)
+    proj_other = flip_tensor(dot(active_peer, proj_weight).astype(BF16))
+    layer_out = mixed + (proj_own + proj_other.astype(F32)) + proj_bias
+    grad_out_turned = add_low(
+        dot(grad_mixed_low, att_own, TN),
+        flip_tensor(dot(grad_mixed_low, att_peer, TN).astype(BF16)),
+    )
+
     joined_grad, grad_qkv_bias, grad_key_scorer = attend_back(
-        qa, ka, kt, va, grad_attended, attended_low, logs, bits, scorer
-    )
-    grad_qkv_weight = dot(normed_one_all, joined_grad, TN)
-    grad_normed_one = scatter_rows(dot(joined_grad, qkv_weight, NT))
+        qa, ka, kt, va, grad_attended, attended, logs, bits, scorer
+    )
+    grad_one_send = dot(rows_at(joined_grad, (1 - side) * own_rows, own_rows), qkv_weight, NT)
+    grad_one_other = flip_tensor(grad_one_send.astype(BF16))
+    grad_qkv_weight = dot(normed_one_all, joined_grad, TN).astype(BF16)
+    last = sum_over_dp(jnp.concatenate([grad_qkv_weight, grad_out_turned], axis=1))
+    joined_cols = qkv_weight.shape[1]
+    grad_qkv_weight = last[:, :joined_cols]
+    grad_out_weight = last[:, joined_cols:].T
+    grad_one_own = dot(rows_at(joined_grad, side * own_rows, own_rows), qkv_weight, NT)
+    grad_normed_one = grad_one_own + grad_one_other.astype(F32)
     grad_in_part, grad_norm1_gain, grad_norm1_shift = norm1_back(grad_normed_one)
     input_grad = grad_mixed + grad_in_part
-    (grad_out_weight, grad_fc_weight, grad_proj_weight) = lax.psum(
-        tuple(g.astype(BF16) for g in (grad_out_weight, grad_fc_weight, grad_proj_weight)), "dp"
-    )
-    grad_qkv_weight = lax.psum(grad_qkv_weight.astype(BF16), "dp")
-    (grad_qkv_bias, grad_key_scorer, grad_fc_bias) = lax.psum(
-        (grad_qkv_bias, grad_key_scorer, grad_fc_bias), "dp"
-    )
-    (
-        grad_out_bias,
-        grad_proj_bias,
+
+    sums = [
+        jnp.sum(grad_mixed, axis=0),
+        jnp.sum(out_grad, axis=0),
         grad_norm1_gain,
         grad_norm1_shift,
         grad_norm2_gain,
         grad_norm2_shift,
-    ) = lax.psum(
-        (
-            grad_out_bias,
-            grad_proj_bias,
-            grad_norm1_gain,
-            grad_norm1_shift,
-            grad_norm2_gain,
-            grad_norm2_shift,
-        ),
-        ("dp", "tensor"),
-    )
+        in_half(grad_qkv_bias, side),
+        in_half(grad_key_scorer, side),
+        in_half(grad_fc_bias, side),
+    ]
+    packed = sum_over_all(jnp.concatenate(sums).reshape(-1, LANES)).reshape(-1)
+    ends = []
+    at = 0
+    for part in sums:
+        ends.append(packed[at : at + part.shape[0]])
+        at += part.shape[0]
+
+    def mine_of(vector):
+        half = vector.shape[0] // 2
+        return lax.dynamic_slice_in_dim(vector, side * half, half, 0)
+
     return (
         layer_out,
         input_grad,
         grad_qkv_weight.astype(F32),
-        grad_qkv_bias,
-        grad_key_scorer,
+        mine_of(ends[6]),
+        mine_of(ends[7]),
         grad_out_weight.astype(F32),
-        grad_out_bias,
+        ends[0],
         grad_fc_weight.astype(F32),
-        grad_fc_bias,
+        mine_of(ends[8]),
         grad_proj_weight.astype(F32),
-        grad_proj_bias,
-        grad_norm1_gain,
-        grad_norm1_shift,
-        grad_norm2_gain,
-        grad_norm2_shift,
+        ends[1],
+        ends[2],
+        ends[3],
+        ends[4],
+        ends[5],
     )
 
 

time: 769 us -> 510 us (0.66)
  waiting for transfers between devices: 352 us -> 163 us
  blocking collectives: 104 us -> 0 us
  other arithmetic: 52.4 us -> 30.5 us
  starting transfers between devices: 12.3 us -> 31.2 us
  local copies, waits for them, and re-layouts: 17.2 us -> 35.7 us
  matrix products: 90.9 us -> 102 us
    ppermute x0 -> x29, waiting for transfers between devices: none -> 163 us  [the longest x11 140 us: flip_tensor(): return lax.ppermute(values, 'tensor', [(0, 1), (1, 0)])]
    reduce_scatter x4 -> x0, waiting for transfers between devices: 140 us -> none  [scatter_rows(): lax.psum_scatter(partial.astype(BF16), 'tensor', scatter_dimension=0, til...]
    all_gather x4 -> x0, waiting for transfers between devices: 134 us -> none  [the longest x1 40.3 us: shards(): lax.all_gather(normed_two.astype(BF16), 'tensor', axis=0, tiled=True)]
    psum x2 -> x0, blocking collectives: 104 us -> none  [the longest x1 64.1 us: shards(): lax.psum((grad_qkv_bias, grad_key_scorer, grad_fc_bias), 'dp')]
    psum x1, waiting for transfers between devices: 78.2 us -> 0.02 us  [shards(): lax.psum((grad_fc_weight.astype(BF16), grad_proj_weight.astype(BF16)), 'dp')]
    ppermute x0 -> x29, starting transfers between devices: none -> 31.1 us  [the longest x18 20.8 us: flip_bit(): return lax.ppermute(values, 'dp', [(n, n ^ 1 << bit) for n in range(total)])]
    reduce_sum x6 -> x2, other arithmetic: 21.6 us -> 1.86 us  [the longest x1 1.45 us: shards(): jnp.sum(out_grad, axis=0)]
    reduce_scatter x4 -> x0, starting transfers between devices: 12.1 us -> none  [scatter_rows(): lax.psum_scatter(partial.astype(BF16), 'tensor', scatter_dimension=0, til...]
  transfers between devices with their start and end apart: 9 -> 30, of which waited for: 9 -> 18; matrix products, arithmetic and copies ran while one was open for 10% -> 23% of each run, Pallas kernels for 1% -> 18%
where the time goes in v2:
time: 510 us; the launch traced here: 500 us
  waiting for transfers between devices  163 us (32%)
  Pallas kernels  122 us (24%)
  matrix products  102 us (20%)
  local copies, waits for them, and re-layouts  35.7 us (7%)
  starting transfers between devices  31.2 us (6%)
  other arithmetic  30.5 us (6%)
  between operations  15.4 us (3%)
    ppermute x11, waiting for transfers between devices, flip_tensor(): return lax.ppermute(values, 'tensor', [(0, 1), (1, 0)])  140 us
    dot_general x21, matrix products, dot(): return lax.dot_general(a, b, dims, preferred_element_type=F32)  102 us
    pallas_call x1, Pallas kernels, attend_back(): pl.pallas_call(attend_back_kernel, grid=(seq // KB,), in_specs=[whole_blo...  61.6 us
    pallas_call x2, Pallas kernels, attend(): pl.pallas_call(attend_kernel, grid_spec=pltpu.PrefetchScalarGridSpec(num_...  30.8 us
    ppermute x18, waiting for transfers between devices, flip_bit(): return lax.ppermute(values, 'dp', [(n, n ^ 1 << bit) for n in range(total)])  23.4 us
    unnamed x135, local copies, waits for them, and re-layouts  21.6 us
    ppermute x18, starting transfers between devices, flip_bit(): return lax.ppermute(values, 'dp', [(n, n ^ 1 << bit) for n in range(total)])  20.8 us
    pallas_call x2, Pallas kernels, qkv_heads(): pl.pallas_call(kernel, grid_spec=pltpu.PrefetchScalarGridSpec(num_scalar_...  18.7 us
  transfers between devices with their start and end apart: 30, of which 18 were waited for; matrix products, arithmetic and copies ran while one was open for 23% of the time, Pallas kernels for 18%

profile of v2, /device:TPU:0, one launch (start us, length us, event | category | flops | bytes accessed | tf_op | source)
XLA Modules:
  0.0 500.4 jit_solution(9932751160876814395)
XLA Ops:
  22.7 11.1 %allowed_bits.1.bits_ref = s32[128,2048]{1,0:T(8,128)} custom-call(s32[64,2048]{1,0:T(8,128)} %and_bitcast_fusion.low_ref, s32[64,2048]{1,0:T(8,128)} %bitcast_select_fusion.flag_ref), custom_call_target="tpu_custom_call" | custom-call | flops 50331648 | bytes 1048576 | tf_op jit(solution)/shard_map/allowed_bits/pallas_call | solution.py:84
  35.3 9.4 %qkv_heads.2 = (bf16[6,2048,128]{2,1,0:T(8,128)(2,1)S(1)}, bf16[6,2048,128]{2,1,0:T(8,128)(2,1)S(1)}, bf16[6,2048,128]{2,1,0:T(8,128)(2,1)}, bf16[6,80,2048]{2,1,0:T(8,128)(2,1)S(1)}, bf16[6,64,2048]{2,1,0:T(8,128)(2,1)S(1)}) custom-call(s32[1]{0:T(128)} %bitcast.at_ref, bf16[1024,768]{1,0:T(8,128)(2,1)} %get-tuple-element.98.norm_ref, ...), custom_call_target="tpu_custom_call" | custom-call | flops 3623878656 | bytes 10485760 | tf_op jit(solution)/shard_map/qkv_heads/pallas_call | solution.py:166
  44.7 10.9 %collective-permute-done.norm_ref = bf16[1024,768]{1,0:T(8,128)(2,1)} collective-permute-done((bf16[1024,768]{1,0:T(8,128)(2,1)}, bf16[1024,768]{1,0:T(8,128)(2,1)}, u32[]{:S(2)}, u32[]{:S(2)}) %collective-permute-start) | collective-permute-done | bytes 1572896 | tf_op jit(solution)/shard_map/ppermute | solution.py:443
  55.5 9.4 %qkv_heads.3 = (bf16[6,2048,128]{2,1,0:T(8,128)(2,1)S(1)}, bf16[6,2048,128]{2,1,0:T(8,128)(2,1)S(1)}, bf16[6,2048,128]{2,1,0:T(8,128)(2,1)}, bf16[6,80,2048]{2,1,0:T(8,128)(2,1)S(1)}, bf16[6,64,2048]{2,1,0:T(8,128)(2,1)S(1)}) custom-call(s32[1]{0:T(128)} %bitcast.1.at_ref, ...), custom_call_target="tpu_custom_call", output_to_operand_aliasing={{0}: (5, {}), {1}: (6, {}), {2}: (7, {}), {3}: (8, {}), {4}... | custom-call | flops 3623878656 | bytes 10485760 | tf_op jit(solution)/shard_map/qkv_heads/pallas_call | solution.py:166
  69.4 20.8 %attend.3 = (bf16[1024,384]{1,0:T(8,128)(2,1)}, f32[6,8,1024]{2,1,0:T(8,128)S(1)}) custom-call(s32[1]{0:T(128)} %bitcast.1.at_ref, bf16[6,2048,128]{2,1,0:T(8,128)(2,1)} %copy-done.1, bf16[6,2048,128]{2,1,0:T(8,128)(2,1)} %copy-done.2, bf16[6,80,2048]{2,1,0:T(8,128)(2,1)S(1)} %get-tuple-element.41.vt_ref, s32[128,2048]{1,0:T(8,128)S(1)} %copy-done.10), custom_call_target="tpu_custom_call" | custom-call | flops 4831838208 | bytes 12582912 | tf_op jit(solution)/shard_map/attend/pallas_call | solution.py:233
  96.5 10.0 %attend.2 = (bf16[1024,384]{1,0:T(8,128)(2,1)S(1)}, f32[6,8,1024]{2,1,0:T(8,128)S(1)}) custom-call(s32[1]{0:T(128)} %bitcast.at_ref, bf16[6,2048,128]{2,1,0:T(8,128)(2,1)} %copy-done.1, bf16[6,2048,128]{2,1,0:T(8,128)(2,1)} %copy-done.2, bf16[6,80,2048]{2,1,0:T(8,128)(2,1)S(1)} %copy-done.4, s32[128,2048]{1,0:T(8,128)S(1)} %copy-done.11), custom_call_target="tpu_custom_call" | custom-call | flops 4831838208 | bytes 12582912 | tf_op jit(solution)/shard_map/attend/pallas_call | solution.py:233
  106.9 16.8 %collective-permute-done.2 = bf16[384,768]{1,0:T(8,128)(2,1)} collective-permute-done((bf16[384,768]{1,0:T(8,128)(2,1)}, bf16[384,768]{1,0:T(8,128)(2,1)}, u32[]{:S(2)}, u32[]{:S(2)}) %collective-permute-start.2) | collective-permute-done | bytes 589856 | tf_op jit(solution)/shard_map/ppermute | solution.py:443
  134.5 4.6 fusion.48
  139.1 18.2 %collective-permute-done.5 = bf16[1024,768]{1,0:T(8,128)(2,1)} collective-permute-done((bf16[1024,768]{1,0:T(8,128)(2,1)}, bf16[1024,768]{1,0:T(8,128)(2,1)}, u32[]{:S(2)}, u32[]{:S(2)}) %collective-permute-start.5) | collective-permute-done | bytes 1572896 | tf_op jit(solution)/shard_map/ppermute | solution.py:443
  157.3 6.0 %fusion.50 = f32[1024,1536]{1,0:T(8,128)} fusion(bf16[1024,768]{1,0:T(8,128)(2,1)} %collective-permute-done.5, bf16[1536,768]{1,0:T(8,128)(2,1)S(1)} %copy-done), kind=kOutput, calls=%fused_computation.135 | convolution fusion | flops 2415919104 | bytes 10223616 | tf_op jit(solution)/shard_map/dot_general | solution.py:30
  163.3 25.8 %collective-permute-done.3 = bf16[1024,768]{1,0:T(8,128)(2,1)S(1)} collective-permute-done((bf16[1024,768]{1,0:T(8,128)(2,1)S(1)}, bf16[1024,768]{1,0:T(8,128)(2,1)S(1)}, u32[]{:S(2)}, u32[]{:S(2)}) %collective-permute-start.3) | collective-permute-done | bytes 1572896 | tf_op jit(solution)/shard_map/ppermute | solution.py:443
  190.3 4.6 fusion.49
  194.9 16.4 %fusion.39 = (f32[1536]{0:T(1024)S(1)}, bf16[1024,1536]{1,0:T(8,128)(2,1)S(1)}, bf16[1024,1536]{1,0:T(8,128)(2,1)}, f32[1536]{0:T(1024)S(1)}, bf16[1024,1536]{1,0:T(8,128)(2,1)}) fusion(f32[1024,1536]{1,0:T(8,128)} %fusion.48, f32[1536]{0:T(1024)S(1)} %copy-done.55, f32[1024,1536]{1,0:T(8,128)} %fusion.49, f32[1024,1536]{1,0:T(8,128)} %fusion.50, ...), kind=kOutput, calls=%fused_computation.125 | convolution fusion | flops 2488267776 | bytes 32262144 | tf_op jit(solution)/shard_map/dot_general | solution.py:30
  215.1 3.8 convolution_convert_fusion.1
  219.1 3.7 convolution_convert_fusion.2
  224.5 4.0 add_convert_fusion.1
  228.5 4.2 fusion.51
  232.7 5.4 %add_convert_fusion = bf16[1536,768]{1,0:T(8,128)(2,1)} fusion(f32[1536,768]{1,0:T(8,128)S(1)} %fusion.51, bf16[1024,768]{1,0:T(8,128)(2,1)S(1)} %copy-done.30, f32[1024,1536]{1,0:T(8,128)S(1)} %bitcast.82, f32[1536]{0:T(1024)S(1)} %copy-done.55), kind=kOutput, calls=%fused_computation.20 | convolution fusion | flops 2434007040 | bytes 14948352 | tf_op jit(solution)/shard_map/dot_general | solution.py:30
  238.1 18.3 %collective-permute-done.6 = bf16[1024,768]{1,0:T(8,128)(2,1)} collective-permute-done((bf16[1024,768]{1,0:T(8,128)(2,1)}, bf16[1024,768]{1,0:T(8,128)(2,1)}, u32[]{:S(2)}, u32[]{:S(2)}) %collective-permute-start.6) | collective-permute-done | bytes 1572896 | tf_op jit(solution)/shard_map/ppermute | solution.py:443
  256.5 8.0 %multiply_reduce_fusion = (f32[768]{0:T(1024)}, f32[1024]{0:T(1024)S(1)}, f32[768]{0:T(1024)}, f32[1024,768]{1,0:T(8,128)S(1)}) fusion(f32[1024,768]{1,0:T(8,128)} %copy-done.16, f32[1024]{0:T(1024)S(1)} %fusion.35, f32[1024]{0:T(1024)S(1)} %broadcast_multiply_fusion, f32[768]{0:T(1024)S(1)} %copy-done.39, bf16[1024,768]{1,0:T(8,128)(2,1)} %collective-permute-done.6, ...), kind=kOutput, calls=%fused_computation.23 | convolution fusion | flops 2423780864 | bytes 13390848 | tf_op jit(solution)/shard_map/dot_general | solution.py:30
  278.3 24.4 %collective-permute-done.9 = bf16[768,384]{1,0:T(8,128)(2,1)S(1)} collective-permute-done((bf16[768,384]{1,0:T(8,128)(2,1)S(1)}, bf16[768,384]{1,0:T(8,128)(2,1)S(1)}, u32[]{:S(2)}, u32[]{:S(2)}) %collective-permute-start.9) | collective-permute-done | bytes 589856 | tf_op jit(solution)/shard_map/ppermute | solution.py:443
  303.8 13.2 %collective-permute-done.7 = bf16[1024,384]{1,0:T(8,128)(2,1)S(1)} collective-permute-done((bf16[1024,384]{1,0:T(8,128)(2,1)S(1)}, bf16[1024,384]{1,0:T(8,128)(2,1)S(1)}, u32[]{:S(2)}, u32[]{:S(2)}) %collective-permute-start.7) | collective-permute-done | bytes 786464 | tf_op jit(solution)/shard_map/ppermute | solution.py:443
  317.9 61.6 %attend_back.1 = (bf16[2048,1152]{1,0:T(8,128)(2,1)}, f32[1,1152]{1,0:T(1,128)}, f32[6,128]{1,0:T(8,128)}) custom-call(bf16[6,2048,128]{2,1,0:T(8,128)(2,1)} %copy-done.1, bf16[6,2048,128]{2,1,0:T(8,128)(2,1)} %copy-done.2, bf16[6,64,2048]{2,1,0:T(8,128)(2,1)} %copy-done.9, bf16[6,2048,128]{2,1,0:T(8,128)(2,1)} %get-tuple-element.47.va_ref, ...), custom_call_target="tpu_custom_call" | custom-call | flops 16106127360 | bytes 25165824 | tf_op jit(solution)/shard_map/attend_back/pallas_call | solution.py:382
  379.5 7.6 %convolution_convert_fusion = bf16[768,1152]{1,0:T(8,128)(2,1)S(1)} fusion(bf16[2048,768]{1,0:T(8,128)(2,1)} %copy-done.25, bf16[2048,1152]{1,0:T(8,128)(2,1)} %get-tuple-element.50), kind=kOutput, calls=%fused_computation.22 | convolution fusion | flops 3624763392 | bytes 9633792 | tf_op jit(solution)/shard_map/dot_general | solution.py:30
  388.9 9.4 %add_add_fusion.4 = f32[1024,768]{1,0:T(8,128)} fusion(f32[1024,768]{1,0:T(8,128)S(1)} %copy-done.18, bf16[1024,768]{1,0:T(8,128)(2,1)} %collective-permute-done.4, f32[768]{0:T(1024)S(1)} %copy-done.56, bf16[1536,768]{1,0:T(8,128)(2,1)S(1)} %copy-done, f32[1024,1536]{1,0:T(8,128)} %fusion.48, f32[1536]{0:T(1024)S(1)} %copy-done.55), kind=kOutput, calls=%fused_computation.31 | convolution fusion | flops 2434793472 | bytes 16524288 | tf_op jit(solution)/shard_map/dot_general | solution.py:30
  412.1 4.6 convert_element_type.191
  422.8 7.0 %collective-permute-done.17 = bf16[4,24,1536]{2,1,0:T(8,128)(2,1)S(1)} collective-permute-done((bf16[4,24,1536]{2,1,0:T(8,128)(2,1)S(1)}, bf16[4,24,1536]{2,1,0:T(8,128)(2,1)S(1)}, u32[]{:S(2)}, u32[]{:S(2)}) %collective-permute-start.17) | collective-permute-done | bytes 294944 | tf_op jit(solution)/shard_map/ppermute | solution.py:435
  432.4 9.0 %collective-permute-done.8 = bf16[1024,768]{1,0:T(8,128)(2,1)} collective-permute-done((bf16[1024,768]{1,0:T(8,128)(2,1)}, bf16[1024,768]{1,0:T(8,128)(2,1)}, u32[]{:S(2)}, u32[]{:S(2)}) %collective-permute-start.8) | collective-permute-done | bytes 1572896 | tf_op jit(solution)/shard_map/ppermute | solution.py:443
  441.4 5.1 %multiply_reduce_fusion.1 = (f32[768]{0:T(1024)S(1)}, f32[1024]{0:T(1024)S(1)}, f32[768]{0:T(1024)S(1)}, f32[1024,768]{1,0:T(8,128)S(1)}) fusion(f32[1024,768]{1,0:T(8,128)S(1)} %copy-done.15, f32[1024]{0:T(1024)S(1)} %copy-done.36, f32[1024]{0:T(1024)S(1)} %copy-done.33, f32[768]{0:T(1024)S(1)} %copy-done.41, ...), kind=kOutput, calls=%fused_computation.24 | convolution fusion | flops 1819801088 | bytes 12014596 | tf_op jit(solution)/shard_map/dot_general | solution.py:30
  447.3 3.5 collective-permute-done.24
  460.1 4.9 collective-permute-done.14
  467.8 4.4 collective-permute-done.15
  (274 shorter events, 119.3 us)
Async XLA Ops:
  7.2 150.1 %copy-start = (bf16[1536,768]{1,0:T(8,128)(2,1)S(1)}, bf16[1536,768]{1,0:T(8,128)(2,1)}, u32[]{:S(2)}) copy-start(bf16[1536,768]{1,0:T(8,128)(2,1)} %param.25) | copy-start | bytes 7077892
  7.2 404.9 %all-reduce.4.cloned.1.call-start = ((), (), s32[]{:S(2)}) async-start(), calls=%async_computation | async-start | bytes 9437184 | tf_op jit(solution)/shard_map/psum | solution.py:589
  17.8 37.7 %collective-permute-start = (bf16[1024,768]{1,0:T(8,128)(2,1)}, bf16[1024,768]{1,0:T(8,128)(2,1)}, u32[]{:S(2)}, u32[]{:S(2)}) collective-permute-start(bf16[1024,768]{1,0:T(8,128)(2,1)} %get-tuple-element.98.norm_ref), channel_id=1, source_target_pairs={{0,1},{1,0},{2,3},{3,2},{4,5},{5,4},{6,7},{7,6},{8,9},{9,8},{10,11... | collective-permute-start | bytes 4718600 | tf_op jit(solution)/shard_map/ppermute | solution.py:443
  20.9 34.6 %copy-start.12 = (f32[6,128]{1,0:T(8,128)}, f32[6,128]{1,0:T(8,128)S(1)}, u32[]{:S(2)}) copy-start(f32[6,128]{1,0:T(8,128)S(1)} %pad.4.scorer_ref) | copy-start | bytes 9220
  90.2 33.4 %collective-permute-start.1 = (bf16[1024,384]{1,0:T(8,128)(2,1)}, bf16[1024,384]{1,0:T(8,128)(2,1)}, u32[]{:S(2)}, u32[]{:S(2)}) collective-permute-start(bf16[1024,384]{1,0:T(8,128)(2,1)} %get-tuple-element.43), channel_id=1, source_target_pairs={{0,1},{1,0},{2,3},{3,2},{4,5},{5,4},{6,7},{7,6},{8,9},{9,8},{10,11... | collective-permute-start | bytes 2359304 | tf_op jit(solution)/shard_map/ppermute | solution.py:443
  91.6 32.0 %collective-permute-start.2 = (bf16[384,768]{1,0:T(8,128)(2,1)}, bf16[384,768]{1,0:T(8,128)(2,1)}, u32[]{:S(2)}, u32[]{:S(2)}) collective-permute-start(bf16[384,768]{1,0:T(8,128)(2,1)} %param.21), channel_id=1, source_target_pairs={{0,1},{1,0},{2,3},{3,2},{4,5},{5,4},{6,7},{7,6},{8,9},{9,8},{10,11... | collective-permute-start | bytes 1769480 | tf_op jit(solution)/shard_map/ppermute | solution.py:443
  93.7 63.7 %collective-permute-start.5 = (bf16[1024,768]{1,0:T(8,128)(2,1)}, bf16[1024,768]{1,0:T(8,128)(2,1)}, u32[]{:S(2)}, u32[]{:S(2)}) collective-permute-start(bf16[1024,768]{1,0:T(8,128)(2,1)} %get-tuple-element.45), channel_id=1, source_target_pairs={{0,1},{1,0},{2,3},{3,2},{4,5},{5,4},{6,7},{7,6},{8,9},{9,8},{10,11... | collective-permute-start | bytes 4718600 | tf_op jit(solution)/shard_map/ppermute | solution.py:443
  129.8 59.4 %collective-permute-start.3 = (bf16[1024,768]{1,0:T(8,128)(2,1)S(1)}, bf16[1024,768]{1,0:T(8,128)(2,1)S(1)}, u32[]{:S(2)}, u32[]{:S(2)}) collective-permute-start(bf16[1024,768]{1,0:T(8,128)(2,1)S(1)} %add_convert_fusion.2), channel_id=1, source_target_pairs={{0,1},{1,0},{2,3},{3,2},{4,5},{5,4},{6,7},{7,6},{8,9},{9,8},{10,11... | collective-permute-start | bytes 4718600 | tf_op jit(solution)/shard_map/ppermute | solution.py:443
  218.8 37.6 %collective-permute-start.6 = (bf16[1024,768]{1,0:T(8,128)(2,1)}, bf16[1024,768]{1,0:T(8,128)(2,1)}, u32[]{:S(2)}, u32[]{:S(2)}) collective-permute-start(bf16[1024,768]{1,0:T(8,128)(2,1)} %convolution_convert_fusion.1), channel_id=1, source_target_pairs={{0,1},{1,0},{2,3},{3,2},{4,5},{5,4},{6,7},{7,6},{8,9},{9,8},{10,11... | collective-permute-start | bytes 4718600 | tf_op jit(solution)/shard_map/ppermute | solution.py:443
  222.8 164.7 %collective-permute-start.4 = (bf16[1024,768]{1,0:T(8,128)(2,1)}, bf16[1024,768]{1,0:T(8,128)(2,1)}, u32[]{:S(2)}, u32[]{:S(2)}) collective-permute-start(bf16[1024,768]{1,0:T(8,128)(2,1)} %convolution_convert_fusion.2), channel_id=1, source_target_pairs={{0,1},{1,0},{2,3},{3,2},{4,5},{5,4},{6,7},{7,6},{8,9},{9,8},{10,11... | collective-permute-start | bytes 4718600 | tf_op jit(solution)/shard_map/ppermute | solution.py:443
  269.8 33.0 %collective-permute-start.9 = (bf16[768,384]{1,0:T(8,128)(2,1)S(1)}, bf16[768,384]{1,0:T(8,128)(2,1)S(1)}, u32[]{:S(2)}, u32[]{:S(2)}) collective-permute-start(bf16[768,384]{1,0:T(8,128)(2,1)S(1)} %convolution_convert_fusion.5), channel_id=1, source_target_pairs={{0,1},{1,0},{2,3},{3,2},{4,5},{5,4},{6,7},{7,6},{8,9},{9,8},{10,11... | collective-permute-start | bytes 1769480 | tf_op jit(solution)/shard_map/ppermute | solution.py:443
  272.2 44.7 %collective-permute-start.7 = (bf16[1024,384]{1,0:T(8,128)(2,1)S(1)}, bf16[1024,384]{1,0:T(8,128)(2,1)S(1)}, u32[]{:S(2)}, u32[]{:S(2)}) collective-permute-start(bf16[1024,384]{1,0:T(8,128)(2,1)S(1)} %convolution_convert_fusion.3), channel_id=1, source_target_pairs={{0,1},{1,0},{2,3},{3,2},{4,5},{5,4},{6,7},{7,6},{8,9},{9,8},{10,11... | collective-permute-start | bytes 2359304 | tf_op jit(solution)/shard_map/ppermute | solution.py:443
  387.4 13.6 %collective-permute-start.10 = (bf16[16,24,1536]{2,1,0:T(8,128)(2,1)S(1)}, bf16[16,24,1536]{2,1,0:T(8,128)(2,1)S(1)}, u32[]{:S(2)}, u32[]{:S(2)}) collective-permute-start(bf16[16,24,1536]{2,1,0:T(8,128)(2,1)S(1)} %constant_dynamic-slice_fusion.6), channel_id=1, source_target_pairs={{0,2},{2,0},{4,6},{6,4},{8,10},{10,8},{12,14},{14,12},{16,18},{18,... | collective-permute-start | bytes 3538952 | tf_op jit(solution)/shard_map/ppermute | solution.py:435
  402.1 19.1 %collective-permute-start.11 = (bf16[4,24,1536]{2,1,0:T(8,128)(2,1)}, bf16[4,24,1536]{2,1,0:T(8,128)(2,1)}, u32[]{:S(2)}, u32[]{:S(2)}) collective-permute-start(bf16[4,24,1536]{2,1,0:T(8,128)(2,1)} %constant_dynamic-slice_fusion.5), channel_id=1, source_target_pairs={{0,4},{2,6},{4,0},{6,2},{8,12},{10,14},{12,8},{14,10},{16,20},{18,... | collective-permute-start | bytes 884744 | tf_op jit(solution)/shard_map/ppermute | solution.py:435
  406.5 35.0 %collective-permute-start.8 = (bf16[1024,768]{1,0:T(8,128)(2,1)}, bf16[1024,768]{1,0:T(8,128)(2,1)}, u32[]{:S(2)}, u32[]{:S(2)}) collective-permute-start(bf16[1024,768]{1,0:T(8,128)(2,1)} %fusion.18), channel_id=1, source_target_pairs={{0,1},{1,0},{2,3},{3,2},{4,5},{5,4},{6,7},{7,6},{8,9},{9,8},{10,11... | collective-permute-start | bytes 4718600 | tf_op jit(solution)/shard_map/ppermute | solution.py:443
  419.6 10.2 %collective-permute-start.17 = (bf16[4,24,1536]{2,1,0:T(8,128)(2,1)S(1)}, bf16[4,24,1536]{2,1,0:T(8,128)(2,1)S(1)}, u32[]{:S(2)}, u32[]{:S(2)}) collective-permute-start(bf16[4,24,1536]{2,1,0:T(8,128)(2,1)S(1)} %constant_dynamic-slice_fusion.2), channel_id=1, source_target_pairs={{0,8},{2,10},{4,12},{6,14},{8,0},{10,2},{12,4},{14,6},{16,24},{18,... | collective-permute-start | bytes 884744 | tf_op jit(solution)/shard_map/ppermute | solution.py:435
  422.3 28.5 %collective-permute-start.12 = (bf16[2,24,1536]{2,1,0:T(8,128)(2,1)S(1)}, bf16[2,24,1536]{2,1,0:T(8,128)(2,1)S(1)}, u32[]{:S(2)}, u32[]{:S(2)}) collective-permute-start(bf16[2,24,1536]{2,1,0:T(8,128)(2,1)S(1)} %constant_dynamic-slice_fusion.4), channel_id=1, source_target_pairs={{0,8},{2,10},{4,12},{6,14},{8,0},{10,2},{12,4},{14,6},{16,24},{18,... | collective-permute-start | bytes 442376 | tf_op jit(solution)/shard_map/ppermute | solution.py:435
  430.0 23.6 %collective-permute-start.18 = (bf16[2,24,1536]{2,1,0:T(8,128)(2,1)S(1)}, bf16[2,24,1536]{2,1,0:T(8,128)(2,1)S(1)}, u32[]{:S(2)}, u32[]{:S(2)}) collective-permute-start(bf16[2,24,1536]{2,1,0:T(8,128)(2,1)S(1)} %constant_dynamic-slice_fusion.1), channel_id=1, source_target_pairs={{0,16},{2,18},{4,20},{6,22},{8,24},{10,26},{12,28},{14,30},{16,0},... | collective-permute-start | bytes 442376 | tf_op jit(solution)/shard_map/ppermute | solution.py:435
  446.6 4.1 collective-permute-start.24
  450.8 3.7 collective-permute-start.25
  450.9 7.2 %collective-permute-start.13 = (bf16[1,24,1536]{2,1,0:T(8,128)(2,1)S(1)}, bf16[1,24,1536]{2,1,0:T(8,128)(2,1)S(1)}, u32[]{:S(2)}, u32[]{:S(2)}) collective-permute-start(bf16[1,24,1536]{2,1,0:T(8,128)(2,1)S(1)} %constant_dynamic-slice_fusion.3), channel_id=1, source_target_pairs={{0,16},{2,18},{4,20},{6,22},{8,24},{10,26},{12,28},{14,30},{16,0},... | collective-permute-start | bytes 221192 | tf_op jit(solution)/shard_map/ppermute | solution.py:435
  453.6 5.7 %collective-permute-start.19 = (bf16[1,24,1536]{2,1,0:T(8,128)(2,1)S(1)}, bf16[1,24,1536]{2,1,0:T(8,128)(2,1)S(1)}, u32[]{:S(2)}, u32[]{:S(2)}) collective-permute-start(bf16[1,24,1536]{2,1,0:T(8,128)(2,1)S(1)} %constant_dynamic-slice_fusion), channel_id=1, source_target_pairs={{0,4},{2,6},{4,0},{6,2},{8,12},{10,14},{12,8},{14,10},{16,20},{18,... | collective-permute-start | bytes 221192 | tf_op jit(solution)/shard_map/ppermute | solution.py:435
  454.4 21.5 %collective-permute-start.26 = (f32[84,128]{1,0:T(8,128)S(1)}, f32[84,128]{1,0:T(8,128)S(1)}, u32[]{:S(2)}, u32[]{:S(2)}) collective-permute-start(f32[84,128]{1,0:T(8,128)S(1)} %fusion.90), channel_id=1, source_target_pairs={{0,4},{2,6},{4,0},{6,2},{8,12},{10,14},{12,8},{14,10},{16,20},{18,... | collective-permute-start | bytes 129032 | tf_op jit(solution)/shard_map/ppermute | solution.py:435
  458.1 6.8 %collective-permute-start.14 = (bf16[1,24,1536]{2,1,0:T(8,128)(2,1)S(1)}, bf16[1,24,1536]{2,1,0:T(8,128)(2,1)S(1)}, u32[]{:S(2)}, u32[]{:S(2)}) collective-permute-start(bf16[1,24,1536]{2,1,0:T(8,128)(2,1)S(1)} %add_convert_fusion.10), channel_id=1, source_target_pairs={{0,16},{2,18},{4,20},{6,22},{8,24},{10,26},{12,28},{14,30},{16,0},... | collective-permute-start | bytes 221192 | tf_op jit(solution)/shard_map/ppermute | solution.py:435
  459.3 5.7 %collective-permute-start.20 = (bf16[1,24,1536]{2,1,0:T(8,128)(2,1)S(1)}, bf16[1,24,1536]{2,1,0:T(8,128)(2,1)S(1)}, u32[]{:S(2)}, u32[]{:S(2)}) collective-permute-start(bf16[1,24,1536]{2,1,0:T(8,128)(2,1)S(1)} %add_convert_fusion.9), channel_id=1, source_target_pairs={{0,4},{2,6},{4,0},{6,2},{8,12},{10,14},{12,8},{14,10},{16,20},{18,... | collective-permute-start | bytes 221192 | tf_op jit(solution)/shard_map/ppermute | solution.py:435
  465.0 7.2 %collective-permute-start.15 = (bf16[2,24,1536]{2,1,0:T(8,128)(2,1)S(1)}, bf16[2,24,1536]{2,1,0:T(8,128)(2,1)S(1)}, u32[]{:S(2)}, u32[]{:S(2)}) collective-permute-start(bf16[2,24,1536]{2,1,0:T(8,128)(2,1)S(1)} %maximum_select_fusion.6), channel_id=1, source_target_pairs={{0,8},{2,10},{4,12},{6,14},{8,0},{10,2},{12,4},{14,6},{16,24},{18,... | collective-permute-start | bytes 442376 | tf_op jit(solution)/shard_map/ppermute | solution.py:435
  465.1 9.1 %collective-permute-start.21 = (bf16[2,24,1536]{2,1,0:T(8,128)(2,1)S(1)}, bf16[2,24,1536]{2,1,0:T(8,128)(2,1)S(1)}, u32[]{:S(2)}, u32[]{:S(2)}) collective-permute-start(bf16[2,24,1536]{2,1,0:T(8,128)(2,1)S(1)} %maximum_select_fusion.7), channel_id=1, source_target_pairs={{0,16},{2,18},{4,20},{6,22},{8,24},{10,26},{12,28},{14,30},{16,0},... | collective-permute-start | bytes 442376 | tf_op jit(solution)/shard_map/ppermute | solution.py:435
  472.2 6.8 %collective-permute-start.16 = (bf16[4,24,1536]{2,1,0:T(8,128)(2,1)S(1)}, bf16[4,24,1536]{2,1,0:T(8,128)(2,1)S(1)}, u32[]{:S(2)}, u32[]{:S(2)}) collective-permute-start(bf16[4,24,1536]{2,1,0:T(8,128)(2,1)S(1)} %maximum_select_fusion.4), channel_id=1, source_target_pairs={{0,4},{2,6},{4,0},{6,2},{8,12},{10,14},{12,8},{14,10},{16,20},{18,... | collective-permute-start | bytes 884744 | tf_op jit(solution)/shard_map/ppermute | solution.py:435
  474.3 6.8 %collective-permute-start.22 = (bf16[4,24,1536]{2,1,0:T(8,128)(2,1)S(1)}, bf16[4,24,1536]{2,1,0:T(8,128)(2,1)S(1)}, u32[]{:S(2)}, u32[]{:S(2)}) collective-permute-start(bf16[4,24,1536]{2,1,0:T(8,128)(2,1)S(1)} %maximum_select_fusion.5), channel_id=1, source_target_pairs={{0,8},{2,10},{4,12},{6,14},{8,0},{10,2},{12,4},{14,6},{16,24},{18,... | collective-permute-start | bytes 884744 | tf_op jit(solution)/shard_map/ppermute | solution.py:435
  476.0 5.5 %collective-permute-start.27 = (f32[84,128]{1,0:T(8,128)S(1)}, f32[84,128]{1,0:T(8,128)S(1)}, u32[]{:S(2)}, u32[]{:S(2)}) collective-permute-start(f32[84,128]{1,0:T(8,128)S(1)} %add.281), channel_id=1, source_target_pairs={{0,8},{2,10},{4,12},{6,14},{8,0},{10,2},{12,4},{14,6},{16,24},{18,... | collective-permute-start | bytes 129032 | tf_op jit(solution)/shard_map/ppermute | solution.py:435
  481.3 7.9 %collective-permute-start.23 = (bf16[16,24,1536]{2,1,0:T(8,128)(2,1)S(1)}, bf16[16,24,1536]{2,1,0:T(8,128)(2,1)S(1)}, u32[]{:S(2)}, u32[]{:S(2)}) collective-permute-start(bf16[16,24,1536]{2,1,0:T(8,128)(2,1)S(1)} %pad_maximum_fusion.1), channel_id=1, source_target_pairs={{0,2},{2,0},{4,6},{6,4},{8,10},{10,8},{12,14},{14,12},{16,18},{18,... | collective-permute-start | bytes 3538952 | tf_op jit(solution)/shard_map/ppermute | solution.py:435
  481.5 5.0 %collective-permute-start.28 = (f32[84,128]{1,0:T(8,128)S(1)}, f32[84,128]{1,0:T(8,128)S(1)}, u32[]{:S(2)}, u32[]{:S(2)}) collective-permute-start(f32[84,128]{1,0:T(8,128)S(1)} %add.282), channel_id=1, source_target_pairs={{0,16},{2,18},{4,20},{6,22},{8,24},{10,26},{12,28},{14,30},{16,0},... | collective-permute-start | bytes 129032 | tf_op jit(solution)/shard_map/ppermute | solution.py:435
  (61 other events, 614.3 us)
Sparse Core Ops, SparseCore 0:
  238.2 117.3 all-reduce.3

commit v3 on v2

v3 whole, which is shorter than its diff:
```python
import functools
import math

import jax
import jax.numpy as jnp
from jax import lax
from jax.experimental import pallas as pl
from jax.experimental.pallas import tpu as pltpu
from jax.sharding import PartitionSpec as P

HD = 64
LANES = 128
WIN = 64
LOG2E = math.log2(math.e)
LN2 = math.log(2.0)
NEG = -1e30
QB = 512
KB = 512
ROWS = 512
VT = 80
NT = (((1,), (1,)), ((), ()))
NN = (((1,), (0,)), ((), ()))
TN = (((0,), (0,)), ((), ()))
F32 = jnp.float32
BF16 = jnp.bfloat16
MIB = 1024 * 1024


def dot(a, b, dims=NN):
    return lax.dot_general(a, b, dims, preferred_element_type=F32)


def split3(x):
    hi = x.astype(BF16).astype(F32)
    rest = x - hi
    mid = rest.astype(BF16).astype(F32)
    low = (rest - mid).astype(BF16).astype(F32)
    return hi, mid, low


def lane_ids(rows):
    return lax.broadcasted_iota(jnp.int32, (rows, LANES), 1)


def put3(base, lanes, first, parts):
    out = base
    for n, part in enumerate(parts):
        out = jnp.where(lanes == first + n, part, out)
    return out


def whole_block(array):
    return pl.BlockSpec(
        array.shape, lambda *_: (0,) * array.ndim, pipeline_mode=pl.Buffered(1)
    )


def scorer_rows(key_scorer):
    return jnp.pad(key_scorer.reshape(-1, HD), ((0, 0), (0, LANES - HD)))


def bits_kernel(low_ref, flag_ref, bits_ref):
    width = bits_ref.shape[1]
    first = pl.program_id(0) * width
    lane = lax.broadcasted_iota(jnp.int32, (LANES, width), 0)
    pos = lax.broadcasted_iota(jnp.int32, (LANES, width), 1) + first
    back = (pos - lane) & (LANES - 1)
    at = pos - back
    bits = jnp.where((back < WIN) & (at >= 0), 1 << (jnp.maximum(at, 0) >> 7), 0)
    for slot in range(low_ref.shape[0]):
        hit = low_ref[slot : slot + 1, :] == lane
        bits = bits | jnp.where(hit, flag_ref[slot : slot + 1, :], 0)
    bits_ref[...] = bits


def allowed_bits(key_index, key_count):
    seq = key_index.shape[0]
    index = key_index.T
    slots = index.shape[0]
    slot = lax.broadcasted_iota(jnp.int32, index.shape, 0)
    used = (slot < key_count[None, :]) & (index >= 0)
    low = index & (LANES - 1)
    flag = jnp.where(used, 1 << (jnp.maximum(index, 0) >> 7), 0)
    width = 256
    spec = pl.BlockSpec((slots, width), lambda i: (0, i))
    return pl.pallas_call(
        bits_kernel,
        grid=(seq // width,),
        in_specs=[spec, spec],
        out_specs=pl.BlockSpec((LANES, width), lambda i: (0, i)),
        out_shape=jax.ShapeDtypeStruct((LANES, seq), jnp.int32),
        cost_estimate=pl.CostEstimate(
            flops=3 * slots * LANES * seq, bytes_accessed=8 * slots * seq, transcendentals=0
        ),
        name="allowed_bits",
    )(low, flag)


def fill_bias(bias_ref, bits_ref, q0, k0):
    depth, width = bias_ref.shape
    bits = bits_ref[:, pl.ds(q0, width)]
    for part in range(depth // LANES):
        shift = k0 // LANES + part
        seen = ((bits >> shift) & 1) == 1
        bias_ref[part * LANES : (part + 1) * LANES, :] = jnp.where(seen, 0.0, NEG)


def qkv_kernel(
    norm_ref, weight_ref, bias_ref, scorer_ref, qa_ref, ka_ref, va_ref, vt_ref, kt_ref
):
    rows = norm_ref.shape[0]
    heads = qa_ref.shape[0]
    lanes = lane_ids(rows)
    real = lanes < HD
    ones = jnp.where((lanes >= HD) & (lanes < HD + 3), 1.0, 0.0)
    for pair in range(heads // 2):
        cols = slice(pair * 6 * HD, (pair + 1) * 6 * HD)
        raw = dot(norm_ref[...], weight_ref[:, cols]) + bias_ref[:, cols]
        raw = raw.astype(BF16).astype(F32)
        blocks = [raw[:, n * LANES : (n + 1) * LANES] for n in range(3)]
        turned = [pltpu.roll(block, HD, 1) for block in blocks]
        groups = (
            (blocks[0], turned[0], blocks[1]),
            (turned[1], blocks[2], turned[2]),
        )
        for side, (query, key, value) in enumerate(groups):
            head = pair * 2 + side
            raw_gate = jnp.sum(key * scorer_ref[head : head + 1, :], axis=1, keepdims=True)
            gate = jnp.minimum(raw_gate, 0.0) - jnp.log1p(jnp.exp(-jnp.abs(raw_gate)))
            key_plain = jnp.where(real, key, 0.0)
            value_ones = jnp.where(real, value, ones)
            qa_ref[head] = jnp.where(real, query * 0.125, ones).astype(BF16)
            ka_ref[head] = put3(key_plain, lanes, HD, split3(gate)).astype(BF16)
            va_ref[head] = value_ones.astype(BF16)
            vt_ref[head] = value_ones.T[:VT, :].astype(BF16)
            kt_ref[head] = key_plain.T[:HD, :].astype(BF16)


def qkv_heads(norm_rows, weight, bias, scorer):
    rows, width = norm_rows.shape
    heads = scorer.shape[0]
    cols = weight.shape[1]
    row_shape = jax.ShapeDtypeStruct((heads, rows, LANES), BF16)
    row_block = pl.BlockSpec((heads, ROWS, LANES), lambda i: (0, i, 0))
    bias = bias.reshape(1, cols)
    return pl.pallas_call(
        qkv_kernel,
        grid=(rows // ROWS,),
        in_specs=[
            pl.BlockSpec((ROWS, width), lambda i: (i, 0)),
            whole_block(weight),
            whole_block(bias),
            whole_block(scorer),
        ],
        out_specs=[
            row_block,
            row_block,
            row_block,
            pl.BlockSpec((heads, VT, ROWS), lambda i: (0, 0, i)),
            pl.BlockSpec((heads, HD, ROWS), lambda i: (0, 0, i)),
        ],
        out_shape=[
            row_shape,
            row_shape,
            row_shape,
            jax.ShapeDtypeStruct((heads, VT, rows), BF16),
            jax.ShapeDtypeStruct((heads, HD, rows), BF16),
        ],
        compiler_params=pltpu.CompilerParams(vmem_limit_bytes=20 * MIB),
        cost_estimate=pl.CostEstimate(
            flops=4 * rows * width * cols, bytes_accessed=10 * MIB, transcendentals=0
        ),
        name="qkv_heads",
    )(norm_rows, weight, bias, scorer)


def attend_block(
    place, q_block, k0, qa_ref, ka_ref, vt_ref, bits_ref, bias_ref, total_ref, peak_ref, corner
):
    heads = qa_ref.shape[0]
    depth, first = corner
    queries = slice(first, QB)
    bias = bias_ref.at[0:depth, queries]
    keys = pl.ds(k0, depth)
    fill_bias(bias, bits_ref, q_block * QB + first, place * KB + k0)

    def scores_of(head):
        return dot(ka_ref[head, keys, :], qa_ref[head, queries, :], NT)

    ahead = scores_of(0)
    for head in range(heads):
        scores = ahead
        if head + 1 < heads:
            ahead = scores_of(head + 1)
        scores = scores * LOG2E + bias[...]
        old = peak_ref[head, :, queries]
        new = jnp.maximum(old, jnp.max(scores, axis=0, keepdims=True))
        weights = jnp.exp2(scores - new[0:1])
        shrink = jnp.exp2(old - new)
        peak_ref[head, :, queries] = new
        part = dot(vt_ref[head, :, keys], weights.astype(BF16))
        total_ref[head, :, queries] = total_ref[head, :, queries] * shrink[0:1] + part


def attend_blocks(count, place, q_block, *refs):
    def step(j, carry):
        k0 = pl.multiple_of(j * KB, KB)
        attend_block(place, q_block, k0, *refs, (KB, 0))
        return carry

    lax.fori_loop(0, count, step, 0)


def attend_diagonal(n, place, q_block, *refs):
    half = KB // 2
    k0 = pl.multiple_of(n * KB, KB)
    attend_block(place, q_block, k0, *refs, (half, 0))
    attend_block(place, q_block, pl.multiple_of(k0 + half, half), *refs, (half, half))


def attend_open(total_ref, peak_ref):
    total_ref[...] = jnp.zeros_like(total_ref)
    peak_ref[...] = jnp.full_like(peak_ref, NEG)


def attend_end(total_ref, peak_ref, out_ref, log_ref):
    heads = total_ref.shape[0]
    for pair in range(heads // 2):
        sides = []
        for head in (2 * pair, 2 * pair + 1):
            mass = total_ref[head, HD : HD + 1, :]
            sides.append(total_ref[head, 0:HD, :] / mass)
            log_ref[head] = peak_ref[head] + jnp.log(mass) * LOG2E
        both = jnp.concatenate(sides, axis=0).T
        out_ref[:, pair * LANES : (pair + 1) * LANES] = both.astype(BF16)


def attend_start_kernel(
    places_ref, qa_ref, ka_ref, vt_ref, bits_ref, total_ref, peak_ref, bias_ref
):
    own = places_ref[0]
    n = pl.program_id(0)
    refs = (qa_ref, ka_ref, vt_ref, bits_ref, bias_ref, total_ref, peak_ref)
    attend_open(total_ref, peak_ref)
    attend_blocks(n, own, own + n, *refs)
    attend_diagonal(n, own, own + n, *refs)


def attend_finish_kernel(
    n,
    places_ref,
    qa_ref,
    ka_ref,
    vt_ref,
    bits_ref,
    total_in_ref,
    peak_in_ref,
    out_ref,
    log_ref,
    bias_ref,
    total_ref,
    peak_ref,
):
    own, peer, later = places_ref[0], places_ref[1], places_ref[2]
    refs = (qa_ref, ka_ref, vt_ref, bits_ref, bias_ref, total_ref, peak_ref)
    total_ref[...] = total_in_ref[...]
    peak_ref[...] = peak_in_ref[...]
    attend_blocks(later * (ka_ref.shape[1] // KB), peer, own + n, *refs)
    attend_end(total_ref, peak_ref, out_ref, log_ref)


def attend_other_kernel(
    n,
    places_ref,
    qa_ref,
    ka_ref,
    vt_ref,
    ka_own_ref,
    vt_own_ref,
    bits_ref,
    out_ref,
    log_ref,
    bias_ref,
    total_ref,
    peak_ref,
):
    own, peer, later = places_ref[0], places_ref[1], places_ref[2]
    block = peer + n
    tail = (bits_ref, bias_ref, total_ref, peak_ref)
    attend_open(total_ref, peak_ref)
    for at in range(n):
        attend_block(peer, block, at * KB, qa_ref, ka_ref, vt_ref, *tail, (KB, 0))
    attend_diagonal(n, peer, block, qa_ref, ka_ref, vt_ref, *tail)
    earlier = (1 - later) * (ka_own_ref.shape[1] // KB)
    attend_blocks(earlier, own, block, qa_ref, ka_own_ref, vt_own_ref, *tail)
    attend_end(total_ref, peak_ref, out_ref, log_ref)


def attend_call(kernel, name, places, qa, others, count, first, state=(), keep=False):
    heads = qa.shape[0]
    total_spec = pl.BlockSpec((heads, VT, QB), lambda i, _: (0, 0, first + i))
    peak_spec = pl.BlockSpec((heads, 8, QB), lambda i, _: (0, 0, first + i))
    log_spec = pl.BlockSpec((heads, 8, QB), lambda i, _: (0, 0, i))
    total_shape = jax.ShapeDtypeStruct((heads, VT, count * QB), F32)
    peak_shape = jax.ShapeDtypeStruct((heads, 8, count * QB), F32)
    scratch = [
        pltpu.VMEM((KB, QB), F32),
        pltpu.VMEM((heads, VT, QB), F32),
        pltpu.VMEM((heads, 8, QB), F32),
    ]
    if keep:
        out_specs, out_shape = [total_spec, peak_spec], [total_shape, peak_shape]
        scratch = scratch[:1]
    else:
        out_specs = [pl.BlockSpec((QB, heads * HD), lambda i, _: (i, 0)), log_spec]
        out_shape = [jax.ShapeDtypeStruct((count * QB, heads * HD), BF16), peak_shape]
    return pl.pallas_call(
        kernel,
        grid_spec=pltpu.PrefetchScalarGridSpec(
            num_scalar_prefetch=1,
            grid=(count,),
            in_specs=[pl.BlockSpec((heads, QB, LANES), lambda i, _: (0, first + i, 0))]
            + [whole_block(array) for array in others]
            + ([total_spec, peak_spec] if state else []),
            out_specs=out_specs,
            scratch_shapes=scratch,
        ),
        out_shape=out_shape,
        compiler_params=pltpu.CompilerParams(vmem_limit_bytes=24 * MIB),
        cost_estimate=pl.CostEstimate(
            flops=2 * count * heads * QB * KB * 2048, bytes_accessed=8 * MIB, transcendentals=0
        ),
        name=name,
    )(places, qa, *others, *state)


def in_vmem():
    return pl.BlockSpec(memory_space=pltpu.VMEM)


def attend_back_kernel(
    own_queries,
    places_ref,
    qa_ref,
    ka_refs,
    kt_refs,
    va_refs,
    grad_refs,
    att_refs,
    log_refs,
    bits_ref,
    dq_ref,
    dk_refs,
    dv_refs,
    bias_ref,
    ga_ref,
):
    heads, rows, _ = qa_ref.shape
    blocks = rows // QB
    lanes = lane_ids(ROWS)
    dq_ref[...] = jnp.zeros_like(dq_ref)
    if own_queries:
        for ref in tuple(dk_refs) + tuple(dv_refs):
            ref[...] = jnp.zeros_like(ref)

    for n in range(len(grad_refs)):
        rows_n = slice(n * ROWS, (n + 1) * ROWS)
        for pair in range(heads // 2):
            cols = slice(pair * LANES, (pair + 1) * LANES)
            grad = grad_refs[n][:, cols].astype(F32)
            prod = grad * att_refs[n][:, cols].astype(F32)
            turned = pltpu.roll(grad, HD, 1)
            for side, values in enumerate((grad, turned)):
                mine = (lanes < HD) if side == 0 else (lanes >= HD)
                inner = jnp.sum(jnp.where(mine, prod, 0.0), axis=1, keepdims=True)
                plain = jnp.where(lanes < HD, values, 0.0)
                filled = put3(plain, lanes, HD, split3(-inner))
                ga_ref[pair * 2 + side, rows_n, :] = filled.astype(BF16)

    q_place, k_places = places_ref[0], (places_ref[0], places_ref[1])
    later = places_ref[2]
    if not own_queries:
        q_place, k_places = k_places[1], (k_places[1], k_places[0])
        later = 1 - later

    def tile(piece, j, n, i, corner):
        depth, first = corner
        width = QB - first
        k1 = pl.multiple_of(j * KB + first, KB // 2)
        q1 = pl.multiple_of(i * QB + first, QB // 2)
        keys = pl.ds(k1, depth)
        queries = pl.ds(q1, width)
        bias = bias_ref.at[0:depth, 0:width]
        fill_bias(bias, bits_ref, q_place * QB + q1, k_places[piece] * KB + k1)
        ka_ref, kt_ref, va_ref = ka_refs[piece], kt_refs[piece], va_refs[piece]
        dk_ref, dv_ref = dk_refs[piece], dv_refs[piece]

        def first_of(head):
            qa = qa_ref[head, queries, :]
            ga = ga_ref[head, queries, :]
            return (
                qa,
                ga,
                dot(ka_ref[head, keys, :], qa, NT),
                dot(va_ref[head, keys, :], ga, NT),
            )

        ahead = first_of(0)
        for head in range(heads):
            qa, ga, scores, inner = ahead
            if head + 1 < heads:
                ahead = first_of(head + 1)
            scores = scores * LOG2E + bias[...]
            if isinstance(n, int):
                logs = log_refs[n][head, 0:1, first:QB]
            else:
                logs = jnp.where(n == 0, log_refs[0][head, 0:1, :], log_refs[1][head, 0:1, :])
            probs = jnp.exp2(scores - logs)
            slopes = (probs * inner).astype(BF16)
            dv_ref[head, keys, :] += dot(probs.astype(BF16), ga)
            dk_ref[head, keys, :] += dot(slopes, qa)
            dq_ref[head, :, queries] += dot(kt_ref[head, :, keys], slopes)

    half = KB // 2
    for n in range(blocks):
        tile(0, n, n, n, (half, 0))
        tile(0, n, n, n, (half, half))
        for j in range(n):
            tile(0, j, n, n, (KB, 0))

    def step(at, carry):
        i = at & (blocks - 1)
        tile(1, at // blocks, i, i, (KB, 0))
        return carry

    lax.fori_loop(0, later * (blocks * blocks), step, 0)


def attend_back(own_queries, places, qa, keys, grads, atts, logs, bits, sums=None):
    heads, rows, _ = qa.shape
    count = len(grads)
    inputs = [places, qa]
    for kind in range(3):
        inputs += [keys[0][kind], keys[1][kind]]
    inputs += list(grads) + list(atts) + list(logs) + [bits]
    given = len(inputs)
    aliases = {}
    if sums is not None:
        aliases = {given + n: 1 + n for n in range(4)}
        inputs += list(sums)
    big = jax.ShapeDtypeStruct((heads, rows, LANES), F32)

    def kernel(*refs):
        places_ref, qa_ref = refs[:2]
        pairs = [refs[2 + 2 * n : 4 + 2 * n] for n in range(3)]
        lists = [refs[8 + n * count : 8 + (n + 1) * count] for n in range(3)]
        bits_ref = refs[8 + 3 * count]
        dq_ref, dk0, dk1, dv0, dv1, bias_ref, ga_ref = refs[len(inputs) :]
        attend_back_kernel(
            own_queries,
            places_ref,
            qa_ref,
            *pairs,
            *lists,
            bits_ref,
            dq_ref,
            (dk0, dk1),
            (dv0, dv1),
            bias_ref,
            ga_ref,
        )

    return pl.pallas_call(
        kernel,
        in_specs=[pl.BlockSpec(memory_space=pltpu.SMEM)] + [in_vmem()] * (len(inputs) - 1),
        out_specs=[in_vmem()] * 5,
        out_shape=[jax.ShapeDtypeStruct((heads, HD, rows), F32)] + [big] * 4,
        scratch_shapes=[pltpu.VMEM((KB, QB), F32), pltpu.VMEM((heads, rows, LANES), BF16)],
        input_output_aliases=aliases,
        compiler_params=pltpu.CompilerParams(vmem_limit_bytes=16 * MIB),
        cost_estimate=pl.CostEstimate(flops=1000000, bytes_accessed=MIB, transcendentals=0),
        name="attend_back",
    )(*inputs)


def join_kernel(
    dq_own_ref,
    dq_peer_ref,
    dk_own_ref,
    dk_peer_ref,
    dv_own_ref,
    dv_peer_ref,
    ka_own_ref,
    ka_peer_ref,
    norm_own_ref,
    norm_peer_ref,
    weight_ref,
    scorer_ref,
    one_own_ref,
    one_peer_ref,
    joined_ref,
    bias_out_ref,
    scorer_out_ref,
    plain_ref,
    times_ref,
):
    heads, rows, _ = dk_own_ref.shape
    span = 256
    lanes = lane_ids(span)
    real = lanes < HD
    for ref in (bias_out_ref, scorer_out_ref, plain_ref, times_ref):
        ref[...] = jnp.zeros_like(ref)

    def piece(first, dq_ref, dk_ref, dv_ref, ka_ref, norm_ref, one_ref):
        def step(at, carry):
            here = pl.ds(pl.multiple_of(at * span, span), span)
            there = pl.ds(pl.multiple_of(at * span + first, span), span)
            for pair in range(heads // 2):
                dq = dq_ref[2 * pair : 2 * pair + 2, :, here].reshape(LANES, span).T * 0.125
                dks, dvs = [], []
                for head in (2 * pair, 2 * pair + 1):
                    scorer = scorer_ref[head : head + 1, :]
                    key = ka_ref[head, here, :].astype(F32)
                    dk = dk_ref[head, here, :]
                    raw_gate = jnp.sum(key * scorer, axis=1, keepdims=True)
                    slope = dk[:, HD : HD + 1] / (1.0 + jnp.exp(raw_gate))
                    scorer_out_ref[head : head + 1, :] += sum_rows(slope * key)
                    dks.append(dk + slope * scorer)
                    dvs.append(dv_ref[head, here, :])
                blocks = (
                    jnp.where(real, dq, pltpu.roll(dks[0], HD, 1)),
                    jnp.where(real, dvs[0], dq),
                    jnp.where(real, dks[1], pltpu.roll(dvs[1], HD, 1)),
                )
                for n, block in enumerate(blocks):
                    cols = slice((pair * 3 + n) * LANES, (pair * 3 + n + 1) * LANES)
                    bias_out_ref[:, cols] += sum_rows(block)
                    joined_ref[there, cols] = block.astype(BF16)
            back = dot(joined_ref[there, :], weight_ref[...], NT)
            one_ref[here, :] = back.astype(one_ref.dtype)
            plain_ref[...] += sum_rows(back)
            times_ref[...] += sum_rows(back * norm_ref[here, :].astype(F32))
            return carry

        lax.fori_loop(0, rows // span, step, 0)

    piece(rows, dq_peer_ref, dk_peer_ref, dv_peer_ref, ka_peer_ref, norm_peer_ref, one_peer_ref)
    piece(0, dq_own_ref, dk_own_ref, dv_own_ref, ka_own_ref, norm_own_ref, one_own_ref)


def join(dqs, dks, dvs, kas, norms, weight, scorer):
    heads = dks[0].shape[0]
    rows, width = norms[0].shape
    cols = weight.shape[1]
    inputs = (*dqs, *dks, *dvs, *kas, *norms, weight, scorer)
    vector = jax.ShapeDtypeStruct((1, width), F32)
    return pl.pallas_call(
        join_kernel,
        in_specs=[in_vmem()] * len(inputs),
        out_specs=[in_vmem()] * 7,
        out_shape=[
            jax.ShapeDtypeStruct((rows, width), F32),
            jax.ShapeDtypeStruct((rows, width), BF16),
            jax.ShapeDtypeStruct((2 * rows, cols), BF16),
            jax.ShapeDtypeStruct((1, cols), F32),
            jax.ShapeDtypeStruct((heads, LANES), F32),
            vector,
            vector,
        ],
        compiler_params=pltpu.CompilerParams(vmem_limit_bytes=20 * MIB),
        cost_estimate=pl.CostEstimate(flops=1000000, bytes_accessed=MIB, transcendentals=0),
        name="join",
    )(*inputs)


SPAN = 256


def normalize(values):
    center = values - jnp.mean(values, axis=-1, keepdims=True)
    scale = lax.rsqrt(jnp.mean(center * center, axis=-1, keepdims=True) + 1e-05)
    return center * scale, scale


def norm_back(slope, hat, scale):
    means = jnp.mean(slope, axis=-1, keepdims=True)
    inner = jnp.mean(slope * hat, axis=-1, keepdims=True)
    return (slope - means - hat * inner) * scale


def row_spec(width, span=SPAN, skip=0):
    return pl.BlockSpec((span, width), lambda i, *_: (i + skip, 0))


def sum_rows(values):
    return jnp.sum(values, axis=0, keepdims=True)


def start_at_zero(*refs):
    @pl.when(pl.program_id(0) == 0)
    def _():
        for ref in refs:
            ref[...] = jnp.zeros_like(ref)


def rows_call(
    kernel, name, rows, inputs, in_specs, outs, flops, span=SPAN, scalars=(), earlier=()
):
    aliases = {}
    body = kernel
    if earlier:
        first = len(scalars) + len(inputs)
        aliases = {first + n: at for n, (at, _) in enumerate(earlier)}
        skip_from, skip_count = first, len(earlier)
        inputs = tuple(inputs) + tuple(array for _, array in earlier)
        in_specs = list(in_specs) + [pl.BlockSpec(memory_space=pl.ANY)] * len(earlier)

        def body(*refs):
            kernel(*refs[:skip_from], *refs[skip_from + skip_count :])

    return pl.pallas_call(
        body,
        grid_spec=pltpu.PrefetchScalarGridSpec(
            num_scalar_prefetch=len(scalars),
            grid=(rows // span,),
            in_specs=in_specs,
            out_specs=[
                pl.BlockSpec((1, width), lambda i, *_: (0, 0))
                if one
                else row_spec(width, span, start // span)
                for one, width, _, _, start in outs
            ],
        ),
        out_shape=[
            jax.ShapeDtypeStruct((1 if one else total, width), kind)
            for one, width, kind, total, _ in outs
        ],
        input_output_aliases=aliases,
        compiler_params=pltpu.CompilerParams(vmem_limit_bytes=24 * MIB),
        cost_estimate=pl.CostEstimate(
            flops=flops, bytes_accessed=8 * rows * 768, transcendentals=0
        ),
        name=name,
    )(*scalars, *inputs)


def norm_one_kernel(in_ref, grad_ref, gain_ref, shift_ref, out_ref, low_ref):
    hat, _ = normalize(in_ref[...])
    out_ref[...] = (hat * gain_ref[...] + shift_ref[...]).astype(BF16)
    low_ref[...] = grad_ref[...].astype(BF16)


def norm_one(layer_in, out_grad, gain, shift):
    rows, width = layer_in.shape
    vector = pl.BlockSpec((1, width), lambda i: (0, 0))
    return rows_call(
        norm_one_kernel,
        "norm_one",
        rows,
        (layer_in, out_grad, gain.reshape(1, width), shift.reshape(1, width)),
        [row_spec(width), row_spec(width), vector, vector],
        [(False, width, BF16, rows, 0), (False, width, BF16, rows, 0)],
        rows * width * 8,
    )


def mix_kernel(
    in_ref, own_ref, peer_ref, w_own_ref, w_peer_ref, bias_ref, gain_ref, shift_ref, mixed_ref, norm_ref
):
    part = dot(own_ref[...], w_own_ref[...]) + dot(peer_ref[...], w_peer_ref[...])
    mixed = in_ref[...] + part + bias_ref[...]
    mixed_ref[...] = mixed
    hat, _ = normalize(mixed)
    norm_ref[...] = (hat * gain_ref[...] + shift_ref[...]).astype(BF16)


def mix(layer_in, own, peer, w_own, w_peer, bias, gain, shift, start, earlier):
    total, width = layer_in.shape
    rows, depth = peer.shape
    skip = start // SPAN
    vector = pl.BlockSpec((1, width), lambda i: (0, 0))
    return rows_call(
        mix_kernel,
        "mix",
        rows,
        (layer_in, own, peer, w_own, w_peer)
        + tuple(v.reshape(1, width) for v in (bias, gain, shift)),
        [
            row_spec(width, skip=skip),
            row_spec(depth),
            row_spec(depth),
            whole_block(w_own),
            whole_block(w_peer),
        ]
        + [vector] * 3,
        [(False, width, F32, total, start), (False, width, BF16, rows, 0)],
        rows * width * depth * 4,
        earlier=earlier,
    )


def feed_kernel(
    norm_ref, grad_ref, fc_ref, bias_ref, proj_ref, active_ref, slope_ref, back_ref, sum_ref
):
    start_at_zero(sum_ref)
    units = fc_ref.shape[1]
    step = 512
    total = None
    for at in range(0, units, step):
        cols = slice(at, at + step)
        hidden = dot(norm_ref[...], fc_ref[:, cols]) + bias_ref[:, cols]
        grad = dot(grad_ref[...], proj_ref[cols, :], NT)
        square = hidden * hidden
        bend = jnp.tanh(hidden * (0.7978845608 + 0.7978845608 * 0.044715 * square))
        half = 0.5 + 0.5 * bend
        active_ref[:, cols] = (hidden * half).astype(BF16)
        inner = 0.7978845608 + 3.0 * 0.7978845608 * 0.044715 * square
        slope = grad * (half + 0.5 * hidden * (1.0 - bend * bend) * inner)
        low = slope.astype(BF16)
        slope_ref[:, cols] = low
        sum_ref[:, cols] += sum_rows(slope)
        part = dot(low, fc_ref[:, cols], NT)
        total = part if total is None else total + part
    back_ref[...] = total.astype(back_ref.dtype)


def feed(norm_rows, grad_rows, grad_start, fc, bias, proj, back_kind, start, total, earlier):
    rows, width = norm_rows.shape
    units = fc.shape[1]
    bias = bias.reshape(1, units)
    return rows_call(
        feed_kernel,
        "feed",
        rows,
        (norm_rows, grad_rows, fc, bias, proj),
        [
            row_spec(width),
            row_spec(width, skip=grad_start // SPAN),
            whole_block(fc),
            whole_block(bias),
            whole_block(proj),
        ],
        [
            (False, units, BF16, total, start),
            (False, units, BF16, total, start),
            (False, width, back_kind, rows, 0),
            (True, units, F32, 1, 0),
        ],
        rows * width * units * 6,
        earlier=earlier,
    )


def mix_back_kernel(
    mixed_ref,
    own_ref,
    other_ref,
    grad_ref,
    gain_ref,
    w_own_ref,
    w_peer_ref,
    out_ref,
    low_ref,
    att_own_ref,
    att_peer_ref,
    gain_out_ref,
    shift_out_ref,
    mixed_out_ref,
    grad_out_ref,
):
    start_at_zero(gain_out_ref, shift_out_ref, mixed_out_ref, grad_out_ref)
    hat, scale = normalize(mixed_ref[...])
    slope = own_ref[...] + other_ref[...].astype(F32)
    gain_out_ref[...] += sum_rows(slope * hat)
    shift_out_ref[...] += sum_rows(slope)
    grad = grad_ref[...]
    grad_out_ref[...] += sum_rows(grad)
    out = grad + norm_back(slope * gain_ref[...], hat, scale)
    mixed_out_ref[...] += sum_rows(out)
    out_ref[...] = out
    low = out.astype(BF16)
    low_ref[...] = low
    att_own_ref[...] = dot(low, w_own_ref[...], NT).astype(BF16)
    att_peer_ref[...] = dot(low, w_peer_ref[...], NT).astype(BF16)


def mix_back(mixed, own, other, grad, gain, w_own, w_peer, start, earlier):
    total, width = mixed.shape
    rows = other.shape[0]
    depth = w_own.shape[0]
    gain = gain.reshape(1, width)
    wide = row_spec(width)
    later = row_spec(width, skip=start // SPAN)
    return rows_call(
        mix_back_kernel,
        "mix_back",
        rows,
        (mixed, own, other, grad, gain, w_own, w_peer),
        [later, wide, wide, later, whole_block(gain), whole_block(w_own), whole_block(w_peer)],
        [
            (False, width, F32, total, start),
            (False, width, BF16, total, start),
            (False, depth, BF16, rows, 0),
            (False, depth, BF16, rows, 0),
            (True, width, F32, 1, 0),
            (True, width, F32, 1, 0),
            (True, width, F32, 1, 0),
            (True, width, F32, 1, 0),
        ],
        rows * width * depth * 4,
        earlier=earlier,
    )


def norm_one_back_kernel(in_ref, own_ref, other_ref, grad_ref, gain_ref, out_ref):
    hat, scale = normalize(in_ref[...])
    slope = (own_ref[...] + other_ref[...].astype(F32)) * gain_ref[...]
    out_ref[...] = grad_ref[...] + norm_back(slope, hat, scale)


def norm_one_back(layer_in, own, other, grad, gain, start, earlier):
    total, width = layer_in.shape
    rows = other.shape[0]
    gain = gain.reshape(1, width)
    later = row_spec(width, skip=start // SPAN)
    (out,) = rows_call(
        norm_one_back_kernel,
        "norm_one_back",
        rows,
        (layer_in, own, other, grad, gain),
        [later, later, row_spec(width), later, whole_block(gain)],
        [(False, width, F32, total, start)],
        rows * width * 20,
        earlier=earlier,
    )
    return out


def flip_bit(values, bit):
    total = lax.axis_size("dp")
    return lax.ppermute(values, "dp", [(n, n ^ (1 << bit)) for n in range(total)])


def flip_core(values):
    return flip_bit(values, 0)


def flip_tensor(values):
    return lax.ppermute(values, "tensor", [(0, 1), (1, 0)])


def rows_at(values, start, count):
    return lax.dynamic_slice_in_dim(values, start, count, 0)


def my_bit(bit):
    return (lax.axis_index("dp") >> bit) & 1


def add_low(one, two):
    return (one.astype(F32) + two.astype(F32)).astype(BF16)


def halve(values, bit):
    half = values.shape[0] // 2
    mine = my_bit(bit)
    return add_low(
        rows_at(values, mine * half, half),
        flip_bit(rows_at(values, (1 - mine) * half, half), bit),
    )


def both_sides(own, other, mine):
    return jnp.where(
        mine == 0,
        jnp.concatenate([own, other], axis=0),
        jnp.concatenate([other, own], axis=0),
    )


def double(values, bit):
    return both_sides(values, flip_bit(values, bit), my_bit(bit))


def ladder_orders():
    rest = list(range(1, lax.axis_size("dp").bit_length() - 1))
    return rest, rest[1:] + rest[:1]


def scatter_over_dp(values, beside):
    orders = ladder_orders()
    rows, cols = values.shape
    pieces = 2 * lax.axis_size("dp")
    mine = halve(values.reshape(pieces, rows // pieces, cols), 0)
    half = pieces // 4
    parts = [mine[:half], mine[half:]]
    for n in range(len(orders[0])):
        parts = [halve(part, order[n]) for part, order in zip(parts, orders)]
        if n == 0:
            parts, beside = lax.optimization_barrier((parts, beside))
    return parts, beside


def gather_over_dp(parts):
    orders = ladder_orders()
    for n in reversed(range(len(orders[0]))):
        parts = [double(part, order[n]) for part, order in zip(parts, orders)]
    whole = double(jnp.concatenate(parts, axis=0), 0)
    return whole.reshape(-1, whole.shape[-1])


def sum_over_all(values):
    values = values + flip_tensor(values)
    for bit in range(lax.axis_size("dp").bit_length() - 1):
        values = values + flip_bit(values, bit)
    return values


def in_half(vector, side):
    out = jnp.zeros((2 * vector.shape[0],), vector.dtype)
    return lax.dynamic_update_slice_in_dim(out, vector, side * vector.shape[0], 0)


def shards(
    layer_in,
    qkv_weight,
    qkv_bias,
    key_scorer,
    out_weight,
    out_bias,
    fc_weight,
    fc_bias,
    proj_weight,
    proj_bias,
    norm1_gain,
    norm1_shift,
    norm2_gain,
    norm2_shift,
    key_index,
    key_count,
    out_grad,
):
    side = lax.axis_index("tensor")
    own_rows = layer_in.shape[0]
    seq = key_index.shape[0]
    half = own_rows // 2
    blocks = own_rows // QB
    places = jnp.stack([side * blocks, (1 - side) * blocks, side]).astype(jnp.int32)

    starts = (0, half)
    norm_own, grad_low = norm_one(layer_in, out_grad, norm1_gain, norm1_shift)
    norm_peer = flip_tensor(norm_own)
    bits = allowed_bits(key_index, key_count)
    scorer = scorer_rows(key_scorer)
    bits, out_later = lax.optimization_barrier((bits, out_weight))
    out_peer = flip_tensor(out_later)

    own = qkv_heads(norm_own, qkv_weight, qkv_bias, scorer)
    own, grad_first = lax.optimization_barrier((own, grad_low[:half]))
    grad_peers = [flip_tensor(grad_first)]
    qa_own, ka_own, va_own, vt_own, kt_own = own
    state = attend_call(
        attend_start_kernel, "attend_start", places, qa_own, (ka_own, vt_own, bits), blocks, 0, (), True
    )
    state, norm_peer = lax.optimization_barrier((state, norm_peer))
    peer = qkv_heads(norm_peer, qkv_weight, qkv_bias, scorer)
    peer, grad_second = lax.optimization_barrier((peer, grad_low[half:]))
    grad_peers.append(flip_tensor(grad_second))
    qa_peer, ka_peer, va_peer, vt_peer, kt_peer = peer
    att_owns, logs_owns, att_sends, logs_sends, att_peers = [], [], [], [], []
    for n in range(blocks):
        att_send, logs_send = attend_call(
            functools.partial(attend_other_kernel, n),
            "attend_other",
            places,
            qa_peer,
            (ka_peer, vt_peer, ka_own, vt_own, bits),
            1,
            n,
        )
        att_own, logs_own = attend_call(
            functools.partial(attend_finish_kernel, n),
            "attend_finish",
            places,
            qa_own,
            (ka_peer, vt_peer, bits),
            1,
            n,
            state,
        )
        att_send, att_own, qa_peer, qa_own = lax.optimization_barrier(
            (att_send, att_own, qa_peer, qa_own)
        )
        if n == 0:
            att_send, grad_peers[0] = lax.optimization_barrier((att_send, grad_peers[0]))
        att_owns.append(att_own)
        logs_owns.append(logs_own)
        att_sends.append(att_send)
        logs_sends.append(logs_send)
        att_peers.append(flip_tensor(att_send))

    mixed = None
    normed, normed_peers = [], []
    for n, at in enumerate(starts):
        mixed, low = mix(
            layer_in,
            att_owns[n],
            att_peers[n],
            out_weight,
            out_peer,
            out_bias,
            norm2_gain,
            norm2_shift,
            at,
            () if mixed is None else ((0, mixed),),
        )
        normed.append(low)
        normed_peers.append(flip_tensor(low))
    active = slopes = None
    backs, back_others, fc_sums = [], [], []
    for n, rows in enumerate(normed + normed_peers):
        active, slopes, back, fc_sum = feed(
            rows,
            grad_low if n < 2 else grad_peers[n - 2],
            n * half if n < 2 else 0,
            fc_weight,
            fc_bias,
            proj_weight,
            F32 if n < 2 else BF16,
            n * half,
            seq,
            () if active is None else ((0, active), (1, slopes)),
        )
        fc_sums.append(fc_sum)
        if n < 2:
            backs.append(back)
        else:
            back_others.append(flip_tensor(back))
    grad_fc_bias = sum(fc_sums[1:], fc_sums[0]).reshape(-1)
    grad_fc_weight = dot(jnp.concatenate(normed + normed_peers, axis=0), slopes, TN)
    grad_proj_weight = dot(active, jnp.concatenate([grad_low] + grad_peers, axis=0), TN)
    proj_own = dot(active[:own_rows], proj_weight).astype(BF16)
    proj_send = dot(active[own_rows:], proj_weight).astype(BF16)
    grad_fc_weight = grad_fc_weight.astype(BF16)
    grad_proj_weight = grad_proj_weight.astype(BF16)
    mixed, grad_fc_weight, grad_proj_weight = lax.optimization_barrier(
        (mixed, grad_fc_weight, grad_proj_weight)
    )
    grad_mixed = grad_mixed_low = None
    grad_att_owns, grad_att_peers, row_sums = [], [], []
    for n, at in enumerate(starts):
        grad_mixed, grad_mixed_low, grad_att_own, grad_att_send, *some = mix_back(
            mixed,
            backs[n],
            back_others[n],
            out_grad,
            norm2_gain,
            out_weight,
            out_peer,
            at,
            ()
            if grad_mixed is None
            else ((0, grad_mixed), (1, grad_mixed_low)),
        )
        row_sums.append(some)
        grad_att_owns.append(grad_att_own)
        grad_att_peers.append(flip_tensor(grad_att_send))
    grad_norm2_gain, grad_norm2_shift, grad_out_bias, grad_proj_bias = (
        one + two for one, two in zip(*row_sums)
    )

    out_send = dot(grad_mixed_low, jnp.concatenate(att_peers, axis=0), TN).astype(BF16)
    out_keep = dot(grad_mixed_low, jnp.concatenate(att_owns, axis=0), TN)
    grad_fc_weight, grad_proj_weight = lax.psum((grad_fc_weight, grad_proj_weight), "dp")
    own_keys, peer_keys = (ka_own, kt_own, va_own), (ka_peer, kt_peer, va_peer)
    _, proj_send, out_send = lax.optimization_barrier((grad_att_send, proj_send, out_send))
    proj_other = flip_tensor(proj_send)
    out_other = flip_tensor(out_send)
    norm_all = jnp.concatenate([norm_own, norm_peer], axis=0)
    qa_own, proj_send, proj_own, out_send, out_keep, norm_all = lax.optimization_barrier(
        (qa_own, proj_send, proj_own, out_send, out_keep, norm_all)
    )
    dq_own, *key_sums = attend_back(
        True, places, qa_own, (own_keys, peer_keys), grad_att_owns, att_owns, logs_owns, bits
    )
    swapped = (key_sums[1], key_sums[0], key_sums[3], key_sums[2])
    dq_peer, *key_sums = attend_back(
        False,
        places,
        qa_peer,
        (peer_keys, own_keys),
        grad_att_peers,
        att_sends,
        logs_sends,
        bits,
        swapped,
    )
    key_sums, proj_other, out_other = lax.optimization_barrier((key_sums, proj_other, out_other))
    dk_peer, dk_own, dv_peer, dv_own = key_sums
    one_own, one_send, joined, grad_qkv_bias, grad_key_scorer, plain_sum, times_sum = join(
        (dq_own, dq_peer),
        (dk_own, dk_peer),
        (dv_own, dv_peer),
        (ka_own, ka_peer),
        (norm_own, norm_peer),
        qkv_weight,
        scorer,
    )
    grad_key_scorer = grad_key_scorer[:, :HD].reshape(-1)
    grad_qkv_bias = grad_qkv_bias.reshape(-1)
    one_other = flip_tensor(one_send)
    grad_qkv_weight = dot(norm_all, joined, TN).astype(BF16)
    layer_out = mixed + (proj_own.astype(F32) + proj_other.astype(F32)) + proj_bias
    grad_out_turned = add_low(out_keep, out_other)
    scattered, (grad_fc_weight, grad_proj_weight) = scatter_over_dp(
        jnp.concatenate([grad_qkv_weight, grad_out_turned], axis=1),
        (grad_fc_weight, grad_proj_weight),
    )
    scattered, one_other = lax.optimization_barrier((scattered, one_other))
    last = gather_over_dp(scattered)
    joined_cols = qkv_weight.shape[1]
    grad_qkv_weight = last[:, :joined_cols]
    grad_out_weight = last[:, joined_cols:].T
    input_grad = norm_one_back(layer_in, one_own, one_other, grad_mixed, norm1_gain, 0, ())

    sums = [
        grad_out_bias,
        grad_proj_bias,
        times_sum,
        plain_sum,
        grad_norm2_gain,
        grad_norm2_shift,
        in_half(grad_qkv_bias, side),
        in_half(grad_key_scorer, side),
        in_half(grad_fc_bias, side),
    ]
    sums = [part.reshape(-1) for part in sums]
    packed = sum_over_all(jnp.concatenate(sums).reshape(-1, LANES)).reshape(-1)
    ends = []
    at = 0
    for part in sums:
        ends.append(packed[at : at + part.shape[0]])
        at += part.shape[0]
    grad_norm1_shift = ends[3]
    grad_norm1_gain = (ends[2] - norm1_shift * ends[3]) / norm1_gain

    def mine_of(vector):
        half = vector.shape[0] // 2
        return lax.dynamic_slice_in_dim(vector, side * half, half, 0)

    return (
        layer_out,
        input_grad,
        grad_qkv_weight.astype(F32),
        mine_of(ends[6]),
        mine_of(ends[7]),
        grad_out_weight.astype(F32),
        ends[0],
        grad_fc_weight.astype(F32),
        mine_of(ends[8]),
        grad_proj_weight.astype(F32),
        ends[1],
        grad_norm1_gain,
        grad_norm1_shift,
        ends[4],
        ends[5],
    )


def solution(mesh):
    rows = P(("dp", "tensor"), None)
    in_specs = (
        rows,
        P(None, "tensor"),
        P("tensor"),
        P("tensor"),
        P("tensor", None),
        P(),
        P(None, "tensor"),
        P("tensor"),
        P("tensor", None),
        P(),
        P(),
        P(),
        P(),
        P(),
        P("dp", None),
        P("dp"),
        rows,
    )
    out_specs = (
        rows,
        rows,
        P(None, "tensor"),
        P("tensor"),
        P("tensor"),
        P("tensor", None),
        P(),
        P(None, "tensor"),
        P("tensor"),
        P("tensor", None),
        P(),
        P(),
        P(),
        P(),
        P(),
    )
    return jax.shard_map(shards, mesh=mesh, in_specs=in_specs, out_specs=out_specs, check_vma=False)
```

time: 510 us -> 435 us (0.85)
  waiting for transfers between devices: 163 us -> 82.8 us
  matrix products: 102 us -> 35.9 us
  Pallas kernels: 122 us -> 173 us
  local copies, waits for them, and re-layouts: 35.7 us -> 49.8 us
  starting transfers between devices: 31.2 us -> 41.7 us
    ppermute x11 -> x16, waiting for transfers between devices: 140 us -> 52.6 us  [flip_tensor(): return lax.ppermute(values, 'tensor', [(0, 1), (1, 0)])]
    dot_general x21 -> x7, matrix products: 102 us -> 35.9 us  [dot(): return lax.dot_general(a, b, dims, preferred_element_type=F32)]
    pallas_call x5 -> x20, Pallas kernels: 111 us -> 162 us  [the longest x2 45.7 us: attend_back(): pl.pallas_call(kernel, in_specs=[pl.BlockSpec(memory_space=pltpu.SMEM)] +...]
    unnamed x135 -> x255, local copies, waits for them, and re-layouts: 21.6 us -> 41.2 us
    reduce_sum x7 -> x0, other arithmetic: 9.88 us -> none  [the longest x3 5.16 us: layer_norm(): center = inputs - jnp.mean(inputs, axis=-1, keepdims=True)]
    ppermute x11 -> x16, starting transfers between devices: 10.3 us -> 19.7 us  [flip_tensor(): return lax.ppermute(values, 'tensor', [(0, 1), (1, 0)])]
    ppermute x18, waiting for transfers between devices: 23.4 us -> 30.1 us  [flip_bit(): return lax.ppermute(values, 'dp', [(n, n ^ 1 << bit) for n in range(total)])]
  transfers between devices with their start and end apart: 30 -> 35, of which waited for: 18 -> 21; matrix products, arithmetic and copies ran while one was open for 23% -> 15% of each run, Pallas kernels for 18% -> 39%
where the time goes in v3:
time: 435 us; the launch traced here: 427 us
  Pallas kernels  173 us (40%)
  waiting for transfers between devices  82.8 us (19%)
  local copies, waits for them, and re-layouts  49.8 us (11%)
  starting transfers between devices  41.7 us (10%)
  matrix products  35.9 us (8%)
  other arithmetic  28.3 us (7%)
  between operations  15.6 us (4%)
    ppermute x16, waiting for transfers between devices, flip_tensor(): return lax.ppermute(values, 'tensor', [(0, 1), (1, 0)])  52.6 us
    pallas_call x2, Pallas kernels, attend_back(): pl.pallas_call(kernel, in_specs=[pl.BlockSpec(memory_space=pltpu.SMEM)] +...  45.7 us
    pallas_call x10, Pallas kernels, rows_call(): pl.pallas_call(body, grid_spec=pltpu.PrefetchScalarGridSpec(num_scalar_pr...  44.6 us
    unnamed x255, local copies, waits for them, and re-layouts  41.2 us
    dot_general x7, matrix products, dot(): return lax.dot_general(a, b, dims, preferred_element_type=F32)  35.9 us
    ppermute x18, waiting for transfers between devices, flip_bit(): return lax.ppermute(values, 'dp', [(n, n ^ 1 << bit) for n in range(total)])  30.1 us
    pallas_call x5, Pallas kernels, attend_call(): pl.pallas_call(kernel, grid_spec=pltpu.PrefetchScalarGridSpec(num_scalar_...  27.9 us
    pallas_call x1, Pallas kernels, join(): pl.pallas_call(join_kernel, in_specs=[in_vmem()] * len(inputs), out_specs...  25.7 us
  transfers between devices with their start and end apart: 35, of which 21 were waited for; matrix products, arithmetic and copies ran while one was open for 15% of the time, Pallas kernels for 39%

profile of v3, /device:TPU:0, one launch (start us, length us, event | category | flops | bytes accessed | tf_op | source)
XLA Modules:
  0.0 426.7 jit_solution(11747488773546833241)
XLA Ops:
  20.8 11.1 %allowed_bits.1.bits_ref.refs_14_ = s32[128,2048]{1,0:T(8,128)} custom-call(s32[64,2048]{1,0:T(8,128)} %and_bitcast_fusion.low_ref, s32[64,2048]{1,0:T(8,128)} %bitcast_select_fusion.flag_ref), custom_call_target="tpu_custom_call" | custom-call | flops 50331648 | bytes 1048576 | tf_op jit(solution)/shard_map/allowed_bits/pallas_call | solution.py:86
  32.1 8.6 %qkv_heads.2 = (bf16[6,1024,128]{2,1,0:T(8,128)(2,1)S(1)}, bf16[6,1024,128]{2,1,0:T(8,128)(2,1)S(1)}, bf16[6,1024,128]{2,1,0:T(8,128)(2,1)S(1)}, bf16[6,80,1024]...) custom-call(bf16[1024,768]{1,0:T(8,128)(2,1)} %get-tuple-element.139.norm_ref.norm_own_ref, bf16[768,1152]{1,0:T(8,128)(2,1)S(1)} %copy-done.39, ...), custom_call_target="tpu_custom_call" | custom-call | flops 3623878656 | bytes 10485760 | tf_op jit(solution)/shard_map/qkv_heads/pallas_call | solution.py:146
  52.0 7.9 %attend_start.1 = (f32[6,80,1024]{2,1,0:T(8,128)S(1)}, f32[6,8,1024]{2,1,0:T(8,128)S(1)}) custom-call(s32[3]{0:T(128)S(1)} %pad_add_fusion.places_ref.refs_0_, bf16[6,1024,128]{2,1,0:T(8,128)(2,1)S(1)} %copy-done.45, bf16[6,1024,128]{2,1,0:T(8,128)(2,1)S(1)} %copy-done.12, bf16[6,80,1024]{2,1,0:T(8,128)(2,1)S(1)} %copy-done.103, s32[128,2048]{1,0:T(8,128)S(1)} %copy-done.23), custom_call_target="tpu_custom_call" | custom-call | flops 12884901888 | bytes 8388608 | tf_op jit(solution)/shard_map/attend_start/pallas_call | solution.py:317
  60.0 9.0 %qkv_heads.3 = (bf16[6,1024,128]{2,1,0:T(8,128)(2,1)S(1)}, bf16[6,1024,128]{2,1,0:T(8,128)(2,1)S(1)}, bf16[6,1024,128]{2,1,0:T(8,128)(2,1)S(1)}, bf16[6,80,1024]...) custom-call(bf16[1024,768]{1,0:T(8,128)(2,1)} %collective-permute-done.norm_ref.norm_peer_ref, bf16[768,1152]{1,0:T(8,128)(2,1)S(1)} %copy-done.40, ...), custom_call_target="tpu_custom_call" | custom-call | flops 3623878656 | bytes 10485760 | tf_op jit(solution)/shard_map/qkv_heads/pallas_call | solution.py:146
  70.1 7.8 %attend_other.2 = (bf16[512,384]{1,0:T(8,128)(2,1)S(1)}, f32[6,8,512]{2,1,0:T(8,128)S(1)}) custom-call(s32[3]{0:T(128)S(1)} %pad_add_fusion.places_ref.refs_0_, bf16[6,1024,128]{2,1,0:T(8,128)(2,1)S(1)} %get-tuple-element.203.qa_ref.refs_1_, bf16[6,1024,128]{2,1,0:T(8,128)(2,1)S(1)} %get-tuple-element.159.ka_ref.refs_3_.refs_2_.ka_peer_ref, ...), custom_call_target="tpu_custom_call" | custom-call | flops 6442450944 | bytes 8388608 | tf_op jit(solution)/shard_map/attend_other/pallas_call | solution.py:317
  80.6 10.0 %attend_other.3 = (bf16[512,384]{1,0:T(8,128)(2,1)S(1)}, f32[6,8,512]{2,1,0:T(8,128)S(1)}) custom-call(s32[3]{0:T(128)S(1)} %pad_add_fusion.places_ref.refs_0_, bf16[6,1024,128]{2,1,0:T(8,128)(2,1)S(1)} %get-tuple-element.203.qa_ref.refs_1_, bf16[6,1024,128]{2,1,0:T(8,128)(2,1)S(1)} %get-tuple-element.159.ka_ref.refs_3_.refs_2_.ka_peer_ref, ...), custom_call_target="tpu_custom_call" | custom-call | flops 6442450944 | bytes 8388608 | tf_op jit(solution)/shard_map/attend_other/pallas_call | solution.py:317
  92.2 6.8 %collective-permute-start.1 = (bf16[512,384]{1,0:T(8,128)(2,1)S(1)}, bf16[512,384]{1,0:T(8,128)(2,1)S(1)}, u32[]{:S(2)}, u32[]{:S(2)}) collective-permute-start(bf16[512,384]{1,0:T(8,128)(2,1)S(1)} %get-tuple-element.170.refs_11_), channel_id=1, source_target_pairs={{0,1},{1,0},{2,3},{3,2},{4,5},{5,4},{6,7},{7,6},{8,9},{9,8},{10,11... | collective-permute-start | bytes 1179656 | tf_op jit(solution)/shard_map/ppermute | solution.py:849
  99.1 4.3 collective-permute-done.4.peer_ref
  115.1 5.0 %feed.4 = (bf16[2048,1536]{1,0:T(8,128)(2,1)S(1)}, bf16[2048,1536]{1,0:T(8,128)(2,1)S(1)}, f32[512,768]{1,0:T(8,128)S(1)}, f32[1,1536]{1,0:T(1,128)S(1)}) custom-call(bf16[512,768]{1,0:T(8,128)(2,1)S(1)} %get-tuple-element.178.norm_ref, bf16[1024,768]{1,0:T(8,128)(2,1)S(1)} %copy-done.28, bf16[768,1536]{1,0:T(8,128)(2,1)S(1)} %copy-done.8, ...), custom_call_target="tpu_custom_call" | custom-call | flops 3623878656 | bytes 3145728 | tf_op jit(solution)/shard_map/feed/pallas_call | solution.py:621
  121.3 5.0 %feed.5 = (bf16[2048,1536]{1,0:T(8,128)(2,1)S(1)}, bf16[2048,1536]{1,0:T(8,128)(2,1)S(1)}, f32[512,768]{1,0:T(8,128)S(1)}, f32[1,1536]{1,0:T(1,128)S(1)}) custom-call(bf16[512,768]{1,0:T(8,128)(2,1)S(1)} %get-tuple-element.179.refs_0_, bf16[1024,768]{1,0:T(8,128)(2,1)S(1)} %copy-done.28, ...), custom_call_target="tpu_custom_call", output_to_operand_aliasing={{0}: (5, {}), {1}: (6, {})} | custom-call | flops 3623878656 | bytes 3145728 | tf_op jit(solution)/shard_map/feed/pallas_call | solution.py:621
  128.7 6.7 %feed.6 = (bf16[2048,1536]{1,0:T(8,128)(2,1)S(1)}, bf16[2048,1536]{1,0:T(8,128)(2,1)S(1)}, bf16[512,768]{1,0:T(8,128)(2,1)}, f32[1,1536]{1,0:T(1,128)S(1)}) custom-call(bf16[512,768]{1,0:T(8,128)(2,1)S(1)} %collective-permute-done.5.refs_0_, bf16[512,768]{1,0:T(8,128)(2,1)} %collective-permute-done.3.refs_1_, ...), custom_call_target="tpu_custom_call", output_to_operand_aliasing={{0}: (5, {}), {1}: (6, {})} | custom-call | flops 3623878656 | bytes 3145728 | tf_op jit(solution)/shard_map/feed/pallas_call | solution.py:621
  136.0 9.5 %collective-permute-done.7.refs_1_ = bf16[512,768]{1,0:T(8,128)(2,1)S(1)} collective-permute-done((bf16[512,768]{1,0:T(8,128)(2,1)S(1)}, bf16[512,768]{1,0:T(8,128)(2,1)S(1)}, u32[]{:S(2)}, u32[]{:S(2)}) %collective-permute-start.7) | collective-permute-done | bytes 786464 | tf_op jit(solution)/shard_map/ppermute | solution.py:849
  145.5 16.9 %collective-permute-done.6.refs_0_ = bf16[512,768]{1,0:T(8,128)(2,1)S(1)} collective-permute-done((bf16[512,768]{1,0:T(8,128)(2,1)S(1)}, bf16[512,768]{1,0:T(8,128)(2,1)S(1)}, u32[]{:S(2)}, u32[]{:S(2)}) %collective-permute-start.6) | collective-permute-done | bytes 786464 | tf_op jit(solution)/shard_map/ppermute | solution.py:849
  162.4 5.7 %feed.7 = (bf16[2048,1536]{1,0:T(8,128)(2,1)S(1)}, bf16[2048,1536]{1,0:T(8,128)(2,1)S(1)}, bf16[512,768]{1,0:T(8,128)(2,1)}, f32[1,1536]{1,0:T(1,128)S(1)}) custom-call(bf16[512,768]{1,0:T(8,128)(2,1)S(1)} %collective-permute-done.6.refs_0_, bf16[512,768]{1,0:T(8,128)(2,1)S(1)} %collective-permute-done.7.refs_1_, ...), custom_call_target="tpu_custom_call", output_to_operand_aliasing={{0}: (5, {}), {1}: (6, {})} | custom-call | flops 3623878656 | bytes 3145728 | tf_op jit(solution)/shard_map/feed/pallas_call | solution.py:621
  168.7 6.3 %convolution_convert_fusion.1 = bf16[768,1536]{1,0:T(8,128)(2,1)} fusion(bf16[2048,1536]{1,0:T(8,128)(2,1)S(1)} %get-tuple-element.188, bf16[512,768]{1,0:T(8,128)(2,1)S(1)} %collective-permute-done.6.refs_0_, bf16[512,768]{1,0:T(8,128)(2,1)S(1)} %collective-permute-done.5.refs_0_, bf16[512,768]{1,0:T(8,128)(2,1)S(1)} %get-tuple-element.179.refs_0_, ...), kind=kOutput, calls=%fused_computation.1 | convolution fusion | flops 4845600768 | bytes 11796480 | tf_op jit(solution)/shard_map/dot_general | solution.py:30
  175.0 8.0 %convolution_convert_fusion = bf16[1536,768]{1,0:T(8,128)(2,1)} fusion(bf16[2048,1536]{1,0:T(8,128)(2,1)S(1)} %get-tuple-element.189, bf16[512,768]{1,0:T(8,128)(2,1)S(1)} %collective-permute-done.7.refs_1_, bf16[512,768]{1,0:T(8,128)(2,1)} %collective-permute-done.3.refs_1_, bf16[1024,768]{1,0:T(8,128)(2,1)S(1)} %copy-done.28), kind=kOutput, calls=%fused_computation | convolution fusion | flops 4842455040 | bytes 11796480 | tf_op jit(solution)/shard_map/dot_general | solution.py:30
  183.0 6.6 %fusion.16 = bf16[1024,768]{1,0:T(8,128)(2,1)} fusion(bf16[1536,768]{1,0:T(8,128)(2,1)} %refs_4_.5, bf16[2048,1536]{1,0:T(8,128)(2,1)} %copy-done), kind=kOutput, calls=%fused_computation.25 | convolution fusion | flops 2416705536 | bytes 7077888 | tf_op jit(solution)/shard_map/dot_general | solution.py:30
  189.6 4.4 %mix_back.2 = (f32[1024,768]{1,0:T(8,128)S(1)}, bf16[1024,768]{1,0:T(8,128)(2,1)S(1)}, bf16[512,384]{1,0:T(8,128)(2,1)S(1)}, bf16[512,384]{1,0:T(8,128)(2,1)}, f...) custom-call(f32[1024,768]{1,0:T(8,128)S(1)} %copy-done.4, ...), custom_call_target="tpu_custom_call" | custom-call | flops 603979776 | bytes 3145728 | tf_op jit(solution)/shard_map/mix_back/pallas_call | solution.py:621
  194.2 4.4 %mix_back.3 = (f32[1024,768]{1,0:T(8,128)S(1)}, bf16[1024,768]{1,0:T(8,128)(2,1)S(1)}, bf16[512,384]{1,0:T(8,128)(2,1)S(1)}, bf16[512,384]{1,0:T(8,128)(2,1)}, f...) custom-call(f32[1024,768]{1,0:T(8,128)S(1)} %copy-done.4, ...), custom_call_target="tpu_custom_call", output_to_operand_aliasing={{0}: (7, {}), {1}: (8, {})} | custom-call | flops 603979776 | bytes 3145728 | tf_op jit(solution)/shard_map/mix_back/pallas_call | solution.py:621
  203.3 3.9 pad_maximum_fusion
  209.2 5.6 %fusion.19 = bf16[1024,768]{1,0:T(8,128)(2,1)} fusion(bf16[1536,768]{1,0:T(8,128)(2,1)S(1)} %copy-done.10, bf16[2048,1536]{1,0:T(8,128)(2,1)} %copy-done), kind=kOutput, calls=%fused_computation.26 | convolution fusion | flops 2416705536 | bytes 7077888 | tf_op jit(solution)/shard_map/dot_general | solution.py:30
  227.2 16.5 %attend_back.2 = (f32[6,64,1024]{2,1,0:T(8,128)S(1)}, f32[6,1024,128]{2,1,0:T(8,128)S(1)}, f32[6,1024,128]{2,1,0:T(8,128)S(1)}, f32[6,1024,128]{2,1,0:T(8,128)S(1)}, f32[6,1024,128]{2,1,0:T(8,128)S(1)}) custom-call(s32[3]{0:T(128)S(1)} %copy-done.84, bf16[6,1024,128]{2,1,0:T(8,128)(2,1)S(1)} %copy-done.47, bf16[6,1024,128]{2,1,0:T(8,128)(2,1)S(1)} %copy-done.14, ...), custom_call_target="tpu_custom_call" | custom-call | flops 1000000 | bytes 1048576 | tf_op jit(solution)/shard_map/attend_back/pallas_call | solution.py:473
  243.8 12.0 %collective-permute-done.10.refs_8_ = bf16[512,384]{1,0:T(8,128)(2,1)} collective-permute-done((bf16[512,384]{1,0:T(8,128)(2,1)}, bf16[512,384]{1,0:T(8,128)(2,1)}, u32[]{:S(2)}, u32[]{:S(2)}) %collective-permute-start.10) | collective-permute-done | bytes 393248 | tf_op jit(solution)/shard_map/ppermute | solution.py:849
  255.8 29.2 %attend_back.3 = (f32[6,64,1024]{2,1,0:T(8,128)S(1)}, f32[6,1024,128]{2,1,0:T(8,128)S(1)}, f32[6,1024,128]{2,1,0:T(8,128)S(1)}, f32[6,1024,128]{2,1,0:T(8,128)S(1)}, f32[6,1024,128]{2,1,0:T(8,128)S(1)}) custom-call(s32[3]{0:T(128)S(1)} %copy-done.84, ...), custom_call_target="tpu_custom_call", output_to_operand_aliasing={{1}: (15, {}), {2}: (16, {}), {3}: (17, {}), {4}: (18, {})} | custom-call | flops 1000000 | bytes 1048576 | tf_op jit(solution)/shard_map/attend_back/pallas_call | solution.py:473
  293.8 25.7 %join.1 = (f32[1024,768]{1,0:T(8,128)S(1)}, bf16[1024,768]{1,0:T(8,128)(2,1)S(1)}, bf16[2048,1152]{1,0:T(8,128)(2,1)S(1)}, f32[1,1152]{1,0:T(1,128)S(1)}, f32[6,...) custom-call(f32[6,64,1024]{2,1,0:T(8,128)S(1)} %get-tuple-element.225.dq_own_ref, ...), custom_call_target="tpu_custom_call" | custom-call | flops 1000000 | bytes 1048576 | tf_op jit(solution)/shard_map/join/pallas_call | solution.py:557
  319.5 4.3 %convolution_convert_fusion.2 = bf16[768,1152]{1,0:T(8,128)(2,1)S(1)} fusion(bf16[2048,768]{1,0:T(8,128)(2,1)S(1)} %copy-done.106, bf16[2048,1152]{1,0:T(8,128)(2,1)S(1)} %get-tuple-element.233), kind=kOutput, calls=%fused_computation.2 | convolution fusion | flops 3624763392 | bytes 9633792 | tf_op jit(solution)/shard_map/dot_general | solution.py:30
  334.5 5.2 %collective-permute-done.15 = bf16[4,24,1536]{2,1,0:T(8,128)(2,1)S(1)} collective-permute-done((bf16[4,24,1536]{2,1,0:T(8,128)(2,1)S(1)}, bf16[4,24,1536]{2,1,0:T(8,128)(2,1)S(1)}, u32[]{:S(2)}, u32[]{:S(2)}) %collective-permute-start.15) | collective-permute-done | bytes 294944 | tf_op jit(solution)/shard_map/ppermute | solution.py:841
  358.0 5.5 %collective-permute-done.21.other_ref = bf16[1024,768]{1,0:T(8,128)(2,1)} collective-permute-done((bf16[1024,768]{1,0:T(8,128)(2,1)}, bf16[1024,768]{1,0:T(8,128)(2,1)}, u32[]{:S(2)}, u32[]{:S(2)}) %collective-permute-start.21) | collective-permute-done | bytes 1572896 | tf_op jit(solution)/shard_map/ppermute | solution.py:849
  370.5 5.3 %collective-permute-done.22 = bf16[1,24,1536]{2,1,0:T(8,128)(2,1)S(1)} collective-permute-done((bf16[1,24,1536]{2,1,0:T(8,128)(2,1)S(1)}, bf16[1,24,1536]{2,1,0:T(8,128)(2,1)S(1)}, u32[]{:S(2)}, u32[]{:S(2)}) %collective-permute-start.22) | collective-permute-done | bytes 73760 | tf_op jit(solution)/shard_map/ppermute | solution.py:841
  385.3 3.8 collective-permute-done.32
  394.2 3.8 add_add_fusion
  408.6 4.8 %norm_one_back.1 = f32[1024,768]{1,0:T(8,128)} custom-call(f32[1024,768]{1,0:T(8,128)S(1)} %copy-done.2, f32[1024,768]{1,0:T(8,128)S(1)} %copy-done.38, bf16[1024,768]{1,0:T(8,128)(2,1)} %collective-permute-done.21.other_ref, f32[1024,768]{1,0:T(8,128)S(1)} %copy-done.22, f32[1,768]{1,0:T(1,128)S(1)} %copy-done.76), custom_call_target="tpu_custom_call" | custom-call | flops 15728640 | bytes 6291456 | tf_op jit(solution)/shard_map/norm_one_back/pallas_call | solution.py:621
  (393 shorter events, 141.6 us)
Async XLA Ops:
  7.2 334.0 %all-reduce.4.cloned.1.call-start = ((), (), s32[]{:S(2)}) async-start(), calls=%async_computation | async-start | bytes 9437184 | tf_op jit(solution)/shard_map/psum | solution.py:1074
  16.1 43.8 %collective-permute-start = (bf16[1024,768]{1,0:T(8,128)(2,1)}, bf16[1024,768]{1,0:T(8,128)(2,1)}, u32[]{:S(2)}, u32[]{:S(2)}) collective-permute-start(bf16[1024,768]{1,0:T(8,128)(2,1)} %get-tuple-element.139.norm_ref.norm_own_ref), channel_id=1, source_target_pairs={{0,1},{1,0},{2,3},{3,2},{4,5},{5,4},{6,7},{7,6},{8,9},{9,8},{10,11... | collective-permute-start | bytes 4718600 | tf_op jit(solution)/shard_map/ppermute | solution.py:849
  32.0 67.2 %collective-permute-start.2 = (bf16[384,768]{1,0:T(8,128)(2,1)}, bf16[384,768]{1,0:T(8,128)(2,1)}, u32[]{:S(2)}, u32[]{:S(2)}) collective-permute-start(bf16[384,768]{1,0:T(8,128)(2,1)} %refs_5_.1), channel_id=1, source_target_pairs={{0,1},{1,0},{2,3},{3,2},{4,5},{5,4},{6,7},{7,6},{8,9},{9,8},{10,11... | collective-permute-start | bytes 1769480 | tf_op jit(solution)/shard_map/ppermute | solution.py:849
  45.9 45.4 %collective-permute-start.3 = (bf16[512,768]{1,0:T(8,128)(2,1)}, bf16[512,768]{1,0:T(8,128)(2,1)}, u32[]{:S(2)}, u32[]{:S(2)}) collective-permute-start(bf16[512,768]{1,0:T(8,128)(2,1)} %get-tuple-element.174), channel_id=1, source_target_pairs={{0,1},{1,0},{2,3},{3,2},{4,5},{5,4},{6,7},{7,6},{8,9},{9,8},{10,11... | collective-permute-start | bytes 2359304 | tf_op jit(solution)/shard_map/ppermute | solution.py:849
  91.3 12.1 %collective-permute-start.4 = (bf16[512,384]{1,0:T(8,128)(2,1)S(1)}, bf16[512,384]{1,0:T(8,128)(2,1)S(1)}, u32[]{:S(2)}, u32[]{:S(2)}) collective-permute-start(bf16[512,384]{1,0:T(8,128)(2,1)S(1)} %get-tuple-element.175.refs_10_), channel_id=1, source_target_pairs={{0,1},{1,0},{2,3},{3,2},{4,5},{5,4},{6,7},{7,6},{8,9},{9,8},{10,11... | collective-permute-start | bytes 1179656 | tf_op jit(solution)/shard_map/ppermute | solution.py:849
  92.2 19.6 %collective-permute-start.1 = (bf16[512,384]{1,0:T(8,128)(2,1)S(1)}, bf16[512,384]{1,0:T(8,128)(2,1)S(1)}, u32[]{:S(2)}, u32[]{:S(2)}) collective-permute-start(bf16[512,384]{1,0:T(8,128)(2,1)S(1)} %get-tuple-element.170.refs_11_), channel_id=1, source_target_pairs={{0,1},{1,0},{2,3},{3,2},{4,5},{5,4},{6,7},{7,6},{8,9},{9,8},{10,11... | collective-permute-start | bytes 1179656 | tf_op jit(solution)/shard_map/ppermute | solution.py:849
  106.5 22.2 %collective-permute-start.5 = (bf16[512,768]{1,0:T(8,128)(2,1)S(1)}, bf16[512,768]{1,0:T(8,128)(2,1)S(1)}, u32[]{:S(2)}, u32[]{:S(2)}) collective-permute-start(bf16[512,768]{1,0:T(8,128)(2,1)S(1)} %get-tuple-element.178.norm_ref), channel_id=1, source_target_pairs={{0,1},{1,0},{2,3},{3,2},{4,5},{5,4},{6,7},{7,6},{8,9},{9,8},{10,11... | collective-permute-start | bytes 2359304 | tf_op jit(solution)/shard_map/ppermute | solution.py:849
  106.6 38.9 %collective-permute-start.7 = (bf16[512,768]{1,0:T(8,128)(2,1)S(1)}, bf16[512,768]{1,0:T(8,128)(2,1)S(1)}, u32[]{:S(2)}, u32[]{:S(2)}) collective-permute-start(bf16[512,768]{1,0:T(8,128)(2,1)S(1)} %copy-done.111), channel_id=1, source_target_pairs={{0,1},{1,0},{2,3},{3,2},{4,5},{5,4},{6,7},{7,6},{8,9},{9,8},{10,11... | collective-permute-start | bytes 2359304 | tf_op jit(solution)/shard_map/ppermute | solution.py:849
  114.9 47.5 %collective-permute-start.6 = (bf16[512,768]{1,0:T(8,128)(2,1)S(1)}, bf16[512,768]{1,0:T(8,128)(2,1)S(1)}, u32[]{:S(2)}, u32[]{:S(2)}) collective-permute-start(bf16[512,768]{1,0:T(8,128)(2,1)S(1)} %get-tuple-element.179.refs_0_), channel_id=1, source_target_pairs={{0,1},{1,0},{2,3},{3,2},{4,5},{5,4},{6,7},{7,6},{8,9},{9,8},{10,11... | collective-permute-start | bytes 2359304 | tf_op jit(solution)/shard_map/ppermute | solution.py:849
  135.4 54.2 %collective-permute-start.9 = (bf16[512,768]{1,0:T(8,128)(2,1)}, bf16[512,768]{1,0:T(8,128)(2,1)}, u32[]{:S(2)}, u32[]{:S(2)}) collective-permute-start(bf16[512,768]{1,0:T(8,128)(2,1)} %get-tuple-element.195), channel_id=1, source_target_pairs={{0,1},{1,0},{2,3},{3,2},{4,5},{5,4},{6,7},{7,6},{8,9},{9,8},{10,11... | collective-permute-start | bytes 2359304 | tf_op jit(solution)/shard_map/ppermute | solution.py:849
  168.7 25.4 %collective-permute-start.8 = (bf16[512,768]{1,0:T(8,128)(2,1)}, bf16[512,768]{1,0:T(8,128)(2,1)}, u32[]{:S(2)}, u32[]{:S(2)}) collective-permute-start(bf16[512,768]{1,0:T(8,128)(2,1)} %get-tuple-element.193), channel_id=1, source_target_pairs={{0,1},{1,0},{2,3},{3,2},{4,5},{5,4},{6,7},{7,6},{8,9},{9,8},{10,11... | collective-permute-start | bytes 2359304 | tf_op jit(solution)/shard_map/ppermute | solution.py:849
  201.1 87.2 %collective-permute-start.12 = (bf16[1024,768]{1,0:T(8,128)(2,1)}, bf16[1024,768]{1,0:T(8,128)(2,1)}, u32[]{:S(2)}, u32[]{:S(2)}) collective-permute-start(bf16[1024,768]{1,0:T(8,128)(2,1)} %fusion.16), channel_id=1, source_target_pairs={{0,1},{1,0},{2,3},{3,2},{4,5},{5,4},{6,7},{7,6},{8,9},{9,8},{10,11... | collective-permute-start | bytes 4718600 | tf_op jit(solution)/shard_map/ppermute | solution.py:849
  207.1 48.6 %collective-permute-start.11 = (bf16[512,384]{1,0:T(8,128)(2,1)}, bf16[512,384]{1,0:T(8,128)(2,1)}, u32[]{:S(2)}, u32[]{:S(2)}) collective-permute-start(bf16[512,384]{1,0:T(8,128)(2,1)} %get-tuple-element.198), channel_id=1, source_target_pairs={{0,1},{1,0},{2,3},{3,2},{4,5},{5,4},{6,7},{7,6},{8,9},{9,8},{10,11... | collective-permute-start | bytes 1179656 | tf_op jit(solution)/shard_map/ppermute | solution.py:849
  207.2 48.5 %collective-permute-start.10 = (bf16[512,384]{1,0:T(8,128)(2,1)}, bf16[512,384]{1,0:T(8,128)(2,1)}, u32[]{:S(2)}, u32[]{:S(2)}) collective-permute-start(bf16[512,384]{1,0:T(8,128)(2,1)} %get-tuple-element.208), channel_id=1, source_target_pairs={{0,1},{1,0},{2,3},{3,2},{4,5},{5,4},{6,7},{7,6},{8,9},{9,8},{10,11... | collective-permute-start | bytes 1179656 | tf_op jit(solution)/shard_map/ppermute | solution.py:849
  209.2 79.2 %collective-permute-start.13 = (bf16[768,384]{1,0:T(8,128)(2,1)}, bf16[768,384]{1,0:T(8,128)(2,1)}, u32[]{:S(2)}, u32[]{:S(2)}) collective-permute-start(bf16[768,384]{1,0:T(8,128)(2,1)} %convolution_convert_fusion.3), channel_id=1, source_target_pairs={{0,1},{1,0},{2,3},{3,2},{4,5},{5,4},{6,7},{7,6},{8,9},{9,8},{10,11... | collective-permute-start | bytes 1769480 | tf_op jit(solution)/shard_map/ppermute | solution.py:849
  326.2 37.3 %collective-permute-start.21 = (bf16[1024,768]{1,0:T(8,128)(2,1)}, bf16[1024,768]{1,0:T(8,128)(2,1)}, u32[]{:S(2)}, u32[]{:S(2)}) collective-permute-start(bf16[1024,768]{1,0:T(8,128)(2,1)} %copy-done.101), channel_id=1, source_target_pairs={{0,1},{1,0},{2,3},{3,2},{4,5},{5,4},{6,7},{7,6},{8,9},{9,8},{10,11... | collective-permute-start | bytes 4718600 | tf_op jit(solution)/shard_map/ppermute | solution.py:849
  330.5 9.1 %collective-permute-start.15 = (bf16[4,24,1536]{2,1,0:T(8,128)(2,1)S(1)}, bf16[4,24,1536]{2,1,0:T(8,128)(2,1)S(1)}, u32[]{:S(2)}, u32[]{:S(2)}) collective-permute-start(bf16[4,24,1536]{2,1,0:T(8,128)(2,1)S(1)} %constant_dynamic-slice_fusion.5), channel_id=1, source_target_pairs={{0,4},{2,6},{4,0},{6,2},{8,12},{10,14},{12,8},{14,10},{16,20},{18,... | collective-permute-start | bytes 884744 | tf_op jit(solution)/shard_map/ppermute | solution.py:841
  332.1 32.9 %collective-permute-start.29 = (f32[84,128]{1,0:T(8,128)S(1)}, f32[84,128]{1,0:T(8,128)S(1)}, u32[]{:S(2)}, u32[]{:S(2)}) collective-permute-start(f32[84,128]{1,0:T(8,128)S(1)} %bitcast.54), channel_id=1, source_target_pairs={{0,1},{1,0},{2,3},{3,2},{4,5},{5,4},{6,7},{7,6},{8,9},{9,8},{10,11... | collective-permute-start | bytes 129032 | tf_op jit(solution)/shard_map/ppermute | solution.py:849
  332.8 8.3 %collective-permute-start.16 = (bf16[4,24,1536]{2,1,0:T(8,128)(2,1)S(1)}, bf16[4,24,1536]{2,1,0:T(8,128)(2,1)S(1)}, u32[]{:S(2)}, u32[]{:S(2)}) collective-permute-start(bf16[4,24,1536]{2,1,0:T(8,128)(2,1)S(1)} %constant_dynamic-slice_fusion.4), channel_id=1, source_target_pairs={{0,8},{2,10},{4,12},{6,14},{8,0},{10,2},{12,4},{14,6},{16,24},{18,... | collective-permute-start | bytes 884744 | tf_op jit(solution)/shard_map/ppermute | solution.py:841
  342.1 7.3 %collective-permute-start.17 = (bf16[2,24,1536]{2,1,0:T(8,128)(2,1)S(1)}, bf16[2,24,1536]{2,1,0:T(8,128)(2,1)S(1)}, u32[]{:S(2)}, u32[]{:S(2)}) collective-permute-start(bf16[2,24,1536]{2,1,0:T(8,128)(2,1)S(1)} %constant_dynamic-slice_fusion.3), channel_id=1, source_target_pairs={{0,8},{2,10},{4,12},{6,14},{8,0},{10,2},{12,4},{14,6},{16,24},{18,... | collective-permute-start | bytes 442376 | tf_op jit(solution)/shard_map/ppermute | solution.py:841
  343.8 9.7 %collective-permute-start.19 = (bf16[2,24,1536]{2,1,0:T(8,128)(2,1)S(1)}, bf16[2,24,1536]{2,1,0:T(8,128)(2,1)S(1)}, u32[]{:S(2)}, u32[]{:S(2)}) collective-permute-start(bf16[2,24,1536]{2,1,0:T(8,128)(2,1)S(1)} %constant_dynamic-slice_fusion.1), channel_id=1, source_target_pairs={{0,16},{2,18},{4,20},{6,22},{8,24},{10,26},{12,28},{14,30},{16,0},... | collective-permute-start | bytes 442376 | tf_op jit(solution)/shard_map/ppermute | solution.py:841
  350.4 6.1 %collective-permute-start.18 = (bf16[1,24,1536]{2,1,0:T(8,128)(2,1)S(1)}, bf16[1,24,1536]{2,1,0:T(8,128)(2,1)S(1)}, u32[]{:S(2)}, u32[]{:S(2)}) collective-permute-start(bf16[1,24,1536]{2,1,0:T(8,128)(2,1)S(1)} %constant_dynamic-slice_fusion.2), channel_id=1, source_target_pairs={{0,16},{2,18},{4,20},{6,22},{8,24},{10,26},{12,28},{14,30},{16,0},... | collective-permute-start | bytes 221192 | tf_op jit(solution)/shard_map/ppermute | solution.py:841
  353.6 4.4 %collective-permute-start.20 = (bf16[1,24,1536]{2,1,0:T(8,128)(2,1)S(1)}, bf16[1,24,1536]{2,1,0:T(8,128)(2,1)S(1)}, u32[]{:S(2)}, u32[]{:S(2)}) collective-permute-start(bf16[1,24,1536]{2,1,0:T(8,128)(2,1)S(1)} %constant_dynamic-slice_fusion), channel_id=1, source_target_pairs={{0,4},{2,6},{4,0},{6,2},{8,12},{10,14},{12,8},{14,10},{16,20},{18,... | collective-permute-start | bytes 221192 | tf_op jit(solution)/shard_map/ppermute | solution.py:841
  365.0 14.3 %collective-permute-start.30 = (f32[84,128]{1,0:T(8,128)S(1)}, f32[84,128]{1,0:T(8,128)S(1)}, u32[]{:S(2)}, u32[]{:S(2)}) collective-permute-start(f32[84,128]{1,0:T(8,128)S(1)} %bitcast_add_fusion), channel_id=1, source_target_pairs={{0,2},{2,0},{4,6},{6,4},{8,10},{10,8},{12,14},{14,12},{16,18},{18,... | collective-permute-start | bytes 129032 | tf_op jit(solution)/shard_map/ppermute | solution.py:841
  365.1 10.8 %collective-permute-start.22 = (bf16[1,24,1536]{2,1,0:T(8,128)(2,1)S(1)}, bf16[1,24,1536]{2,1,0:T(8,128)(2,1)S(1)}, u32[]{:S(2)}, u32[]{:S(2)}) collective-permute-start(bf16[1,24,1536]{2,1,0:T(8,128)(2,1)S(1)} %add_convert_fusion.7), channel_id=1, source_target_pairs={{0,16},{2,18},{4,20},{6,22},{8,24},{10,26},{12,28},{14,30},{16,0},... | collective-permute-start | bytes 221192 | tf_op jit(solution)/shard_map/ppermute | solution.py:841
  367.9 10.8 %collective-permute-start.26 = (bf16[2,24,1536]{2,1,0:T(8,128)(2,1)S(1)}, bf16[2,24,1536]{2,1,0:T(8,128)(2,1)S(1)}, u32[]{:S(2)}, u32[]{:S(2)}) collective-permute-start(bf16[2,24,1536]{2,1,0:T(8,128)(2,1)S(1)} %maximum_select_fusion.6), channel_id=1, source_target_pairs={{0,16},{2,18},{4,20},{6,22},{8,24},{10,26},{12,28},{14,30},{16,0},... | collective-permute-start | bytes 442376 | tf_op jit(solution)/shard_map/ppermute | solution.py:841
  375.9 6.6 %collective-permute-start.23 = (bf16[2,24,1536]{2,1,0:T(8,128)(2,1)S(1)}, bf16[2,24,1536]{2,1,0:T(8,128)(2,1)S(1)}, u32[]{:S(2)}, u32[]{:S(2)}) collective-permute-start(bf16[2,24,1536]{2,1,0:T(8,128)(2,1)S(1)} %maximum_select_fusion.5), channel_id=1, source_target_pairs={{0,8},{2,10},{4,12},{6,14},{8,0},{10,2},{12,4},{14,6},{16,24},{18,... | collective-permute-start | bytes 442376 | tf_op jit(solution)/shard_map/ppermute | solution.py:841
  378.7 12.6 %collective-permute-start.27 = (bf16[4,24,1536]{2,1,0:T(8,128)(2,1)S(1)}, bf16[4,24,1536]{2,1,0:T(8,128)(2,1)}, u32[]{:S(2)}, u32[]{:S(2)}) collective-permute-start(bf16[4,24,1536]{2,1,0:T(8,128)(2,1)S(1)} %maximum_select_fusion.4), channel_id=1, source_target_pairs={{0,8},{2,10},{4,12},{6,14},{8,0},{10,2},{12,4},{14,6},{16,24},{18,... | collective-permute-start | bytes 884744 | tf_op jit(solution)/shard_map/ppermute | solution.py:841
  383.3 9.2 %collective-permute-start.24 = (bf16[4,24,1536]{2,1,0:T(8,128)(2,1)}, bf16[4,24,1536]{2,1,0:T(8,128)(2,1)}, u32[]{:S(2)}, u32[]{:S(2)}) collective-permute-start(bf16[4,24,1536]{2,1,0:T(8,128)(2,1)} %maximum_select_fusion.3), channel_id=1, source_target_pairs={{0,4},{2,6},{4,0},{6,2},{8,12},{10,14},{12,8},{14,10},{16,20},{18,... | collective-permute-start | bytes 884744 | tf_op jit(solution)/shard_map/ppermute | solution.py:841
  383.5 5.5 %collective-permute-start.32 = (f32[84,128]{1,0:T(8,128)S(1)}, f32[84,128]{1,0:T(8,128)S(1)}, u32[]{:S(2)}, u32[]{:S(2)}) collective-permute-start(f32[84,128]{1,0:T(8,128)S(1)} %add.174), channel_id=1, source_target_pairs={{0,8},{2,10},{4,12},{6,14},{8,0},{10,2},{12,4},{14,6},{16,24},{18,... | collective-permute-start | bytes 129032 | tf_op jit(solution)/shard_map/ppermute | solution.py:841
  389.1 8.9 %collective-permute-start.33 = (f32[84,128]{1,0:T(8,128)S(1)}, f32[84,128]{1,0:T(8,128)S(1)}, u32[]{:S(2)}, u32[]{:S(2)}) collective-permute-start(f32[84,128]{1,0:T(8,128)S(1)} %add.175), channel_id=1, source_target_pairs={{0,16},{2,18},{4,20},{6,22},{8,24},{10,26},{12,28},{14,30},{16,0},... | collective-permute-start | bytes 129032 | tf_op jit(solution)/shard_map/ppermute | solution.py:841
  394.1 19.3 %collective-permute-start.28 = (bf16[16,24,1536]{2,1,0:T(8,128)(2,1)S(1)}, bf16[16,24,1536]{2,1,0:T(8,128)(2,1)S(1)}, u32[]{:S(2)}, u32[]{:S(2)}) collective-permute-start(bf16[16,24,1536]{2,1,0:T(8,128)(2,1)S(1)} %pad_maximum_fusion.2), channel_id=1, source_target_pairs={{0,2},{2,0},{4,6},{6,4},{8,10},{10,8},{12,14},{14,12},{16,18},{18,... | collective-permute-start | bytes 3538952 | tf_op jit(solution)/shard_map/ppermute | solution.py:841
  (126 other events, 779.6 us)
Sparse Core Ops, SparseCore 0:
  215.0 118.9 all-reduce.3
